TPU v7x, 32 devices: a whole 2x2x4 slice. The times are simulated.
32 devices in a mesh: section: 2 (over core), rows: 16 (over z, y, x).
Axes of the slice: x: 2, y: 2, z: 4, core: 2. Of those that a mesh axis runs over, the one named last changes fastest.
Arguments:
- byte_ids: int32 [32, 1024], P('rows'), may hold values from 0 to 259
- hash_ids: int32 [32, 1024, 3], P('rows'), may hold values from 0 to 131071, as said below
- patch_lengths: int32 [32, 256], P('rows'), may hold values from 1 to 16, 1024 in all within a row
- row_lengths: int32 [32], P('rows'), may hold values from 128 to 256
- byte_table: bfloat16 [260, 1024], P(None, 'section'), may hold values from -3 to 3
- hash_tables: bfloat16 [3, 131072, 1024], P(None, 'rows', 'section'), may hold values from -3 to 3
- norm_gains: bfloat16 [2, 2, 1024], P('section'), may hold values from 0.5 to 1.5
- w_qkv: bfloat16 [2, 1024, 3072], P('section'), may hold values from -0.1875 to 0.1875
- w_out: bfloat16 [2, 1024, 1024], P('section'), may hold values from -0.75 to 0.75
- w_gate_up: bfloat16 [2, 1024, 5632], P('section'), may hold values from -0.1875 to 0.1875
- w_down: bfloat16 [2, 2816, 1024], P('section'), may hold values from -0.109375 to 0.109375
- cotangent: bfloat16 [2, 32, 256, 1024], P('section', 'rows'), may hold values from -6 to 6
Outputs:
- section_out: bfloat16 [2, 32, 256, 1024], P('section', 'rows')
- byte_table_grad: float32 [260, 1024], P(None, 'section')
- hash_grad: float32 [3, 131072, 1024], P(None, 'rows', 'section')
- gains_grad: float32 [2, 2, 1024], P('section', None, 'rows')
- qkv_grad: float32 [2, 1024, 3072], P('section', 'rows')
- out_grad: float32 [2, 1024, 1024], P('section', 'rows')
- gate_up_grad: float32 [2, 1024, 5632], P('section', 'rows')
- down_grad: float32 [2, 2816, 1024], P('section', None, 'rows')
Inputs may be any that keep to these rules, and one draw needn't show every extreme that they name: `hash_ids`: within the 2 sequences of one index of rows, the ids of each table fall in every run of 8192 rows starting at a multiple of 8192 exactly 128 times. `patch_lengths`: each sequence's patch lengths sum to 1024.
All inputs are finite; a program needn't handle non-finite values.
Results may differ from a plain program's by a relative error of at most 0.035.
Values may be sent and summed in bfloat16 or wider, within the bound.
A program may use at most 640 MiB of HBM per device.

v0:
```python
import jax
import jax.numpy as jnp
from jax import lax
from jax.sharding import PartitionSpec as P

D = 1024
HEADS = 16
HEAD = 64
FF = 2816
L = 1024
MOST = 16
M = 2
P_SIZE = 256


epsilon = 1e-05


def shifted_2(block, axis, distance):
    devices = range(lax.axis_size(axis))
    route = [(i - distance, i) for i in devices if i - distance in devices]
    return lax.ppermute(block, axis, route)


def matmul(left_side, right_side):
    return jnp.dot(left_side, right_side, preferred_element_type=jnp.float32)


def outer_sum(left_side, right_side):
    return jnp.einsum("ra,rb->ab", left_side, right_side, preferred_element_type=jnp.float32)


def times_transposed(left_side, right_side):
    return jnp.einsum("ra,ba->rb", left_side, right_side, preferred_element_type=jnp.float32)


def normalize(inputs, norm_gain):
    inverse = lax.rsqrt(jnp.mean(inputs * inputs, axis=-1, keepdims=True) + epsilon)
    return (inputs * inverse * norm_gain, inverse)


def normalize_back(inputs, norm_gain, inverse, grad_normed):
    scaled = inputs * inverse
    grad_gain = jnp.sum(grad_normed * scaled, axis=0)
    grad_scaled = grad_normed * norm_gain
    grad_inputs = inverse * (
        grad_scaled - scaled * jnp.mean(grad_scaled * scaled, axis=-1, keepdims=True)
    )
    return (grad_inputs, grad_gain)


def softmax_rows(scores):
    shifted = jnp.exp(scores - jnp.max(scores, axis=-1, keepdims=True))
    return shifted / jnp.sum(shifted, axis=-1, keepdims=True)


def softmax_back(attention, grad_attention):
    return (
        attention * (grad_attention - jnp.sum(attention * grad_attention, axis=-1, keepdims=True))
    ).astype(jnp.bfloat16)


def slot_layout(lengths):
    starts = jnp.cumsum(lengths) - lengths
    offsets = jnp.arange(MOST, dtype=jnp.int32)
    slot_index = jnp.minimum(starts[:, None] + offsets[None, :], L - 1)
    members = offsets[None, :] < lengths[:, None]
    return (slot_index, members, starts)


def byte_places(starts, lengths):
    byte_positions = jnp.arange(L, dtype=jnp.int32)
    after_start = starts[:, None] <= byte_positions[None, :]
    membership = after_start & (byte_positions[None, :] < (starts + lengths)[:, None])
    byte_patch = jnp.sum(after_start.astype(jnp.int32), axis=0) - 1
    byte_slot = byte_patch * MOST + byte_positions - jnp.take(starts, byte_patch)
    return (membership, byte_patch, byte_slot)


def feed_forward(hidden_in, norm_gain, w_gate_up, w_down):
    normed, inverse = normalize(hidden_in, norm_gain)
    joined = matmul(normed.astype(jnp.bfloat16), w_gate_up)
    inner_rows = (jax.nn.silu(joined[:, :FF]) * joined[:, FF:]).astype(jnp.bfloat16)
    return hidden_in + matmul(inner_rows, w_down)


def feed_back(hidden_in, norm_gain, w_gate_up, w_down, grad_out):
    normed, inverse = normalize(hidden_in, norm_gain)
    normed_low = normed.astype(jnp.bfloat16)
    joined = matmul(normed_low, w_gate_up)
    gate_part, up_part = (joined[:, :FF], joined[:, FF:])
    sigmoid_gate = jax.nn.sigmoid(gate_part)
    inner_rows = (gate_part * sigmoid_gate * up_part).astype(jnp.bfloat16)
    grad_branch = grad_out.astype(jnp.bfloat16)
    grad_down = outer_sum(inner_rows, grad_branch)
    grad_inner = times_transposed(grad_branch, w_down)
    grad_gate = grad_inner * up_part * sigmoid_gate * (1.0 + gate_part * (1.0 - sigmoid_gate))
    grad_up = grad_inner * gate_part * sigmoid_gate
    grad_joined = jnp.concatenate([grad_gate, grad_up], axis=1).astype(jnp.bfloat16)
    grad_gate_up = outer_sum(normed_low, grad_joined)
    grad_normed = times_transposed(grad_joined, w_gate_up)
    grad_in, grad_gain = normalize_back(hidden_in, norm_gain, inverse, grad_normed)
    return (grad_out + grad_in, grad_gain, grad_gate_up, grad_down)


def encoder_parts(layer_weights, byte_rows, lengths):
    norm_gains, w_qkv, w_out = (layer_weights[0], layer_weights[1], layer_weights[2])
    slot_index, members, starts = slot_layout(lengths)
    membership, byte_patch, byte_slot = byte_places(starts, lengths)
    counts = lengths.astype(jnp.float32)[:, None]
    pooled = matmul(membership.astype(jnp.bfloat16), byte_rows) / counts
    normed, inverse = normalize(pooled, norm_gains[0])
    normed_low = normed.astype(jnp.bfloat16)
    queries = matmul(normed_low, w_qkv[:, :D]).astype(jnp.bfloat16).reshape(P_SIZE, HEADS, HEAD)
    key_value = matmul(byte_rows, w_qkv[:, D:]).astype(jnp.bfloat16)
    pair_slots = jnp.take(key_value, slot_index, axis=0).reshape(P_SIZE, MOST, 2, HEADS, HEAD)
    scores = (
        jnp.einsum(
            "phd,pkhd->phk", queries, pair_slots[:, :, 0], preferred_element_type=jnp.float32
        )
        * 0.125
    )
    attention = softmax_rows(jnp.where(members[:, None, :], scores, -jnp.inf))
    attended = jnp.einsum(
        "phk,pkhd->phd",
        attention.astype(jnp.bfloat16),
        pair_slots[:, :, 1],
        preferred_element_type=jnp.float32,
    )
    attended = attended.astype(jnp.bfloat16).reshape(P_SIZE, D)
    middle = pooled + matmul(attended, w_out)
    return (
        byte_patch,
        byte_slot,
        counts,
        pooled,
        inverse,
        normed_low,
        queries,
        pair_slots,
        attention,
        attended,
        middle,
    )


def encoder_forward(layer_weights, byte_rows, lengths, patch_valid):
    parts = encoder_parts(layer_weights, byte_rows, lengths)
    pooled, middle = (parts[3], parts[10])
    output_rows = feed_forward(middle, layer_weights[0][1], layer_weights[3], layer_weights[4])
    return jnp.where(patch_valid[:, None], output_rows, pooled)


def encoder_backward(layer_weights, byte_rows, lengths, patch_valid, grad_out):
    norm_gains, w_qkv, w_out, w_gate_up, w_down = layer_weights
    (
        byte_patch,
        byte_slot,
        counts,
        pooled,
        inverse,
        normed_low,
        queries,
        pair_slots,
        attention,
        attended,
        middle,
    ) = encoder_parts(layer_weights, byte_rows, lengths)
    grad_kept = jnp.where(patch_valid[:, None], grad_out, 0.0)
    grad_middle, gain_second, grad_gate_up, grad_down = feed_back(
        middle, norm_gains[1], w_gate_up, w_down, grad_kept
    )
    grad_branch = grad_middle.astype(jnp.bfloat16)
    grad_out_proj = outer_sum(attended, grad_branch)
    grad_attended = (
        times_transposed(grad_branch, w_out).astype(jnp.bfloat16).reshape(P_SIZE, HEADS, HEAD)
    )
    grad_attention = jnp.einsum(
        "phd,pkhd->phk", grad_attended, pair_slots[:, :, 1], preferred_element_type=jnp.float32
    )
    grad_scores = softmax_back(attention, grad_attention)
    grad_queries = (
        jnp.einsum(
            "phk,pkhd->phd", grad_scores, pair_slots[:, :, 0], preferred_element_type=jnp.float32
        )
        * 0.125
    )
    grad_queries = grad_queries.astype(jnp.bfloat16).reshape(P_SIZE, D)
    grad_keys = (
        jnp.einsum("phk,phd->pkhd", grad_scores, queries, preferred_element_type=jnp.float32)
        * 0.125
    )
    grad_values = jnp.einsum(
        "phk,phd->pkhd",
        attention.astype(jnp.bfloat16),
        grad_attended,
        preferred_element_type=jnp.float32,
    )
    grad_pairs = jnp.stack([grad_keys, grad_values], axis=2).reshape(P_SIZE * MOST, 2 * D)
    grad_key_value = jnp.take(grad_pairs, byte_slot, axis=0).astype(jnp.bfloat16)
    grad_qkv = jnp.concatenate(
        [outer_sum(normed_low, grad_queries), outer_sum(byte_rows, grad_key_value)], axis=1
    )
    grad_normed = times_transposed(grad_queries, w_qkv[:, :D])
    grad_in, gain_first = normalize_back(pooled, norm_gains[0], inverse, grad_normed)
    grad_pooled = jnp.where(patch_valid[:, None], 0.0, grad_out) + grad_middle + grad_in
    grad_bytes = jnp.take(grad_pooled / counts, byte_patch, axis=0)
    grad_bytes = grad_bytes + times_transposed(grad_key_value, w_qkv[:, D:])
    weight_grads = (
        jnp.stack([gain_first, gain_second]),
        grad_qkv,
        grad_out_proj,
        grad_gate_up,
        grad_down,
    )
    return (grad_bytes, weight_grads)


def causal_parts(layer_weights, inputs):
    norm_gains, w_qkv, w_out = (layer_weights[0], layer_weights[1], layer_weights[2])
    normed, inverse = normalize(inputs, norm_gains[0])
    normed_low = normed.astype(jnp.bfloat16)
    mixed_rows = matmul(normed_low, w_qkv).astype(jnp.bfloat16).reshape(P_SIZE, 3, HEADS, HEAD)
    scores = (
        jnp.einsum(
            "qhd,khd->hqk", mixed_rows[:, 0], mixed_rows[:, 1], preferred_element_type=jnp.float32
        )
        * 0.125
    )
    positions = jnp.arange(P_SIZE, dtype=jnp.int32)
    causal = positions[:, None] >= positions[None, :]
    attention = softmax_rows(jnp.where(causal[None], scores, -jnp.inf))
    attended = jnp.einsum(
        "hqk,khd->qhd",
        attention.astype(jnp.bfloat16),
        mixed_rows[:, 2],
        preferred_element_type=jnp.float32,
    )
    attended = attended.astype(jnp.bfloat16).reshape(P_SIZE, D)
    middle = inputs + matmul(attended, w_out)
    return (inverse, normed_low, mixed_rows, attention, attended, middle)


def global_forward(layer_weights, inputs, patch_valid):
    middle = causal_parts(layer_weights, inputs)[5]
    output_rows = feed_forward(middle, layer_weights[0][1], layer_weights[3], layer_weights[4])
    return jnp.where(patch_valid[:, None], output_rows, inputs)


def global_backward(layer_weights, inputs, patch_valid, grad_out):
    norm_gains, w_qkv, w_out, w_gate_up, w_down = layer_weights
    inverse, normed_low, mixed_rows, attention, attended, middle = causal_parts(
        layer_weights, inputs
    )
    grad_kept = jnp.where(patch_valid[:, None], grad_out, 0.0)
    grad_middle, gain_second, grad_gate_up, grad_down = feed_back(
        middle, norm_gains[1], w_gate_up, w_down, grad_kept
    )
    grad_branch = grad_middle.astype(jnp.bfloat16)
    grad_out_proj = outer_sum(attended, grad_branch)
    grad_attended = (
        times_transposed(grad_branch, w_out).astype(jnp.bfloat16).reshape(P_SIZE, HEADS, HEAD)
    )
    query_heads, key_heads, value_heads = (mixed_rows[:, 0], mixed_rows[:, 1], mixed_rows[:, 2])
    grad_attention = jnp.einsum(
        "qhd,khd->hqk", grad_attended, value_heads, preferred_element_type=jnp.float32
    )
    grad_scores = softmax_back(attention, grad_attention)
    grad_queries = (
        jnp.einsum("hqk,khd->qhd", grad_scores, key_heads, preferred_element_type=jnp.float32)
        * 0.125
    )
    grad_keys = (
        jnp.einsum("hqk,qhd->khd", grad_scores, query_heads, preferred_element_type=jnp.float32)
        * 0.125
    )
    grad_values = jnp.einsum(
        "hqk,qhd->khd",
        attention.astype(jnp.bfloat16),
        grad_attended,
        preferred_element_type=jnp.float32,
    )
    grad_mixed = (
        jnp.stack([grad_queries, grad_keys, grad_values], axis=1)
        .astype(jnp.bfloat16)
        .reshape(P_SIZE, 3 * D)
    )
    grad_qkv = outer_sum(normed_low, grad_mixed)
    grad_normed = times_transposed(grad_mixed, w_qkv)
    grad_in, gain_first = normalize_back(inputs, norm_gains[0], inverse, grad_normed)
    grad_inputs = jnp.where(patch_valid[:, None], 0.0, grad_out) + grad_middle + grad_in
    weight_grads = (
        jnp.stack([gain_first, gain_second]),
        grad_qkv,
        grad_out_proj,
        grad_gate_up,
        grad_down,
    )
    return (grad_inputs, weight_grads)


def on_device(
    byte_ids,
    hash_ids,
    patch_lengths,
    row_lengths,
    byte_table,
    hash_tables,
    norm_gains,
    w_qkv,
    w_out,
    w_gate_up,
    w_down,
    cotangent,
):
    layer_weights = (norm_gains[0], w_qkv[0], w_out[0], w_gate_up[0], w_down[0])
    section_first = lax.axis_index("section") == 0
    devices = lax.axis_size("rows")
    count_tables, shard_rows, half_width = hash_tables.shape
    positions = M * L
    flat_ids = hash_ids.reshape(positions, count_tables).T
    owners = flat_ids // shard_rows
    local_rows = (
        flat_ids % shard_rows + jnp.arange(count_tables, dtype=jnp.int32)[:, None] * shard_rows
    )
    ordering = jnp.argsort(owners, axis=1, stable=True)
    inverse_order = jnp.argsort(ordering, axis=1)
    grouped = jnp.take_along_axis(local_rows, ordering, axis=1).reshape(count_tables, devices, -1)
    flat_tables = hash_tables.reshape(count_tables * shard_rows, half_width)
    requested = lax.all_to_all(grouped, "rows", split_axis=1, concat_axis=1, tiled=True)
    found_rows = jnp.take(flat_tables, requested, axis=0)
    returned, requested = (
        lax.all_to_all(found_rows, "rows", split_axis=1, concat_axis=1, tiled=True),
        requested,
    )
    returned = jnp.take_along_axis(
        returned.reshape(count_tables, positions, half_width), inverse_order[:, :, None], axis=1
    )
    one_hot = (
        byte_ids.reshape(positions)[:, None]
        == jnp.arange(byte_table.shape[0], dtype=jnp.int32)[None, :]
    ).astype(jnp.bfloat16)
    own_half = (matmul(one_hot, byte_table) + jnp.sum(returned.astype(jnp.float32), axis=0)).astype(
        jnp.bfloat16
    )
    other_half = shifted_2(own_half, "section", -1)
    byte_rows = jnp.concatenate([own_half, other_half], axis=1).reshape(M, L, D)
    patch_valid = jnp.arange(P_SIZE, dtype=jnp.int32)[None, :] < row_lengths[:, None]

    def run_first(operands):
        rows_in, lengths, valid_first, received, valid_second = operands
        return encoder_forward(layer_weights, rows_in, lengths, valid_first).astype(jnp.bfloat16)

    def run_second(operands):
        rows_in, lengths, valid_first, received, valid_second = operands
        return global_forward(layer_weights, received.astype(jnp.float32), valid_second).astype(
            jnp.bfloat16
        )

    def run_spare(operands):
        return jnp.zeros((P_SIZE, D), jnp.bfloat16)

    received = jnp.zeros((P_SIZE, D), jnp.bfloat16)
    inputs_second = []
    results = []
    for tick_index in range(M + 1):
        first_batch = min(tick_index, M - 1)
        second_batch = max(tick_index - 1, 0)
        operands = (
            byte_rows[first_batch],
            patch_lengths[first_batch],
            patch_valid[first_batch],
            received,
            patch_valid[second_batch],
        )
        if tick_index == 0:
            branches = (run_first, run_spare)
        elif tick_index == M:
            branches = (run_spare, run_second)
        else:
            branches = (run_first, run_second)
        result = lax.cond(section_first, branches[0], branches[1], operands)
        results.append(result)
        if tick_index < M:
            received = shifted_2(result, "section", 1)
            inputs_second.append(received)
    section_out = jnp.stack(
        [
            jnp.where(section_first, results[micro_batch], results[micro_batch + 1])
            for micro_batch in range(M)
        ]
    )[None]
    upstream = cotangent[0].astype(jnp.float32)

    def zero_grads():
        return tuple((jnp.zeros(weight_array.shape, jnp.float32) for weight_array in layer_weights))

    def back_first(operands):
        rows_in, lengths, valid_first, received_in, valid_second, grad_out = operands
        grad_bytes, weight_grads = encoder_backward(
            layer_weights, rows_in, lengths, valid_first, grad_out
        )
        return (jnp.zeros((P_SIZE, D), jnp.bfloat16), grad_bytes, weight_grads)

    def back_second(operands):
        rows_in, lengths, valid_first, received_in, valid_second, grad_out = operands
        grad_inputs, weight_grads = global_backward(
            layer_weights, received_in.astype(jnp.float32), valid_second, grad_out
        )
        return (grad_inputs.astype(jnp.bfloat16), jnp.zeros((L, D), jnp.float32), weight_grads)

    def back_spare(operands):
        return (jnp.zeros((P_SIZE, D), jnp.bfloat16), jnp.zeros((L, D), jnp.float32), zero_grads())

    totals = zero_grads()
    byte_grads = [jnp.zeros((L, D), jnp.float32) for micro_batch in range(M)]
    returned_grad = jnp.zeros((P_SIZE, D), jnp.bfloat16)
    for tick_index in range(M + 1):
        first_batch = min(M - tick_index, M - 1)
        second_batch = max(M - 1 - tick_index, 0)
        grad_first = upstream[first_batch] + returned_grad.astype(jnp.float32)
        grad_out = jnp.where(section_first, grad_first, upstream[second_batch])
        operands = (
            byte_rows[first_batch],
            patch_lengths[first_batch],
            patch_valid[first_batch],
            inputs_second[second_batch],
            patch_valid[second_batch],
            grad_out,
        )
        if tick_index == 0:
            branches = (back_spare, back_second)
        elif tick_index == M:
            branches = (back_first, back_spare)
        else:
            branches = (back_first, back_second)
        sent_grad, grad_bytes, weight_grads = lax.cond(
            section_first, branches[0], branches[1], operands
        )
        if tick_index >= 1:
            byte_grads[first_batch] = grad_bytes
        totals = tuple((running + addend for running, addend in zip(totals, weight_grads)))
        if tick_index < M:
            returned_grad = shifted_2(sent_grad, "section", -1)
    totals = (
        lax.psum_scatter(totals[0], "rows", scatter_dimension=1, tiled=True),
        lax.psum_scatter(totals[1], "rows", scatter_dimension=0, tiled=True),
        lax.psum_scatter(totals[2], "rows", scatter_dimension=0, tiled=True),
        lax.psum_scatter(totals[3], "rows", scatter_dimension=0, tiled=True),
        lax.psum_scatter(totals[4], "rows", scatter_dimension=1, tiled=True),
    )
    grad_rows = jnp.stack(byte_grads).reshape(positions, D).astype(jnp.bfloat16)
    upper_half = shifted_2(grad_rows[:, half_width:], "section", 1)
    own_grad = jnp.where(section_first, grad_rows[:, :half_width], upper_half)
    byte_table_grad = lax.psum(outer_sum(one_hot, own_grad), "rows")
    sorted_grad = jnp.take(own_grad, ordering, axis=0).reshape(
        count_tables, devices, -1, half_width
    )
    arrived = lax.all_to_all(sorted_grad, "rows", split_axis=1, concat_axis=1, tiled=True)
    hash_grad = jax.ops.segment_sum(
        arrived.reshape(-1, half_width).astype(jnp.float32),
        requested.reshape(-1),
        num_segments=count_tables * shard_rows,
    )
    hash_grad = hash_grad.reshape(count_tables, shard_rows, half_width)
    return (
        section_out,
        byte_table_grad,
        hash_grad,
        totals[0][None],
        totals[1][None],
        totals[2][None],
        totals[3][None],
        totals[4][None],
    )


def solution(mesh):
    return jax.shard_map(
        on_device,
        mesh=mesh,
        in_specs=(
            P("rows", None),
            P("rows", None, None),
            P("rows", None),
            P("rows"),
            P(None, "section"),
            P(None, "rows", "section"),
            P("section", None, None),
            P("section", None, None),
            P("section", None, None),
            P("section", None, None),
            P("section", None, None),
            P("section", "rows", None, None),
        ),
        out_specs=(
            P("section", "rows", None, None),
            P(None, "section"),
            P(None, "rows", "section"),
            P("section", None, "rows"),
            P("section", "rows", None),
            P("section", "rows", None),
            P("section", "rows", None),
            P("section", None, "rows"),
        ),
        check_vma=False,
    )
```

profile of v0, /device:TPU:0, one launch (start us, length us, event | category | flops | bytes accessed | tf_op | source)
XLA Modules:
  0.0 2812.3 jit_solution(10437719894862134980)
XLA Ops:
  16.4 52.1 %gather_fusion.12 = s32[6144]{0:T(1024)S(1)} fusion(s32[3,2048]{1,0:T(4,128)S(1)} %get-tuple-element.716, s32[6144]{0:T(1024)S(1)} %reshape.738), kind=kCustom, calls=%fused_computation.12 | custom fusion | bytes 98304 | tf_op jit(solution)/shard_map/jit(take_along_axis)/gather | solution.py:328
  68.5 15.5 all_to_all.15
  84.7 37.1 %gather_fusion.10 = bf16[6144,512]{1,0:T(8,128)(2,1)} fusion(bf16[24576,512]{1,0:T(8,128)(2,1)} %bitcast.453, s32[6144]{0:T(1024)S(1)} %broadcast_clamp_fusion.7), kind=kCustom, calls=%fused_computation.10 | custom fusion | bytes 12607488 | tf_op jit(solution)/shard_map/jit(_take)/gather | solution.py:331
  145.7 103.0 %all-to-all-done.1 = bf16[3,16,128,512]{3,2,0,1:T(8,128)(2,1)} async-done(((bf16[3,16,128,512]{3,2,0,1:T(8,128)(2,1)}), bf16[3,16,128,512]{3,2,0,1:T(8,128)(2,1)}, u32[]{:S(2)}, u32[]{:S(2)}) %all-to-all-start.1) | async-done | bytes 6291488 | tf_op jit(solution)/shard_map/all_to_all | solution.py:333
  254.8 112.8 %gather_fusion.13 = bf16[6144,512]{1,0:T(8,128)(2,1)} fusion(bf16[3,2048,512]{2,1,0:T(8,128)(2,1)} %bitcast.436, s32[6144]{0:T(1024)S(1)} %reshape.744), kind=kCustom, calls=%fused_computation.13 | custom fusion | bytes 12632064 | tf_op jit(solution)/shard_map/jit(take_along_axis)/gather | solution.py:336
  394.2 120.8 %conditional.11 = (bf16[256,1024]{1,0:T(8,128)(2,1)}) conditional(s32[]{:T(128)} %convert_element_type.381, () %tuple.68, (pred[1,256]{1,0:T(4,128)(4,1)S(1)}, s32[256]{0:T(256)S(1)}, bf16[1024,1024]{0,1:T(8,128)(2,1)}, s32[1,256]{1,0:T(1,128)S(1)}, bf16[2,1024]{1,0:T(2,128)(2,1)S(1)}, /*index=5*/bf16[1024,3072]{1,0:T(8,128)(2,1)}, ...), branch_computations={%region_3.4_spmd, %region_4.12_spmd} | conditional | flops 10379892736 | bytes 186312576 | solution.py:382
  412.5 34.3 %gather_fusion = bf16[4096,2048]{1,0:T(8,128)(2,1)} fusion(bf16[1024,2048]{1,0:T(8,128)(2,1)} %fusion.109, s32[4096]{0:T(1024)S(1)} %broadcast_clamp_fusion), kind=kCustom, calls=%fused_computation.clone | custom fusion | bytes 33570816 | tf_op jit(solution)/shard_map/cond/branch_1_fun/jit(_take)/gather | solution.py:116
  446.8 23.8 copy.281
  470.6 14.1 broadcast_select_fusion
  518.0 123.9 %conditional.12 = (bf16[256,1024]{1,0:T(8,128)(2,1)S(1)}) conditional(s32[]{:T(128)} %convert_element_type.381, (pred[1,256]{1,0:T(4,128)(4,1)S(1)}, bf16[256,1024]{1,0:T(8,128)(2,1)S(1)}, bf16[2,1024]{1,0:T(2,128)(2,1)S(1)}, bf16[1024,3072]{1,0:T(8,128)(2,1)}, bf16[1024,1024]{1,0:T(8,128)(2,1)S(1)}, /*index=5*/bf16[1024,5632]{1,0:T(8,128)(2,1)}, ...), branch_computations={%region_11.17_spmd, %region_16.24_spmd} | conditional | flops 10379892736 | bytes 194701248
  539.6 34.2 %gather_fusion.1 = bf16[4096,2048]{1,0:T(8,128)(2,1)} fusion(bf16[1024,2048]{1,0:T(8,128)(2,1)} %fusion.162, s32[4096]{0:T(1024)S(1)} %broadcast_clamp_fusion.1), kind=kCustom, calls=%fused_computation.4.clone | custom fusion | bytes 33570816 | tf_op jit(solution)/shard_map/cond/branch_1_fun/jit(_take)/gather | solution.py:116
  573.8 23.8 copy.284
  597.6 14.1 broadcast_select_fusion.1
  647.8 29.6 %conditional.14 = (bf16[256,1024]{1,0:T(8,128)(2,1)S(1)}, f32[2,1024]{1,0:T(2,128)S(1)}, f32[1024,3072]{1,0:T(8,128)}, f32[1024,1024]{1,0:T(8,128)S(1)}, f32[1024,5632]{1,0:T(8,128)}, /*index=5*/f32[2816,1024]{0,1:T(8,128)}) conditional(s32[]{:T(128)} %convert_element_type.381, (pred[1,256]{1,0:T(4,128)(4,1)S(1)}, f32[256,1024]{1,0:T(8,128)}, ...), branch_computations={%region_29.40_spmd.clone, %region_39.41_spmd} | conditional | flops 19120652288 | bytes 436810048 | solution.py:437
  678.7 51.4 %collective-permute-done.3 = bf16[256,1024]{1,0:T(8,128)(2,1)S(1)} collective-permute-done((bf16[256,1024]{1,0:T(8,128)(2,1)S(1)}, bf16[256,1024]{1,0:T(8,128)(2,1)S(1)}, u32[]{:S(2)}, u32[]{:S(2)}) %collective-permute-start.3) | collective-permute-done | bytes 524320 | tf_op jit(solution)/shard_map/ppermute | solution.py:22
  732.0 366.5 %conditional.15 = (bf16[256,1024]{1,0:T(8,128)(2,1)S(1)}, f32[2,1024]{1,0:T(2,128)S(1)}, f32[1024,1024]{1,0:T(8,128)}, f32[1024,5632]{1,0:T(8,128)}, bf16[1,1024...) conditional(s32[]{:T(128)} %convert_element_type.381, (pred[1,256]{1,0:T(4,128)(4,1)S(1)}, ...), branch_computations={%region_40.51_spmd, %region_50.67_spmd} | conditional | flops 28596518912 | bytes 649171520 | solution.py:437
  754.9 34.5 %gather_fusion.2 = bf16[4096,2048]{1,0:T(8,128)(2,1)} fusion(bf16[1024,2048]{1,0:T(8,128)(2,1)} %convolution_convert_fusion.6, s32[4096]{0:T(1024)S(1)} %broadcast_clamp_fusion.2), kind=kCustom, calls=%fused_computation.5.clone | custom fusion | bytes 33570816 | tf_op jit(solution)/shard_map/cond/branch_1_fun/jit(_take)/gather | solution.py:116
  789.4 23.8 copy.287
  896.0 22.5 multiply_bitcast_fusion
  918.4 22.7 pad_maximum_fusion.5
  941.2 46.3 %reshape.604 = bf16[4096,2048]{1,0:T(8,128)(2,1)} reshape(bf16[256,16,2,16,64]{4,3,2,1,0:T(8,128)(2,1)} %pad_maximum_fusion.5) | data formatting | bytes 33554432 | tf_op jit(solution)/shard_map/cond/branch_1_fun/reshape | solution.py:199
  994.6 16.7 gather_fusion.4
  1011.3 11.0 convolution_bitcast_fusion
  1032.9 12.1 pad_maximum_fusion.6
  1045.0 12.8 copy.416
  1066.6 10.6 fusion.218
  1103.4 365.3 %conditional.16 = (f32[2,1024]{1,0:T(2,128)S(1)}, f32[1024,1024]{1,0:T(8,128)}, f32[1024,5632]{1,0:T(8,128)}, bf16[1,1024,1024]{2,1,0:T(8,128)(2,1)}, f32[1024,3072]{1,0:T(8,128)}, /*index=5*/f32[2816,1024]{0,1:T(8,128)}) conditional(s32[]{:T(128)} %convert_element_type.381, () %tuple.74, (s32[1,256]{1,0:T(1,128)}, s32[256]{0:T(256)}, ...), branch_computations={%region_63.68_spmd, %region_64.81_spmd} | conditional | flops 28597043200 | bytes 660202112 | solution.py:437
  1124.4 34.1 %gather_fusion.6 = bf16[4096,2048]{1,0:T(8,128)(2,1)} fusion(bf16[1024,2048]{1,0:T(8,128)(2,1)} %convolution_convert_fusion.8, s32[4096]{0:T(1024)S(1)} %broadcast_clamp_fusion.4), kind=kCustom, calls=%fused_computation.6.clone | custom fusion | bytes 33570816 | tf_op jit(solution)/shard_map/cond/branch_1_fun/jit(_take)/gather | solution.py:116
  1158.4 23.8 copy.293
  1265.6 22.5 multiply_bitcast_fusion.2
  1288.1 22.7 pad_maximum_fusion.11
  1310.8 45.9 %reshape.612 = bf16[4096,2048]{1,0:T(8,128)(2,1)} reshape(bf16[256,16,2,16,64]{4,3,2,1,0:T(8,128)(2,1)} %pad_maximum_fusion.11) | data formatting | bytes 33554432 | tf_op jit(solution)/shard_map/cond/branch_1_fun/reshape | solution.py:199
  1363.8 17.0 gather_fusion.8
  1380.8 11.1 convolution_bitcast_fusion.1
  1402.3 12.1 pad_maximum_fusion.12
  1414.5 13.0 copy.420
  1436.3 10.6 fusion.266
  1491.9 16.4 add_add_fusion.2
  1508.4 19.1 add_add_fusion.1
  1527.5 30.5 %add_add_fusion = f32[1024,5632]{1,0:T(8,128)} fusion(f32[1024,5632]{1,0:T(8,128)} %get-tuple-element.290, f32[1024,5632]{1,0:T(8,128)} %get-tuple-element.288, f32[1024,5632]{1,0:T(8,128)} %get-tuple-element.289), kind=kLoop, calls=%fused_computation.584 | loop fusion | flops 11534336 | bytes 92274688 | tf_op jit(solution)/shard_map/add | solution.py:442
  1558.8 25.5 gather_fusion.11
  1591.3 28.5 %all-to-all-start.2 = ((bf16[3,16,128,512]{3,2,0,1:T(8,128)(2,1)}), bf16[3,16,128,512]{3,2,0,1:T(8,128)(2,1)}, u32[]{:S(2)}, u32[]{:S(2)}) async-start(bf16[3,16,128,512]{3,2,0,1:T(8,128)(2,1)} %copy_select_fusion), calls=%async_computation.2 | async-start | bytes 12582912 | tf_op jit(solution)/shard_map/all_to_all | solution.py:459
  1631.1 111.5 %all-to-all-done.2 = bf16[3,16,128,512]{3,2,0,1:T(8,128)(2,1)} async-done(((bf16[3,16,128,512]{3,2,0,1:T(8,128)(2,1)}), bf16[3,16,128,512]{3,2,0,1:T(8,128)(2,1)}, u32[]{:S(2)}, u32[]{:S(2)}) %all-to-all-start.2) | async-done | bytes 6291488 | tf_op jit(solution)/shard_map/all_to_all | solution.py:459
  1748.7 58.2 %scatter_custom_fusion = f32[24576,512]{1,0:T(8,128)} fusion(s32[6144]{0:T(1024)} %bitcast.547, f32[]{:T(128)} %constant.311.clone.1, bf16[6144,512]{1,0:T(8,128)(2,1)} %bitcast.465), kind=kCustom, calls=%fused_computation.582 | custom fusion | flops 6291456 | bytes 56623616 | tf_op jit(solution)/shard_map/scatter-add | solution.py:460
  1806.9 62.6 %reduce-scatter.10.cloned.1.call-done = f32[64,1024]{1,0:T(8,128)} async-done(((f32[1024,1024]{1,0:T(8,128)}), f32[64,1024]{1,0:T(8,128)}) %reduce-scatter.10.cloned.1.call-update) | async-done | bytes 262160 | tf_op jit(solution)/shard_map/reduce_scatter | solution.py:448
  1869.5 243.2 %reduce-scatter.14.cloned.1.call-done = f32[2816,64]{0,1:T(8,128)} async-done(((f32[2816,1024]{0,1:T(8,128)}), f32[2816,64]{0,1:T(8,128)}) %reduce-scatter.14.cloned.1.call-update) | async-done | bytes 720912 | tf_op jit(solution)/shard_map/reduce_scatter | solution.py:450
  2112.7 214.9 %reduce-scatter.8.cloned.1.call-done = f32[64,3072]{1,0:T(8,128)} async-done(((f32[1024,3072]{1,0:T(8,128)}), f32[64,3072]{1,0:T(8,128)}) %reduce-scatter.8.cloned.1.call-update) | async-done | bytes 786448 | tf_op jit(solution)/shard_map/reduce_scatter | solution.py:447
  2327.7 475.6 %reduce-scatter.12.cloned.1.call-done = f32[64,5632]{1,0:T(8,128)} async-done(((f32[1024,5632]{1,0:T(8,128)}), f32[64,5632]{1,0:T(8,128)}) %reduce-scatter.12.cloned.1.call-update) | async-done | bytes 1441808 | tf_op jit(solution)/shard_map/reduce_scatter | solution.py:449
  (450 shorter events, 548.9 us)
Async XLA Ops:
  7.2 372.4 %copy-start = (bf16[260,512]{1,0:T(8,128)(2,1)S(1)}, bf16[260,512]{1,0:T(8,128)(2,1)}, u32[]{:S(2)}) copy-start(bf16[260,512]{1,0:T(8,128)(2,1)} %param.36) | copy-start | bytes 798724
  128.5 120.1 %all-to-all-start.1 = ((bf16[3,16,128,512]{3,2,0,1:T(8,128)(2,1)}), bf16[3,16,128,512]{3,2,0,1:T(8,128)(2,1)}, u32[]{:S(2)}, u32[]{:S(2)}) async-start(bf16[3,16,128,512]{3,2,0,1:T(8,128)(2,1)} %copy_select_fusion.1), calls=%async_computation.1 | async-start | bytes 12582912 | tf_op jit(solution)/shard_map/all_to_all | solution.py:333
  133.3 10.8 sort.39.cloned.1.call-start
  134.0 1495.7 %reduce-scatter.16.cloned.1.call-start = ((), (), s32[]{:S(2)}) async-start(), calls=%async_computation.13 | async-start | bytes 557056
  134.1 245.4 %copy-start.105 = (s32[1,8,2,128]{3,1,2,0:T(8,128)}, s32[1,8,2,128]{3,1,2,0:T(8,128)S(1)}, u32[]{:S(2)}) copy-start(s32[1,8,2,128]{3,1,2,0:T(8,128)S(1)} %copy.468) | copy-start | bytes 24580
  383.9 6.4 collective-permute-start
  385.3 346.6 %copy-start.113 = (pred[1,256]{1,0:T(4,128)(4,1)}, pred[1,256]{1,0:T(4,128)(4,1)S(1)}, u32[]{:S(2)}) copy-start(pred[1,256]{1,0:T(4,128)(4,1)S(1)} %get-tuple-element.719) | copy-start | bytes 772
  385.3 8.9 copy-start.99
  385.3 8.9 copy-start.2
  385.3 8.8 copy-start.93
  515.0 3.0 collective-permute-start.1
  597.6 14.2 copy-start.63
  625.3 9.8 copy-start.61
  641.9 5.4 collective-permute-start.2
  677.4 54.6 %copy-start.36 = (f32[1024,1024]{1,0:T(8,128)}, f32[1024,1024]{1,0:T(8,128)S(1)}, u32[]{:S(2)}) copy-start(f32[1024,1024]{1,0:T(8,128)S(1)} %get-tuple-element.285) | copy-start | bytes 12582916
  677.4 54.6 %copy-start.109 = (f32[2,1024]{1,0:T(2,128)}, f32[2,1024]{1,0:T(2,128)S(1)}, u32[]{:S(2)}) copy-start(f32[2,1024]{1,0:T(2,128)S(1)} %get-tuple-element.279) | copy-start | bytes 24580
  677.4 52.7 %collective-permute-start.3 = (bf16[256,1024]{1,0:T(8,128)(2,1)S(1)}, bf16[256,1024]{1,0:T(8,128)(2,1)S(1)}, u32[]{:S(2)}, u32[]{:S(2)}) collective-permute-start(bf16[256,1024]{1,0:T(8,128)(2,1)S(1)} %get-tuple-element.275), channel_id=1, source_target_pairs={{16,0},{17,1},{18,2},{19,3},{20,4},{21,5},{22,6},{23,7},{24,8},{25... | collective-permute-start | bytes 1572872 | tf_op jit(solution)/shard_map/ppermute | solution.py:22
  846.9 10.6 copy-start.59
  847.7 9.8 copy-start.22
  847.7 9.8 copy-start.15
  857.5 8.4 copy-start.23
  885.7 7.7 copy-start.40
  1066.6 10.6 copy-start.24
  1066.6 10.6 copy-start.78
  1066.6 10.6 copy-start.80
  1077.3 9.6 copy-start.60
  1098.5 3.8 collective-permute-start.4
  1111.1 13.3 copy-start.115
  1216.3 10.7 copy-start.57
  1217.2 25.7 copy-start.20
  1217.2 9.8 copy-start.68
  1217.2 9.8 copy-start.69
  1255.4 7.7 copy-start.39
  1436.2 10.6 copy-start.21
  1436.2 10.6 copy-start.82
  1436.3 10.6 copy-start.84
  1446.9 10.1 copy-start.58
  1473.8 5.2 collective-permute-start.5
  1477.5 329.4 %all-reduce.2.cloned.1.call-start = ((), (), s32[]{:S(2)}) async-start(), calls=%async_computation.8 | async-start | bytes 1081344 | tf_op jit(solution)/shard_map/psum | solution.py:455
  1483.0 386.5 %reduce-scatter.10.cloned.1.call-start = ((), (), s32[]{:S(2)}) async-start(), calls=%async_computation.10 | async-start | bytes 4456448 | tf_op jit(solution)/shard_map/reduce_scatter | solution.py:448
  1491.8 620.9 %reduce-scatter.14.cloned.1.call-start = ((), (), s32[]{:S(2)}) async-start(), calls=%async_computation.12 | async-start | bytes 12255232 | tf_op jit(solution)/shard_map/reduce_scatter | solution.py:450
  1508.3 819.4 %reduce-scatter.8.cloned.1.call-start = ((), (), s32[]{:S(2)}) async-start(), calls=%async_computation.9 | async-start | bytes 13369344 | tf_op jit(solution)/shard_map/reduce_scatter | solution.py:447
  1527.5 1275.8 %reduce-scatter.12.cloned.1.call-start = ((), (), s32[]{:S(2)}) async-start(), calls=%async_computation.11 | async-start | bytes 24510464 | tf_op jit(solution)/shard_map/reduce_scatter | solution.py:449
  1591.3 28.5 %copy-start.3 = (bf16[1,1024,1024]{2,1,0:T(8,128)(2,1)S(1)}, bf16[1,1024,1024]{2,1,0:T(8,128)(2,1)}, u32[]{:S(2)}) copy-start(bf16[1,1024,1024]{2,1,0:T(8,128)(2,1)} %param.40) | copy-start | bytes 6291460
  1591.3 28.5 %copy-start.94 = (bf16[1,2,1024]{2,1,0:T(2,128)(2,1)S(1)}, bf16[1,2,1024]{2,1,0:T(2,128)(2,1)}, u32[]{:S(2)}) copy-start(bf16[1,2,1024]{2,1,0:T(2,128)(2,1)} %param.38) | copy-start | bytes 12292
  1591.3 28.5 %copy-start.114 = (pred[1,256]{1,0:T(4,128)(4,1)S(1)}, pred[1,256]{1,0:T(4,128)(4,1)}, u32[]{:S(2)}) copy-start(pred[1,256]{1,0:T(4,128)(4,1)} %copy-done.113) | copy-start | bytes 772
  1591.3 151.3 %all-to-all-start.2 = ((bf16[3,16,128,512]{3,2,0,1:T(8,128)(2,1)}), bf16[3,16,128,512]{3,2,0,1:T(8,128)(2,1)}, u32[]{:S(2)}, u32[]{:S(2)}) async-start(bf16[3,16,128,512]{3,2,0,1:T(8,128)(2,1)} %copy_select_fusion), calls=%async_computation.2 | async-start | bytes 12582912 | tf_op jit(solution)/shard_map/all_to_all | solution.py:459
  1748.7 1056.4 %copy-start.1 = (bf16[260,512]{1,0:T(8,128)(2,1)S(1)}, bf16[260,512]{1,0:T(8,128)(2,1)}, u32[]{:S(2)}) copy-start(bf16[260,512]{1,0:T(8,128)(2,1)} %param.36) | copy-start | bytes 798724
  (64 other events, 273.4 us)
Sparse Core Ops, SparseCore 0:
  11.1 3.4 sort.41.cloned.1.call-done
  137.3 6.4 sort.43.cloned.1.call-done
  1477.6 99.2 reduce-scatter.15
  1583.6 187.0 all-reduce.1
  1773.4 96.0 reduce-scatter.9
  1872.2 240.4 reduce-scatter.13
  2119.0 208.6 reduce-scatter.7
  2330.7 472.5 reduce-scatter.11
  (2 shorter events, 0.0 us)
where the time goes:
time: 2830 us; the launch traced here: 2810 us
  waiting for transfers between devices  1270 us (45%)
  local copies, waits for them, and re-layouts  758 us (27%)
  other arithmetic  431 us (15%)
  matrix products  248 us (9%)
  starting transfers between devices  43.7 us (2%)
    reduce_scatter x1, waiting for transfers between devices, on_device(): lax.psum_scatter(totals[3], 'rows', scatter_dimension=0, tiled=True)  476 us
    reduce_scatter x1, waiting for transfers between devices, on_device(): lax.psum_scatter(totals[4], 'rows', scatter_dimension=1, tiled=True)  243 us
    gather x8, local copies, waits for them, and re-layouts, encoder_parts(): jnp.take(key_value, slot_index, axis=0)  232 us
    reduce_scatter x1, waiting for transfers between devices, on_device(): lax.psum_scatter(totals[1], 'rows', scatter_dimension=0, tiled=True)  215 us
    dot_general x23, matrix products, matmul(): return jnp.dot(left_side, right_side, preferred_element_type=jnp.float32)  117 us
    gather x2, local copies, waits for them, and re-layouts, on_device(): jnp.take_along_axis(returned.reshape(count_tables, positions, half_width)...  113 us
    all_to_all x1, waiting for transfers between devices, on_device(): lax.all_to_all(sorted_grad, 'rows', split_axis=1, concat_axis=1, tiled=True)  112 us
    all_to_all x1, waiting for transfers between devices, on_device(): lax.all_to_all(found_rows, 'rows', split_axis=1, concat_axis=1, tiled=True)  103 us
  transfers between devices with their start and end apart: 14, of which 11 were waited for; matrix products, arithmetic and copies ran while one was open for 7% of the time, Pallas kernels for 0%

commit v1 on v0

v1 whole, which is shorter than its diff:
```python
import functools

import jax
import jax.numpy as jnp
from jax import lax
from jax.experimental import pallas as pl
from jax.experimental.pallas import tpu as pltpu
from jax.sharding import PartitionSpec as P

D = 1024
HEADS = 16
HEAD = 64
FF = 2816
L = 1024
MOST = 16
M = 2
P_SIZE = 256
GROUP = 512
VMEM_BYTES = 48 * 1024 * 1024

epsilon = 1e-05
f32 = jnp.float32
bf16 = jnp.bfloat16


def dot(left, right):
    return jnp.dot(left, right, preferred_element_type=f32)


def dot_nt(left, right):
    return lax.dot_general(left, right, (((1,), (1,)), ((), ())), preferred_element_type=f32)


def dot_tn(left, right):
    return lax.dot_general(left, right, (((0,), (0,)), ((), ())), preferred_element_type=f32)


def params(*semantics):
    return pltpu.CompilerParams(vmem_limit_bytes=VMEM_BYTES, dimension_semantics=semantics)


def combine_kernel(slots_ref, ids_ref, rows_ref, table_ref, out_ref):
    tile = out_ref.shape[0]
    first = pl.program_id(0) * tile
    places = first + lax.broadcasted_iota(jnp.int32, (tile, slots_ref.shape[1]), 0)
    chosen = (places == slots_ref[...]).astype(f32).astype(bf16)
    words = lax.broadcasted_iota(jnp.int32, (tile, table_ref.shape[0]), 1)
    word = (words == ids_ref[...]).astype(f32).astype(bf16)
    total = dot(chosen, rows_ref[...]) + dot(word, table_ref[...])
    out_ref[...] = total.astype(bf16)


def combine(slots, ids, rows, table):
    count, width = rows.shape
    positions = ids.shape[0]
    tile = 256
    return pl.pallas_call(
        combine_kernel,
        grid=(positions // tile,),
        in_specs=[
            pl.BlockSpec((1, count), lambda i: (0, 0)),
            pl.BlockSpec((tile, 1), lambda i: (i, 0)),
            pl.BlockSpec((count, width), lambda i: (0, 0)),
            pl.BlockSpec(table.shape, lambda i: (0, 0)),
        ],
        out_specs=pl.BlockSpec((tile, width), lambda i: (i, 0)),
        out_shape=jax.ShapeDtypeStruct((positions, width), bf16),
        compiler_params=params("arbitrary"),
        cost_estimate=pl.CostEstimate(
            flops=2 * positions * count * width, bytes_accessed=12 * count * width // 4, transcendentals=0
        ),
        name="combine_rows",
    )(slots, ids, rows, table)


def spread_kernel(slots_ref, grads_ref, out_ref):
    positions = grads_ref.shape[0]
    places = lax.broadcasted_iota(jnp.int32, (out_ref.shape[0], positions), 1)
    chosen = (places == slots_ref[...]).astype(f32).astype(bf16)
    out_ref[...] = dot(chosen, grads_ref[...]).astype(bf16)


def spread(slots, grads):
    count = slots.shape[0]
    positions, width = grads.shape
    tile = 256
    return pl.pallas_call(
        spread_kernel,
        grid=(count // tile,),
        in_specs=[
            pl.BlockSpec((tile, 1), lambda i: (i, 0)),
            pl.BlockSpec((positions, width), lambda i: (0, 0)),
        ],
        out_specs=pl.BlockSpec((tile, width), lambda i: (i, 0)),
        out_shape=jax.ShapeDtypeStruct((count, width), bf16),
        compiler_params=params("arbitrary"),
        cost_estimate=pl.CostEstimate(
            flops=2 * positions * count * width, bytes_accessed=3 * count * width, transcendentals=0
        ),
        name="spread_grads",
    )(slots, grads)


def head_marks(heads, width):
    feature = lax.shift_right_logical(lax.broadcasted_iota(jnp.int32, (heads, width), 1), 6)
    return (feature == lax.broadcasted_iota(jnp.int32, (heads, width), 0)).astype(f32).astype(bf16)


def patch_marks(patch_row_ref, patch_col_ref):
    by_patch = (
        lax.broadcasted_iota(jnp.int32, (P_SIZE, L), 0) == patch_row_ref[...]
    ).astype(f32).astype(bf16)
    by_byte = (
        lax.broadcasted_iota(jnp.int32, (L, P_SIZE), 1) == patch_col_ref[...]
    ).astype(f32).astype(bf16)
    return by_patch, by_byte


def per_head(marks, products):
    high = products.astype(bf16)
    low = (products - high.astype(f32)).astype(bf16)
    return dot_nt(marks, high) + dot_nt(marks, low)


def neighbours(patches, heads):
    wide = jnp.broadcast_to(patches, (heads, L))
    back = [(d, pltpu.roll(wide, d, 1) == wide) for d in (1, 2, 4, 8)]
    ahead = [(L - d, pltpu.roll(wide, L - d, 1) == wide) for d in (1, 2, 4, 8)]
    return back, ahead


def scan_max(values, steps):
    for distance, same in steps:
        values = jnp.where(same, jnp.maximum(values, pltpu.roll(values, distance, 1)), values)
    return values


def scan_sum(values, steps):
    for distance, same in steps:
        values = jnp.where(same, values + pltpu.roll(values, distance, 1), values)
    return values


def patch_attention_kernel(
    patch_row_ref, patch_col_ref, query_ref, key_ref, value_ref, attention_ref, attended_ref
):
    heads, width = attention_ref.shape[0], query_ref.shape[1]
    marks = head_marks(heads, width)
    by_patch, by_byte = patch_marks(patch_row_ref, patch_col_ref)
    queries = dot(by_byte, query_ref[...])
    scores = per_head(marks, queries * key_ref[...].astype(f32)) * 0.125
    back, ahead = neighbours(patch_row_ref[...], heads)
    top = scan_max(scan_max(scores, back), ahead)
    shifted = jnp.exp(scores - top)
    total = scan_sum(shifted, back) + scan_sum(shifted, ahead) - shifted
    attention = shifted / total
    attention_ref[...] = attention
    weights = dot_tn(attention.astype(bf16), marks)
    weighted = (weights * value_ref[...].astype(f32)).astype(bf16)
    attended_ref[...] = dot(by_patch, weighted).astype(bf16)


def patch_attention(patch_row, patch_col, queries, key_value):
    groups = D // GROUP
    return pl.pallas_call(
        patch_attention_kernel,
        grid=(groups,),
        in_specs=[
            pl.BlockSpec((1, L), lambda i: (0, 0)),
            pl.BlockSpec((L, 1), lambda i: (0, 0)),
            pl.BlockSpec((P_SIZE, GROUP), lambda i: (0, i)),
            pl.BlockSpec((L, GROUP), lambda i: (0, i)),
            pl.BlockSpec((L, GROUP), lambda i: (0, i + groups)),
        ],
        out_specs=[
            pl.BlockSpec((HEADS // groups, L), lambda i: (i, 0)),
            pl.BlockSpec((P_SIZE, GROUP), lambda i: (0, i)),
        ],
        out_shape=[
            jax.ShapeDtypeStruct((HEADS, L), f32),
            jax.ShapeDtypeStruct((P_SIZE, D), bf16),
        ],
        compiler_params=params("arbitrary"),
        cost_estimate=pl.CostEstimate(flops=4 * 10**9, bytes_accessed=6 * 10**6, transcendentals=16384),
        name="patch_attention",
    )(patch_row, patch_col, queries, key_value, key_value)


def patch_attention_back_kernel(
    patch_row_ref,
    patch_col_ref,
    query_ref,
    key_ref,
    value_ref,
    attention_ref,
    grad_ref,
    grad_query_ref,
    grad_key_ref,
    grad_value_ref,
):
    heads, width = attention_ref.shape[0], query_ref.shape[1]
    marks = head_marks(heads, width)
    by_patch, by_byte = patch_marks(patch_row_ref, patch_col_ref)
    grads = dot(by_byte, grad_ref[...])
    attention = attention_ref[...]
    grad_attention = per_head(marks, grads * value_ref[...].astype(f32))
    weights = dot_tn(attention.astype(bf16), marks)
    grad_value_ref[...] = (weights * grads).astype(bf16)
    back, ahead = neighbours(patch_row_ref[...], heads)
    terms = attention * grad_attention
    total = scan_sum(terms, back) + scan_sum(terms, ahead) - terms
    grad_scores = (attention * (grad_attention - total)).astype(bf16)
    spread_scores = dot_tn(grad_scores, marks) * 0.125
    grad_key_ref[...] = (spread_scores * dot(by_byte, query_ref[...])).astype(bf16)
    weighted = (spread_scores * key_ref[...].astype(f32)).astype(bf16)
    grad_query_ref[...] = dot(by_patch, weighted).astype(bf16)


def patch_attention_back(patch_row, patch_col, queries, key_value, attention, grad_attended):
    groups = D // GROUP
    byte_block = pl.BlockSpec((L, GROUP), lambda i: (0, i))
    patch_block = pl.BlockSpec((P_SIZE, GROUP), lambda i: (0, i))
    return pl.pallas_call(
        patch_attention_back_kernel,
        grid=(groups,),
        in_specs=[
            pl.BlockSpec((1, L), lambda i: (0, 0)),
            pl.BlockSpec((L, 1), lambda i: (0, 0)),
            patch_block,
            byte_block,
            pl.BlockSpec((L, GROUP), lambda i: (0, i + groups)),
            pl.BlockSpec((HEADS // groups, L), lambda i: (i, 0)),
            patch_block,
        ],
        out_specs=[patch_block, byte_block, byte_block],
        out_shape=[
            jax.ShapeDtypeStruct((P_SIZE, D), bf16),
            jax.ShapeDtypeStruct((L, D), bf16),
            jax.ShapeDtypeStruct((L, D), bf16),
        ],
        compiler_params=params("arbitrary"),
        cost_estimate=pl.CostEstimate(flops=6 * 10**9, bytes_accessed=10 * 10**6, transcendentals=0),
        name="patch_attention_back",
    )(patch_row, patch_col, queries, key_value, key_value, attention, grad_attended)


def causal_softmax(queries, keys):
    scores = dot_nt(queries, keys) * 0.125
    size = scores.shape[0]
    allowed = lax.broadcasted_iota(jnp.int32, (size, size), 0) >= lax.broadcasted_iota(
        jnp.int32, (size, size), 1
    )
    scores = jnp.where(allowed, scores, -jnp.inf)
    shifted = jnp.exp(scores - jnp.max(scores, axis=-1, keepdims=True))
    return shifted / jnp.sum(shifted, axis=-1, keepdims=True)


def pair_masks(shape):
    lane = lax.broadcasted_iota(jnp.int32, shape, 1)
    return [lane < HEAD, lane >= HEAD]


def causal_kernel(query_ref, key_ref, value_ref, out_ref):
    queries, keys, values = query_ref[...], key_ref[...], value_ref[...]
    masks = pair_masks(queries.shape)
    parts = []
    for mask in masks:
        attention = causal_softmax(jnp.where(mask, queries, 0), keys).astype(bf16)
        parts.append(dot(attention, values))
    out_ref[...] = jnp.where(masks[0], parts[0], parts[1]).astype(bf16)


def causal_attention(mixed):
    pairs = HEADS // 2
    return pl.pallas_call(
        causal_kernel,
        grid=(pairs,),
        in_specs=[
            pl.BlockSpec((P_SIZE, 2 * HEAD), lambda i: (0, i)),
            pl.BlockSpec((P_SIZE, 2 * HEAD), lambda i: (0, i + pairs)),
            pl.BlockSpec((P_SIZE, 2 * HEAD), lambda i: (0, i + 2 * pairs)),
        ],
        out_specs=pl.BlockSpec((P_SIZE, 2 * HEAD), lambda i: (0, i)),
        out_shape=jax.ShapeDtypeStruct((P_SIZE, D), bf16),
        compiler_params=params("arbitrary"),
        cost_estimate=pl.CostEstimate(flops=2 * 10**9, bytes_accessed=2 * 10**6, transcendentals=10**6),
        name="causal_attention",
    )(mixed, mixed, mixed)


def causal_back_kernel(query_ref, key_ref, value_ref, grad_ref, gq_ref, gk_ref, gv_ref):
    queries, keys, values, grads = query_ref[...], key_ref[...], value_ref[...], grad_ref[...]
    masks = pair_masks(queries.shape)
    results = []
    for mask in masks:
        attention = causal_softmax(jnp.where(mask, queries, 0), keys)
        grad_attention = dot_nt(jnp.where(mask, grads, 0), values)
        total = jnp.sum(attention * grad_attention, axis=-1, keepdims=True)
        grad_scores = (attention * (grad_attention - total)).astype(bf16)
        results.append(
            (
                dot(grad_scores, keys) * 0.125,
                dot_tn(grad_scores, queries) * 0.125,
                dot_tn(attention.astype(bf16), grads),
            )
        )
    for ref, first, second in zip((gq_ref, gk_ref, gv_ref), results[0], results[1]):
        ref[...] = jnp.where(masks[0], first, second).astype(bf16)


def causal_attention_back(mixed, grad_attended):
    pairs = HEADS // 2
    block = pl.BlockSpec((P_SIZE, 2 * HEAD), lambda i: (0, i))
    return pl.pallas_call(
        causal_back_kernel,
        grid=(pairs,),
        in_specs=[
            block,
            pl.BlockSpec((P_SIZE, 2 * HEAD), lambda i: (0, i + pairs)),
            pl.BlockSpec((P_SIZE, 2 * HEAD), lambda i: (0, i + 2 * pairs)),
            block,
        ],
        out_specs=[block] * 3,
        out_shape=[jax.ShapeDtypeStruct((P_SIZE, D), bf16)] * 3,
        compiler_params=params("arbitrary"),
        cost_estimate=pl.CostEstimate(flops=4 * 10**9, bytes_accessed=4 * 10**6, transcendentals=10**6),
        name="causal_attention_back",
    )(mixed, mixed, mixed, grad_attended)


def normalize(inputs, gain):
    inverse = lax.rsqrt(jnp.mean(inputs * inputs, axis=-1, keepdims=True) + epsilon)
    return (inputs * inverse * gain).astype(bf16), inverse


def normalize_back(inputs, gain, inverse, grad_normed):
    scaled = inputs * inverse
    grad_gain = jnp.sum(grad_normed * scaled, axis=0)
    grad_scaled = grad_normed * gain
    grad_inputs = inverse * (
        grad_scaled - scaled * jnp.mean(grad_scaled * scaled, axis=-1, keepdims=True)
    )
    return grad_inputs, grad_gain


def feed_forward(hidden, gain, w_gate_up, w_down):
    normed, inverse = normalize(hidden, gain)
    joined = dot(normed, w_gate_up)
    inner = (jax.nn.silu(joined[:, :FF]) * joined[:, FF:]).astype(bf16)
    return hidden + dot(inner, w_down), (normed, inverse, joined, inner)


def feed_back(hidden, gain, w_gate_up, w_down, kept, grad_out):
    normed, inverse, joined, inner = kept
    gate, up = joined[:, :FF], joined[:, FF:]
    sigmoid = jax.nn.sigmoid(gate)
    grad_branch = grad_out.astype(bf16)
    grad_inner = dot_nt(grad_branch, w_down)
    grad_gate = grad_inner * up * sigmoid * (1.0 + gate * (1.0 - sigmoid))
    grad_up = grad_inner * gate * sigmoid
    grad_joined = jnp.concatenate([grad_gate, grad_up], axis=1).astype(bf16)
    grad_normed = dot_nt(grad_joined, w_gate_up)
    grad_in, grad_gain = normalize_back(hidden, gain, inverse, grad_normed)
    return grad_out + grad_in, grad_gain, grad_joined, grad_branch


def factors(count):
    sides = [1, 1, 1]
    prime = 2
    while count > 1:
        while count % prime == 0:
            sides[sides.index(min(sides))] *= prime
            count //= prime
        prime += 1
    return sides


def sum_along(block, sides, kept, which):
    stride = 1
    for side in sides[which + 1 :]:
        stride *= side
    size = sides[which]
    if size == 1:
        return block
    total = sides[0] * sides[1] * sides[2]
    place = (lax.axis_index("rows") // stride) % size
    axis = kept.index(which)

    def part(index):
        return lax.dynamic_index_in_dim(block, index, axis, keepdims=False)

    result = part(place).astype(f32)
    for step in range(1, size):
        route = []
        for device in range(total):
            own = (device // stride) % size
            route.append((device, device + ((own + step) % size - own) * stride))
        arrived = lax.ppermute(part((place + step) % size), "rows", route)
        result = result + arrived.astype(f32)
    return result.astype(bf16)


def scatter_sum(block, order):
    devices = lax.axis_size("rows")
    sides = factors(devices)
    kept = [0, 1, 2]
    block = block.reshape(*sides, block.shape[0] // devices, block.shape[1])
    for which in order:
        if sides[which] == 1:
            block = block.reshape([s for d, s in enumerate(block.shape) if d != kept.index(which)])
        else:
            block = sum_along(block, sides, kept, which)
        kept.remove(which)
    return block


def swap(array):
    return lax.ppermute(array, "section", [(0, 1), (1, 0)])


def on_device(
    byte_ids,
    hash_ids,
    patch_lengths,
    row_lengths,
    byte_table,
    hash_tables,
    norm_gains,
    w_qkv,
    w_out,
    w_gate_up,
    w_down,
    cotangent,
):
    section = lax.axis_index("section")
    first_core = section == 0
    devices = lax.axis_size("rows")
    count_tables, shard_rows, half_width = hash_tables.shape
    positions = M * L

    def both(array):
        return lax.all_gather(array, "section", axis=0, tiled=True)

    flat_ids = hash_ids.reshape(positions, count_tables).T
    owners = flat_ids // shard_rows
    local_rows = flat_ids % shard_rows + jnp.arange(count_tables, dtype=jnp.int32)[:, None] * shard_rows
    order_key = owners * positions + jnp.arange(positions, dtype=jnp.int32)[None, :]
    order_key, grouped = lax.sort((order_key, local_rows), dimension=1, num_keys=1)

    def by_owner(array):
        return array.reshape(count_tables, devices, -1).transpose(1, 0, 2).reshape(devices, -1)

    slots = by_owner(order_key % positions).reshape(-1)
    requested = lax.all_to_all(by_owner(grouped), "rows", split_axis=0, concat_axis=0, tiled=True)
    flat_tables = hash_tables.reshape(count_tables * shard_rows, half_width)
    found_rows = jnp.take(flat_tables, requested, axis=0)
    returned = lax.all_to_all(found_rows, "rows", split_axis=0, concat_axis=0, tiled=True)

    gains = both(norm_gains).astype(f32)
    qkv_both, out_both = both(w_qkv), both(w_out)
    gate_up_both, down_both = both(w_gate_up), both(w_down)

    lengths = lax.dynamic_index_in_dim(patch_lengths, section, 0, keepdims=False)
    row_length = lax.dynamic_index_in_dim(row_lengths, section, 0, keepdims=False)
    starts = jnp.cumsum(lengths) - lengths
    byte_positions = jnp.arange(L, dtype=jnp.int32)
    byte_patch = jnp.sum((starts[:, None] <= byte_positions[None, :]).astype(jnp.int32), axis=0) - 1
    patch_row, patch_col = byte_patch[None, :], byte_patch[:, None]
    patches = jnp.arange(P_SIZE, dtype=jnp.int32)
    member = (patches[:, None] == patch_row).astype(bf16)
    member_byte = (patches[None, :] == patch_col).astype(bf16)
    counts = lengths.astype(f32)[:, None]
    valid = (patches < row_length)[:, None]

    own_cotangent = lax.dynamic_index_in_dim(cotangent[0], section, 0, keepdims=False)
    sent_cotangent = swap(lax.dynamic_index_in_dim(cotangent[0], 1 - section, 0, keepdims=False))
    cotangent_one = jnp.where(first_core, own_cotangent, sent_cotangent).astype(f32)
    cotangent_two = jnp.where(first_core, sent_cotangent, own_cotangent).astype(f32)

    flat_bytes = byte_ids.reshape(positions)
    table_rows = byte_table.shape[0]
    padded = jnp.pad(byte_table, ((0, -table_rows % 128), (0, 0)))
    own_half = combine(
        slots[None, :], flat_bytes[:, None], returned.reshape(-1, half_width), padded
    ).reshape(M, L, half_width)
    kept_half = lax.dynamic_index_in_dim(own_half, section, 0, keepdims=False)
    sent_half = swap(lax.dynamic_index_in_dim(own_half, 1 - section, 0, keepdims=False))
    byte_rows = jnp.concatenate(
        [jnp.where(first_core, kept_half, sent_half), jnp.where(first_core, sent_half, kept_half)], axis=1
    )

    pooled = dot(member, byte_rows) / counts
    normed_one, inverse_one = normalize(pooled, gains[0, 0])
    queries_one = dot(normed_one, qkv_both[0, :, :D]).astype(bf16)
    byte_pairs = dot(byte_rows, qkv_both[0, :, D:]).astype(bf16)
    attention_one, attended_one = patch_attention(patch_row, patch_col, queries_one, byte_pairs)
    middle_one = pooled + dot(attended_one, out_both[0])
    result_one, kept_one = feed_forward(middle_one, gains[0, 1], gate_up_both[0], down_both[0])
    encoded = jnp.where(valid, result_one, pooled).astype(bf16)

    inputs_two = encoded.astype(f32)
    normed_two, inverse_two = normalize(inputs_two, gains[1, 0])
    mixed = dot(normed_two, qkv_both[1]).astype(bf16)
    attended_two = causal_attention(mixed)
    middle_two = inputs_two + dot(attended_two, out_both[1])
    result_two, kept_two = feed_forward(middle_two, gains[1, 1], gate_up_both[1], down_both[1])
    final = jnp.where(valid, result_two, inputs_two).astype(bf16)
    sent_out = swap(jnp.where(first_core, final, encoded))
    kept_out = jnp.where(first_core, encoded, final)
    section_out = jnp.where(
        first_core, jnp.stack([kept_out, sent_out]), jnp.stack([sent_out, kept_out])
    )[None]

    def share(left, right):
        width = right.shape[1] // 2
        mine = lax.dynamic_slice_in_dim(right, section * width, width, axis=1)
        theirs = lax.dynamic_slice_in_dim(right, (1 - section) * width, width, axis=1)
        lefts = jnp.concatenate([left, swap(left)], axis=0)
        rights = jnp.concatenate([mine, swap(theirs)], axis=0)
        return dot_tn(lefts, rights).astype(bf16)

    grad_kept = jnp.where(valid, cotangent_two, 0.0)
    grad_middle, gain_two_second, grad_joined, grad_branch = feed_back(
        middle_two, gains[1, 1], gate_up_both[1], down_both[1], kept_two, grad_kept
    )
    gate_up_two = scatter_sum(share(kept_two[0], grad_joined), (2, 1, 0))
    down_two = scatter_sum(share(grad_branch, kept_two[3]), (1, 2, 0))
    grad_low = grad_middle.astype(bf16)
    grad_attended = dot_nt(grad_low, out_both[1]).astype(bf16)
    grad_mixed = jnp.concatenate(causal_attention_back(mixed, grad_attended), axis=1)
    rest_two = scatter_sum(
        jnp.concatenate([share(normed_two, grad_mixed), share(attended_two, grad_low)], axis=1), (1, 2, 0)
    )
    grad_normed = dot_nt(grad_mixed, qkv_both[1])
    grad_in, gain_two_first = normalize_back(inputs_two, gains[1, 0], inverse_two, grad_normed)
    grad_encoded = jnp.where(valid, 0.0, cotangent_two) + grad_middle + grad_in

    grad_out = cotangent_one + grad_encoded.astype(bf16).astype(f32)
    grad_kept = jnp.where(valid, grad_out, 0.0)
    grad_middle, gain_one_second, grad_joined, grad_branch = feed_back(
        middle_one, gains[0, 1], gate_up_both[0], down_both[0], kept_one, grad_kept
    )
    gate_up_one = scatter_sum(share(kept_one[0], grad_joined), (2, 1, 0))
    down_one = scatter_sum(share(grad_branch, kept_one[3]), (1, 2, 0))
    grad_low = grad_middle.astype(bf16)
    grad_attended = dot_nt(grad_low, out_both[0]).astype(bf16)
    grad_queries, grad_keys, grad_values = patch_attention_back(
        patch_row, patch_col, queries_one, byte_pairs, attention_one, grad_attended
    )
    grad_pairs = jnp.concatenate([grad_keys, grad_values], axis=1)
    grad_normed = dot_nt(grad_queries, qkv_both[0, :, :D])
    grad_in, gain_one_first = normalize_back(pooled, gains[0, 0], inverse_one, grad_normed)
    grad_pooled = jnp.where(valid, 0.0, grad_out) + grad_middle + grad_in
    grad_bytes = dot(member_byte, (grad_pooled / counts).astype(bf16))
    grad_bytes = (grad_bytes + dot_nt(grad_pairs, qkv_both[0, :, D:])).astype(bf16)

    grad_halves = grad_bytes.reshape(L, 2, half_width)
    kept_grad = lax.dynamic_index_in_dim(grad_halves, section, 1, keepdims=False)
    sent_grad = swap(lax.dynamic_index_in_dim(grad_halves, 1 - section, 1, keepdims=False))
    own_grad = jnp.where(
        first_core,
        jnp.concatenate([kept_grad, sent_grad], axis=0),
        jnp.concatenate([sent_grad, kept_grad], axis=0),
    )
    slot_grads = spread(slots[:, None], own_grad).reshape(devices, -1, half_width)
    arrived = lax.all_to_all(slot_grads, "rows", split_axis=0, concat_axis=0, tiled=True)
    hash_grad = jax.ops.segment_sum(
        arrived.reshape(-1, half_width).astype(f32),
        requested.reshape(-1),
        num_segments=count_tables * shard_rows,
    ).reshape(count_tables, shard_rows, half_width)
    words = (flat_bytes[:, None] == jnp.arange(table_rows, dtype=jnp.int32)[None, :]).astype(bf16)
    byte_table_grad = lax.psum(dot_tn(words, own_grad), "rows")

    rest_one = scatter_sum(
        jnp.concatenate(
            [share(normed_one, grad_queries), share(byte_rows, grad_pairs), share(attended_one, grad_low)],
            axis=1,
        ),
        (1, 2, 0),
    )

    sums_one = jnp.concatenate([gate_up_one, down_one, rest_one], axis=1)
    sums_two = jnp.concatenate([gate_up_two, down_two, rest_two], axis=1)
    kept_sums = jnp.where(first_core, sums_one, sums_two)
    sent_sums = swap(jnp.where(first_core, sums_two, sums_one))
    lower = jnp.where(first_core, kept_sums, sent_sums).astype(f32)
    upper = jnp.where(first_core, sent_sums, kept_sums).astype(f32)
    half_ff = FF // 2
    gate_up_grad = jnp.concatenate([lower[:, :FF], upper[:, :FF]], axis=1)
    down_grad = jnp.concatenate([lower[:, FF : FF + half_ff], upper[:, FF : FF + half_ff]], axis=1).T
    low_rest, high_rest = lower[:, FF + half_ff :], upper[:, FF + half_ff :]
    half = D // 2
    out_grad = jnp.concatenate([low_rest[:, -half:], high_rest[:, -half:]], axis=1)
    pieces_one = [low_rest[:, :half], high_rest[:, :half], low_rest[:, half : 3 * half], high_rest[:, half : 3 * half]]
    pieces_two = [low_rest[:, : 3 * half], high_rest[:, : 3 * half]]
    qkv_grad = jnp.where(
        first_core, jnp.concatenate(pieces_one, axis=1), jnp.concatenate(pieces_two, axis=1)
    )

    gain_sums = jnp.stack([gain_one_first, gain_one_second, gain_two_first, gain_two_second])
    gain_sums = lax.psum_scatter(gain_sums, "rows", scatter_dimension=1, tiled=True)
    gain_sums = (gain_sums + swap(gain_sums)).reshape(2, 2, -1)
    gains_grad = lax.dynamic_index_in_dim(gain_sums, section, 0, keepdims=True)

    return (
        section_out,
        byte_table_grad,
        hash_grad,
        gains_grad,
        qkv_grad[None],
        out_grad[None],
        gate_up_grad[None],
        down_grad[None],
    )


def solution(mesh):
    return jax.shard_map(
        on_device,
        mesh=mesh,
        in_specs=(
            P("rows", None),
            P("rows", None, None),
            P("rows", None),
            P("rows"),
            P(None, "section"),
            P(None, "rows", "section"),
            P("section", None, None),
            P("section", None, None),
            P("section", None, None),
            P("section", None, None),
            P("section", None, None),
            P("section", "rows", None, None),
        ),
        out_specs=(
            P("section", "rows", None, None),
            P(None, "section"),
            P(None, "rows", "section"),
            P("section", None, "rows"),
            P("section", "rows", None),
            P("section", "rows", None),
            P("section", "rows", None),
            P("section", None, "rows"),
        ),
        check_vma=False,
    )
```

time: 2830 us -> 1140 us (0.40)
  waiting for transfers between devices: 1270 us -> 559 us
  local copies, waits for them, and re-layouts: 758 us -> 119 us
  other arithmetic: 431 us -> 114 us
  matrix products: 248 us -> 135 us
  Pallas kernels: 0 us -> 72.9 us
  starting transfers between devices: 43.7 us -> 93.2 us
    reduce_scatter x4 -> x0, waiting for transfers between devices: 996 us -> none  [the longest x1 476 us: on_device(): lax.psum_scatter(totals[3], 'rows', scatter_dimension=0, tiled=True)]
    gather x19 -> x0, local copies, waits for them, and re-layouts: 481 us -> none  [the longest x8 232 us: encoder_parts(): jnp.take(key_value, slot_index, axis=0)]
    ppermute x6 -> x54, waiting for transfers between devices: 62.1 us -> 324 us  [the longest x30 323 us: sum_along(): arrived = lax.ppermute(part((place + step) % size), 'rows', route)]
    another operation x22 -> x3, other arithmetic: 104 us -> 0.37 us  [the longest x4 90.4 us: encoder_backward(): jnp.stack([grad_keys, grad_values], axis=2).reshape(P_SIZE * MOST, 2 * D)]
    all_to_all x2, waiting for transfers between devices: 214 us -> 113 us  [the longest x1 113 us: on_device(): lax.all_to_all(found_rows, 'rows', split_axis=0, concat_axis=0, tiled=True)]
    dot_general x42 -> x30, matrix products: 230 us -> 135 us  [the longest x11 49.9 us: dot(): return jnp.dot(left, right, preferred_element_type=f32)]
    reshape x3 -> x0, local copies, waits for them, and re-layouts: 92.2 us -> none  [the longest x2 92.2 us: encoder_backward(): jnp.stack([grad_keys, grad_values], axis=2).reshape(P_SIZE * MOST, 2 * D)]
    unnamed x7, waiting for transfers between devices: 0.1 us -> 80.9 us
  transfers between devices with their start and end apart: 14 -> 62, of which waited for: 11 -> 19; matrix products, arithmetic and copies ran while one was open for 7% -> 30% of each run, Pallas kernels for 0% -> 6%
where the time goes in v1:
time: 1140 us; the launch traced here: 1130 us
  waiting for transfers between devices  559 us (49%)
  matrix products  135 us (12%)
  local copies, waits for them, and re-layouts  119 us (10%)
  other arithmetic  114 us (10%)
  starting transfers between devices  93.2 us (8%)
  Pallas kernels  72.9 us (6%)
  between operations  17.6 us (2%)
  blocking collectives  17.4 us (2%)
    ppermute x30, waiting for transfers between devices, sum_along(): arrived = lax.ppermute(part((place + step) % size), 'rows', route)  323 us
    all_to_all x1, waiting for transfers between devices, on_device(): lax.all_to_all(found_rows, 'rows', split_axis=0, concat_axis=0, tiled=True)  113 us
    unnamed x7, waiting for transfers between devices  80.9 us
    scatter-add x1, other arithmetic, on_device(): jax.ops.segment_sum(arrived.reshape(-1, half_width).astype(f32), requeste...  58.2 us
    ppermute x30, starting transfers between devices, sum_along(): arrived = lax.ppermute(part((place + step) % size), 'rows', route)  52.8 us
    dot_general x11, matrix products, dot(): return jnp.dot(left, right, preferred_element_type=f32)  49.9 us
    dot_general x9, matrix products, dot_nt(): lax.dot_general(left, right, (((1,), (1,)), ((), ())), preferred_element_...  44.8 us
    psum x1, waiting for transfers between devices, on_device(): byte_table_grad = lax.psum(dot_tn(words, own_grad), 'rows')  41.8 us
  transfers between devices with their start and end apart: 62, of which 19 were waited for; matrix products, arithmetic and copies ran while one was open for 30% of the time, Pallas kernels for 6%

profile of v1, /device:TPU:0, one launch (start us, length us, event | category | flops | bytes accessed | tf_op | source)
XLA Modules:
  0.0 1128.2 jit_solution(15254611581888303741)
XLA Ops:
  11.3 9.6 sort.17.cloned.1.call-done
  21.7 15.5 %all_to_all.26 = s32[16,1,384]{2,1,0:T(1,128)S(1)} all-to-all(s32[16,1,384]{2,1,0:T(1,128)S(1)} %all_to_all.22), channel_id=1, replica_groups=mesh['section'=2,'rows'=16] {'rows'}, dimensions={0} | all-to-all | bytes 49152 | tf_op jit(solution)/shard_map/all_to_all | solution.py:454
  37.2 37.1 %gather_fusion = bf16[6144,512]{1,0:T(8,128)(2,1)} fusion(bf16[24576,512]{1,0:T(8,128)(2,1)} %bitcast.350, s32[6144]{0:T(1024)S(1)} %broadcast_clamp_fusion), kind=kCustom, calls=%fused_computation | custom fusion | bytes 12607488 | tf_op jit(solution)/shard_map/jit(_take)/gather | solution.py:456
  74.3 7.8 broadcast_select_fusion
  82.1 4.6 all-to-all-start.1
  89.9 112.7 %all-to-all-done.1 = bf16[16,384,512]{2,1,0:T(8,128)(2,1)} async-done(((bf16[16,384,512]{2,1,0:T(8,128)(2,1)}), bf16[16,384,512]{2,1,0:T(8,128)(2,1)}, u32[]{:S(2)}, u32[]{:S(2)}) %all-to-all-start.1) | async-done | bytes 6291488 | tf_op jit(solution)/shard_map/all_to_all | solution.py:457
  202.5 18.5 %combine_rows.1 = bf16[2048,512]{1,0:T(8,128)(2,1)S(1)} custom-call(s32[1,6144]{1,0:T(1,128)S(1)} %broadcast_in_dim_reshape_reshape.6.slots_ref, s32[2048,1]{1,0:T(8,128)S(1)} %bitcast.346, bf16[6144,512]{1,0:T(8,128)(2,1)} %bitcast.13.rows_ref, bf16[384,512]{1,0:T(8,128)(2,1)S(1)} %pad.4.table_ref), custom_call_target="tpu_custom_call" | custom-call | flops 12884901888 | bytes 9437184 | tf_op jit(solution)/shard_map/combine_rows/pallas_call | solution.py:57
  241.2 7.4 convolution_convert_fusion.5.key_ref.value_ref
  248.6 6.8 patch_attention.1
  262.2 6.2 fusion.4
  272.8 5.4 fusion.91
  278.5 4.8 fusion.26.query_ref.key_ref.value_ref
  283.3 8.9 causal_attention.1
  295.2 10.3 fusion.6
  305.5 5.9 multiply_convert_fusion.3
  311.4 7.9 multiply_reduce_fusion
  322.0 11.4 %causal_attention_back.1 = (bf16[256,1024]{1,0:T(8,128)(2,1)S(1)}, bf16[256,1024]{1,0:T(8,128)(2,1)S(1)}, bf16[256,1024]{1,0:T(8,128)(2,1)S(1)}) custom-call(bf16[256,3072]{1,0:T(8,128)(2,1)S(1)} %fusion.26.query_ref.key_ref.value_ref, bf16[256,3072]{1,0:T(8,128)(2,1)S(1)} %fusion.26.query_ref.key_ref.value_ref, ...), custom_call_target="tpu_custom_call" | custom-call | flops 4000000000 | bytes 4000000 | tf_op jit(solution)/shard_map/causal_attention_back/pallas_call | solution.py:314
  333.6 6.0 fusion.90
  340.7 5.5 multiply_convert_fusion.1
  346.3 7.2 multiply_reduce_fusion.1
  356.9 8.4 patch_attention_back.1
  378.6 6.4 fusion.27
  386.7 5.5 select_bitcast_fusion
  434.4 18.8 %spread_grads.1 = bf16[6144,512]{1,0:T(8,128)(2,1)} custom-call(s32[6144,1]{1,0:T(8,128)S(1)} %broadcast_in_dim_reshape_reshape.8.slots_ref, bf16[2048,512]{1,0:T(8,128)(2,1)S(1)} %maximum_select_fusion.grads_ref), custom_call_target="tpu_custom_call" | custom-call | flops 12884901888 | bytes 9437184 | tf_op jit(solution)/shard_map/spread_grads/pallas_call | solution.py:87
  453.3 28.8 %all-to-all-start.2 = ((bf16[16,384,512]{2,1,0:T(8,128)(2,1)}), bf16[16,384,512]{2,1,0:T(8,128)(2,1)}, u32[]{:S(2)}, u32[]{:S(2)}) async-start(bf16[16,384,512]{2,1,0:T(8,128)(2,1)} %bitcast.357), calls=%async_computation.2 | async-start | bytes 12582912 | tf_op jit(solution)/shard_map/all_to_all | solution.py:566
  484.2 7.4 convolution_convert_fusion
  493.7 7.5 convolution_convert_fusion.1
  501.2 6.9 fusion.41
  510.7 6.5 copy.83
  520.6 52.7 %collective-permute-done.39 = bf16[4,2,64,1408]{3,2,0,1:T(8,128)(2,1)} collective-permute-done((bf16[4,2,64,1408]{3,2,0,1:T(8,128)(2,1)}, bf16[4,2,64,1408]{3,2,0,1:T(8,128)(2,1)}, u32[]{:S(2)}, u32[]{:S(2)}) %collective-permute-start.39) | collective-permute-done | bytes 1441824 | tf_op jit(solution)/shard_map/ppermute | solution.py:398
  577.2 37.8 %collective-permute-done.14 = bf16[4,2,64,1408]{3,2,0,1:T(8,128)(2,1)} collective-permute-done((bf16[4,2,64,1408]{3,2,0,1:T(8,128)(2,1)S(1)}, bf16[4,2,64,1408]{3,2,0,1:T(8,128)(2,1)}, u32[]{:S(2)}, u32[]{:S(2)}) %collective-permute-start.14) | collective-permute-done | bytes 1441824 | tf_op jit(solution)/shard_map/ppermute | solution.py:398
  618.4 41.4 %collective-permute-done.48 = bf16[4,2,64,2048]{3,2,0,1:T(8,128)(2,1)S(1)} collective-permute-done((bf16[4,2,64,2048]{3,2,0,1:T(8,128)(2,1)}, bf16[4,2,64,2048]{3,2,0,1:T(8,128)(2,1)S(1)}, u32[]{:S(2)}, u32[]{:S(2)}) %collective-permute-start.48) | collective-permute-done | bytes 2097184 | tf_op jit(solution)/shard_map/ppermute | solution.py:398
  679.8 7.9 constant_dynamic-slice_fusion.11
  696.6 6.3 collective-permute-done.17
  710.8 4.7 collective-permute-done.52
  715.5 9.8 collective-permute-done.51
  726.7 29.4 %collective-permute-done.32 = bf16[4,2,64,2816]{3,2,0,1:T(8,128)(2,1)S(1)} collective-permute-done((bf16[4,2,64,2816]{3,2,0,1:T(8,128)(2,1)S(1)}, bf16[4,2,64,2816]{3,2,0,1:T(8,128)(2,1)S(1)}, u32[]{:S(2)}, u32[]{:S(2)}) %collective-permute-start.32) | collective-permute-done | bytes 2883616 | tf_op jit(solution)/shard_map/ppermute | solution.py:398
  757.6 60.3 %collective-permute-done.7 = bf16[4,2,64,2816]{3,2,0,1:T(8,128)(2,1)S(1)} collective-permute-done((bf16[4,2,64,2816]{3,2,0,1:T(8,128)(2,1)S(1)}, bf16[4,2,64,2816]{3,2,0,1:T(8,128)(2,1)S(1)}, u32[]{:S(2)}, u32[]{:S(2)}) %collective-permute-start.7) | collective-permute-done | bytes 2883616 | tf_op jit(solution)/shard_map/ppermute | solution.py:398
  818.7 15.5 %collective-permute-done.26 = bf16[4,64,2048]{2,1,0:T(8,128)(2,1)S(1)} collective-permute-done((bf16[4,64,2048]{2,1,0:T(8,128)(2,1)S(1)}, bf16[4,64,2048]{2,1,0:T(8,128)(2,1)S(1)}, u32[]{:S(2)}, u32[]{:S(2)}) %collective-permute-start.26) | collective-permute-done | bytes 1048608 | tf_op jit(solution)/shard_map/ppermute | solution.py:398
  839.3 6.1 collective-permute-done.29
  846.1 9.5 collective-permute-done.28
  856.3 14.6 %collective-permute-start.35 = (bf16[64,2816]{1,0:T(8,128)(2,1)S(1)}, bf16[64,2816]{1,0:T(8,128)(2,1)S(1)}, u32[]{:S(2)}, u32[]{:S(2)}) collective-permute-start(bf16[64,2816]{1,0:T(8,128)(2,1)S(1)} %get-tuple-element.81), channel_id=1, source_target_pairs={{0,8},{1,9},{2,10},{3,11},{4,12},{5,13},{6,14},{7,15},{8,0},{9,1},... | collective-permute-start | bytes 1081352 | tf_op jit(solution)/shard_map/ppermute | solution.py:398
  875.2 5.9 collective-permute-done.36
  883.3 26.6 %collective-permute-done.35 = bf16[64,2816]{1,0:T(8,128)(2,1)S(1)} collective-permute-done((bf16[64,2816]{1,0:T(8,128)(2,1)S(1)}, bf16[64,2816]{1,0:T(8,128)(2,1)S(1)}, u32[]{:S(2)}, u32[]{:S(2)}) %collective-permute-start.35) | collective-permute-done | bytes 360480 | tf_op jit(solution)/shard_map/ppermute | solution.py:398
  910.2 13.9 %collective-permute-done.10 = bf16[64,2816]{1,0:T(8,128)(2,1)S(1)} collective-permute-done((bf16[64,2816]{1,0:T(8,128)(2,1)S(1)}, bf16[64,2816]{1,0:T(8,128)(2,1)S(1)}, u32[]{:S(2)}, u32[]{:S(2)}) %collective-permute-start.10) | collective-permute-done | bytes 360480 | tf_op jit(solution)/shard_map/ppermute | solution.py:398
  926.8 78.6 %reduce-scatter.4.cloned.1.call-done = f32[64,4]{1,0:T(8,128)} async-done(((f32[1024,4]{1,0:T(8,128)}), f32[64,4]{1,0:T(8,128)}) %reduce-scatter.4.cloned.1.call-update) | async-done | bytes 1040
  1018.5 58.2 %scatter_custom_fusion = f32[24576,512]{1,0:T(8,128)} fusion(s32[6144]{0:T(1024)} %bitcast.370, f32[]{:T(128)} %constant.424.clone.1, bf16[6144,512]{1,0:T(8,128)(2,1)} %bitcast.116), kind=kCustom, calls=%fused_computation.2 | custom fusion | flops 6291456 | bytes 56623616 | tf_op jit(solution)/shard_map/scatter-add | solution.py:567
  1076.7 41.8 %all-reduce.3.cloned.1.call-done = f32[260,512]{1,0:T(8,128)} async-done(((f32[260,512]{1,0:T(8,128)}), f32[260,512]{1,0:T(8,128)}) %all-reduce.3.cloned.1.call-update) | async-done | bytes 532496 | tf_op jit(solution)/shard_map/psum | solution.py:573
  (451 shorter events, 193.8 us)
Async XLA Ops:
  9.5 229.0 %all-gather.5.cloned.1.call-start = ((), (), s32[]{:S(2)}) async-start(), calls=%async_computation.4 | async-start | bytes 18874368 | tf_op jit(solution)/shard_map/all_gather | solution.py:442
  10.1 247.3 %all-gather.7.cloned.1.call-start = ((), (), s32[]{:S(2)}) async-start(), calls=%async_computation.5 | async-start | bytes 6291456 | tf_op jit(solution)/shard_map/all_gather | solution.py:442
  10.7 251.5 %all-gather.9.cloned.1.call-start = ((), (), s32[]{:S(2)}) async-start(), calls=%async_computation.6 | async-start | bytes 34603008 | tf_op jit(solution)/shard_map/all_gather | solution.py:442
  82.1 120.4 %all-to-all-start.1 = ((bf16[16,384,512]{2,1,0:T(8,128)(2,1)}), bf16[16,384,512]{2,1,0:T(8,128)(2,1)}, u32[]{:S(2)}, u32[]{:S(2)}) async-start(bf16[16,384,512]{2,1,0:T(8,128)(2,1)} %broadcast_select_fusion), calls=%async_computation.1 | async-start | bytes 12582912 | tf_op jit(solution)/shard_map/all_to_all | solution.py:457
  86.8 186.0 %all-gather.11.cloned.1.call-start = ((), (), s32[]{:S(2)}) async-start(), calls=%async_computation.7 | async-start | bytes 17301504 | tf_op jit(solution)/shard_map/all_gather | solution.py:442
  88.8 142.2 %collective-permute-start.2 = (bf16[256,1024]{1,0:T(8,128)(2,1)}, bf16[256,1024]{1,0:T(8,128)(2,1)}, u32[]{:S(2)}, u32[]{:S(2)}) collective-permute-start(bf16[256,1024]{1,0:T(8,128)(2,1)} %dynamic-slice_bitcast_fusion.8), channel_id=1, source_target_pairs={{0,16},{16,0},{1,17},{17,1},{2,18},{18,2},{3,19},{19,3},{4,20},{20... | collective-permute-start | bytes 1572872 | tf_op jit(solution)/shard_map/ppermute | solution.py:418
  238.4 157.4 %collective-permute-start.19 = (bf16[256,1024]{1,0:T(8,128)(2,1)}, bf16[256,1024]{1,0:T(8,128)(2,1)}, u32[]{:S(2)}, u32[]{:S(2)}) collective-permute-start(bf16[256,1024]{1,0:T(8,128)(2,1)} %multiply_convert_fusion.8), channel_id=1, source_target_pairs={{0,16},{16,0},{1,17},{17,1},{2,18},{18,2},{3,19},{19,3},{4,20},{20... | collective-permute-start | bytes 1572872 | tf_op jit(solution)/shard_map/ppermute | solution.py:418
  255.4 140.2 %collective-permute-start.23 = (bf16[256,1024]{1,0:T(8,128)(2,1)}, bf16[256,1024]{1,0:T(8,128)(2,1)}, u32[]{:S(2)}, u32[]{:S(2)}) collective-permute-start(bf16[256,1024]{1,0:T(8,128)(2,1)} %get-tuple-element.20), channel_id=1, source_target_pairs={{0,16},{16,0},{1,17},{17,1},{2,18},{18,2},{3,19},{19,3},{4,20},{20... | collective-permute-start | bytes 1572872 | tf_op jit(solution)/shard_map/ppermute | solution.py:418
  292.2 119.9 %collective-permute-start.46 = (bf16[256,1024]{1,0:T(8,128)(2,1)}, bf16[256,1024]{1,0:T(8,128)(2,1)}, u32[]{:S(2)}, u32[]{:S(2)}) collective-permute-start(bf16[256,1024]{1,0:T(8,128)(2,1)} %causal_attention.1), channel_id=1, source_target_pairs={{0,16},{16,0},{1,17},{17,1},{2,18},{18,2},{3,19},{19,3},{4,20},{20... | collective-permute-start | bytes 1572872 | tf_op jit(solution)/shard_map/ppermute | solution.py:418
  369.2 29.5 %collective-permute-start.47 = (bf16[256,512]{1,0:T(8,128)(2,1)S(1)}, bf16[256,512]{1,0:T(8,128)(2,1)S(1)}, u32[]{:S(2)}, u32[]{:S(2)}) collective-permute-start(bf16[256,512]{1,0:T(8,128)(2,1)S(1)} %copy-done.72), channel_id=1, source_target_pairs={{0,16},{16,0},{1,17},{17,1},{2,18},{18,2},{3,19},{19,3},{4,20},{20... | collective-permute-start | bytes 786440 | tf_op jit(solution)/shard_map/ppermute | solution.py:418
  373.1 25.7 %collective-permute-start.24 = (bf16[256,512]{1,0:T(8,128)(2,1)S(1)}, bf16[256,512]{1,0:T(8,128)(2,1)S(1)}, u32[]{:S(2)}, u32[]{:S(2)}) collective-permute-start(bf16[256,512]{1,0:T(8,128)(2,1)S(1)} %copy-done.71), channel_id=1, source_target_pairs={{0,16},{16,0},{1,17},{17,1},{2,18},{18,2},{3,19},{19,3},{4,20},{20... | collective-permute-start | bytes 786440 | tf_op jit(solution)/shard_map/ppermute | solution.py:418
  395.6 19.2 %collective-permute-start.38 = (bf16[256,1408]{1,0:T(8,128)(2,1)}, bf16[256,1408]{1,0:T(8,128)(2,1)}, u32[]{:S(2)}, u32[]{:S(2)}) collective-permute-start(bf16[256,1408]{1,0:T(8,128)(2,1)} %get-tuple-element.83), channel_id=1, source_target_pairs={{0,16},{16,0},{1,17},{17,1},{2,18},{18,2},{3,19},{19,3},{4,20},{20... | collective-permute-start | bytes 2162696 | tf_op jit(solution)/shard_map/ppermute | solution.py:418
  398.6 15.8 %collective-permute-start.37 = (bf16[256,1024]{1,0:T(8,128)(2,1)}, bf16[256,1024]{1,0:T(8,128)(2,1)}, u32[]{:S(2)}, u32[]{:S(2)}) collective-permute-start(bf16[256,1024]{1,0:T(8,128)(2,1)} %get-tuple-element.39), channel_id=1, source_target_pairs={{0,16},{16,0},{1,17},{17,1},{2,18},{18,2},{3,19},{19,3},{4,20},{20... | collective-permute-start | bytes 1572872 | tf_op jit(solution)/shard_map/ppermute | solution.py:418
  398.9 20.0 %collective-permute-start.13 = (bf16[256,1408]{1,0:T(8,128)(2,1)}, bf16[256,1408]{1,0:T(8,128)(2,1)}, u32[]{:S(2)}, u32[]{:S(2)}) collective-permute-start(bf16[256,1408]{1,0:T(8,128)(2,1)} %get-tuple-element.78), channel_id=1, source_target_pairs={{0,16},{16,0},{1,17},{17,1},{2,18},{18,2},{3,19},{19,3},{4,20},{20... | collective-permute-start | bytes 2162696 | tf_op jit(solution)/shard_map/ppermute | solution.py:418
  412.0 79.6 %collective-permute-start.5 = (bf16[256,1024]{1,0:T(8,128)(2,1)}, bf16[256,1024]{1,0:T(8,128)(2,1)}, u32[]{:S(2)}, u32[]{:S(2)}) collective-permute-start(bf16[256,1024]{1,0:T(8,128)(2,1)} %multiply_convert_fusion.7), channel_id=1, source_target_pairs={{0,16},{16,0},{1,17},{17,1},{2,18},{18,2},{3,19},{19,3},{4,20},{20... | collective-permute-start | bytes 1572872 | tf_op jit(solution)/shard_map/ppermute | solution.py:418
  414.5 86.7 %collective-permute-start.21 = (bf16[1024,1024]{1,0:T(8,128)(2,1)}, bf16[1024,1024]{1,0:T(8,128)(2,1)}, u32[]{:S(2)}, u32[]{:S(2)}) collective-permute-start(bf16[1024,1024]{1,0:T(8,128)(2,1)} %pad_maximum_fusion.6), channel_id=1, source_target_pairs={{0,16},{16,0},{1,17},{17,1},{2,18},{18,2},{3,19},{19,3},{4,20},{20... | collective-permute-start | bytes 6291464 | tf_op jit(solution)/shard_map/ppermute | solution.py:418
  427.1 55.2 %collective-permute-start.31 = (bf16[256,2816]{1,0:T(8,128)(2,1)}, bf16[256,2816]{1,0:T(8,128)(2,1)}, u32[]{:S(2)}, u32[]{:S(2)}) collective-permute-start(bf16[256,2816]{1,0:T(8,128)(2,1)} %get-tuple-element.61), channel_id=1, source_target_pairs={{0,16},{16,0},{1,17},{17,1},{2,18},{18,2},{3,19},{19,3},{4,20},{20... | collective-permute-start | bytes 4325384 | tf_op jit(solution)/shard_map/ppermute | solution.py:418
  433.1 68.1 %collective-permute-start.22 = (bf16[1024,1024]{1,0:T(8,128)(2,1)}, bf16[1024,1024]{1,0:T(8,128)(2,1)}, u32[]{:S(2)}, u32[]{:S(2)}) collective-permute-start(bf16[1024,1024]{1,0:T(8,128)(2,1)} %get-tuple-element.51), channel_id=1, source_target_pairs={{0,16},{16,0},{1,17},{17,1},{2,18},{18,2},{3,19},{19,3},{4,20},{20... | collective-permute-start | bytes 6291464 | tf_op jit(solution)/shard_map/ppermute | solution.py:418
  434.1 57.7 %collective-permute-start.6 = (bf16[256,2816]{1,0:T(8,128)(2,1)}, bf16[256,2816]{1,0:T(8,128)(2,1)}, u32[]{:S(2)}, u32[]{:S(2)}) collective-permute-start(bf16[256,2816]{1,0:T(8,128)(2,1)} %get-tuple-element.57), channel_id=1, source_target_pairs={{0,16},{16,0},{1,17},{17,1},{2,18},{18,2},{3,19},{19,3},{4,20},{20... | collective-permute-start | bytes 4325384 | tf_op jit(solution)/shard_map/ppermute | solution.py:418
  453.3 565.3 %all-to-all-start.2 = ((bf16[16,384,512]{2,1,0:T(8,128)(2,1)}), bf16[16,384,512]{2,1,0:T(8,128)(2,1)}, u32[]{:S(2)}, u32[]{:S(2)}) async-start(bf16[16,384,512]{2,1,0:T(8,128)(2,1)} %bitcast.357), calls=%async_computation.2 | async-start | bytes 12582912 | tf_op jit(solution)/shard_map/all_to_all | solution.py:566
  482.0 523.4 %reduce-scatter.4.cloned.1.call-start = ((), (), s32[]{:S(2)}) async-start(), calls=%async_computation.9 | async-start | bytes 557056
  482.3 91.0 %collective-permute-start.39 = (bf16[4,2,64,1408]{3,2,0,1:T(8,128)(2,1)}, bf16[4,2,64,1408]{3,2,0,1:T(8,128)(2,1)}, u32[]{:S(2)}, u32[]{:S(2)}) collective-permute-start(bf16[4,2,64,1408]{3,2,0,1:T(8,128)(2,1)} %bitcast.341), channel_id=1, source_target_pairs={{0,2},{1,3},{2,0},{3,1},{4,6},{5,7},{6,4},{7,5},{8,10},{9,11},{10,... | collective-permute-start | bytes 4325384 | tf_op jit(solution)/shard_map/ppermute | solution.py:398
  491.7 123.3 %collective-permute-start.14 = (bf16[4,2,64,1408]{3,2,0,1:T(8,128)(2,1)S(1)}, bf16[4,2,64,1408]{3,2,0,1:T(8,128)(2,1)}, u32[]{:S(2)}, u32[]{:S(2)}) collective-permute-start(bf16[4,2,64,1408]{3,2,0,1:T(8,128)(2,1)S(1)} %bitcast.368), channel_id=1, source_target_pairs={{0,2},{1,3},{2,0},{3,1},{4,6},{5,7},{6,4},{7,5},{8,10},{9,11},{10,... | collective-permute-start | bytes 4325384 | tf_op jit(solution)/shard_map/ppermute | solution.py:398
  491.8 168.0 %collective-permute-start.48 = (bf16[4,2,64,2048]{3,2,0,1:T(8,128)(2,1)}, bf16[4,2,64,2048]{3,2,0,1:T(8,128)(2,1)S(1)}, u32[]{:S(2)}, u32[]{:S(2)}) collective-permute-start(bf16[4,2,64,2048]{3,2,0,1:T(8,128)(2,1)} %bitcast.340), channel_id=1, source_target_pairs={{0,2},{1,3},{2,0},{3,1},{4,6},{5,7},{6,4},{7,5},{8,10},{9,11},{10,... | collective-permute-start | bytes 6291464 | tf_op jit(solution)/shard_map/ppermute | solution.py:398
  520.4 186.7 %collective-permute-start.25 = (bf16[4,2,64,2048]{3,2,1,0:T(8,128)(2,1)}, bf16[4,2,64,2048]{3,2,1,0:T(8,128)(2,1)}, u32[]{:S(2)}, u32[]{:S(2)}) collective-permute-start(bf16[4,2,64,2048]{3,2,1,0:T(8,128)(2,1)} %dynamic-slice_bitcast_fusion), channel_id=1, source_target_pairs={{0,2},{1,3},{2,0},{3,1},{4,6},{5,7},{6,4},{7,5},{8,10},{9,11},{10,... | collective-permute-start | bytes 6291464 | tf_op jit(solution)/shard_map/ppermute | solution.py:398
  575.2 90.9 %collective-permute-start.40 = (bf16[4,64,1408]{2,1,0:T(8,128)(2,1)S(1)}, bf16[4,64,1408]{2,1,0:T(8,128)(2,1)S(1)}, u32[]{:S(2)}, u32[]{:S(2)}) collective-permute-start(bf16[4,64,1408]{2,1,0:T(8,128)(2,1)S(1)} %dynamic-slice_bitcast_fusion.6), channel_id=1, source_target_pairs={{0,1},{1,0},{2,3},{3,2},{4,5},{5,4},{6,7},{7,6},{8,9},{9,8},{10,11... | collective-permute-start | bytes 2162696 | tf_op jit(solution)/shard_map/ppermute | solution.py:398
  616.9 53.5 %collective-permute-start.15 = (bf16[4,64,1408]{2,1,0:T(8,128)(2,1)S(1)}, bf16[4,64,1408]{2,1,0:T(8,128)(2,1)S(1)}, u32[]{:S(2)}, u32[]{:S(2)}) collective-permute-start(bf16[4,64,1408]{2,1,0:T(8,128)(2,1)S(1)} %dynamic-slice_bitcast_fusion.7), channel_id=1, source_target_pairs={{0,1},{1,0},{2,3},{3,2},{4,5},{5,4},{6,7},{7,6},{8,9},{9,8},{10,11... | collective-permute-start | bytes 2162696 | tf_op jit(solution)/shard_map/ppermute | solution.py:398
  664.6 40.0 %collective-permute-start.49 = (bf16[4,64,2048]{2,1,0:T(8,128)(2,1)}, bf16[4,64,2048]{2,1,0:T(8,128)(2,1)}, u32[]{:S(2)}, u32[]{:S(2)}) collective-permute-start(bf16[4,64,2048]{2,1,0:T(8,128)(2,1)} %dynamic-slice_bitcast_fusion.3), channel_id=1, source_target_pairs={{0,1},{1,0},{2,3},{3,2},{4,5},{5,4},{6,7},{7,6},{8,9},{9,8},{10,11... | collective-permute-start | bytes 3145736 | tf_op jit(solution)/shard_map/ppermute | solution.py:398
  670.4 20.2 %collective-permute-start.42 = (bf16[64,1408]{1,0:T(8,128)(2,1)}, bf16[64,1408]{1,0:T(8,128)(2,1)}, u32[]{:S(2)}, u32[]{:S(2)}) collective-permute-start(bf16[64,1408]{1,0:T(8,128)(2,1)} %get-tuple-element.97), channel_id=1, source_target_pairs={{0,8},{1,9},{2,10},{3,11},{4,12},{5,13},{6,14},{7,15},{8,0},{9,1},... | collective-permute-start | bytes 540680 | tf_op jit(solution)/shard_map/ppermute | solution.py:398
  670.4 20.8 %collective-permute-start.41 = (bf16[64,1408]{1,0:T(8,128)(2,1)}, bf16[64,1408]{1,0:T(8,128)(2,1)}, u32[]{:S(2)}, u32[]{:S(2)}) collective-permute-start(bf16[64,1408]{1,0:T(8,128)(2,1)} %get-tuple-element.95), channel_id=1, source_target_pairs={{0,4},{1,5},{2,6},{3,7},{4,8},{5,9},{6,10},{7,11},{8,12},{9,13},{1... | collective-permute-start | bytes 540680 | tf_op jit(solution)/shard_map/ppermute | solution.py:398
  675.4 19.9 %collective-permute-start.18 = (bf16[64,1408]{1,0:T(8,128)(2,1)}, bf16[64,1408]{1,0:T(8,128)(2,1)}, u32[]{:S(2)}, u32[]{:S(2)}) collective-permute-start(bf16[64,1408]{1,0:T(8,128)(2,1)} %get-tuple-element.93), channel_id=1, source_target_pairs={{0,12},{1,13},{2,14},{3,15},{4,0},{5,1},{6,2},{7,3},{8,4},{9,5},{1... | collective-permute-start | bytes 540680 | tf_op jit(solution)/shard_map/ppermute | solution.py:398
  690.6 65.5 %collective-permute-start.32 = (bf16[4,2,64,2816]{3,2,0,1:T(8,128)(2,1)S(1)}, bf16[4,2,64,2816]{3,2,0,1:T(8,128)(2,1)S(1)}, u32[]{:S(2)}, u32[]{:S(2)}) collective-permute-start(bf16[4,2,64,2816]{3,2,0,1:T(8,128)(2,1)S(1)} %bitcast.364), channel_id=1, source_target_pairs={{0,1},{1,0},{2,3},{3,2},{4,5},{5,4},{6,7},{7,6},{8,9},{9,8},{10,11... | collective-permute-start | bytes 8650760 | tf_op jit(solution)/shard_map/ppermute | solution.py:398
  702.9 115.0 %collective-permute-start.7 = (bf16[4,2,64,2816]{3,2,0,1:T(8,128)(2,1)S(1)}, bf16[4,2,64,2816]{3,2,0,1:T(8,128)(2,1)S(1)}, u32[]{:S(2)}, u32[]{:S(2)}) collective-permute-start(bf16[4,2,64,2816]{3,2,0,1:T(8,128)(2,1)S(1)} %bitcast.363), channel_id=1, source_target_pairs={{0,1},{1,0},{2,3},{3,2},{4,5},{5,4},{6,7},{7,6},{8,9},{9,8},{10,11... | collective-permute-start | bytes 8650760 | tf_op jit(solution)/shard_map/ppermute | solution.py:398
  706.3 19.0 %collective-permute-start.51 = (bf16[64,2048]{1,0:T(8,128)(2,1)S(1)}, bf16[64,2048]{1,0:T(8,128)(2,1)S(1)}, u32[]{:S(2)}, u32[]{:S(2)}) collective-permute-start(bf16[64,2048]{1,0:T(8,128)(2,1)S(1)} %get-tuple-element.89), channel_id=1, source_target_pairs={{0,8},{1,9},{2,10},{3,11},{4,12},{5,13},{6,14},{7,15},{8,0},{9,1},... | collective-permute-start | bytes 786440 | tf_op jit(solution)/shard_map/ppermute | solution.py:398
  707.1 19.4 %collective-permute-start.50 = (bf16[64,2048]{1,0:T(8,128)(2,1)S(1)}, bf16[64,2048]{1,0:T(8,128)(2,1)S(1)}, u32[]{:S(2)}, u32[]{:S(2)}) collective-permute-start(bf16[64,2048]{1,0:T(8,128)(2,1)S(1)} %get-tuple-element.87), channel_id=1, source_target_pairs={{0,4},{1,5},{2,6},{3,7},{4,8},{5,9},{6,10},{7,11},{8,12},{9,13},{1... | collective-permute-start | bytes 786440 | tf_op jit(solution)/shard_map/ppermute | solution.py:398
  715.5 292.5 %collective-permute-start.1 = (bf16[256,1024]{1,0:T(8,128)(2,1)}, bf16[256,1024]{1,0:T(8,128)(2,1)}, u32[]{:S(2)}, u32[]{:S(2)}) collective-permute-start(bf16[256,1024]{1,0:T(8,128)(2,1)} %get-tuple-element.91), channel_id=1, source_target_pairs={{0,16},{16,0},{1,17},{17,1},{2,18},{18,2},{3,19},{19,3},{4,20},{20... | collective-permute-start | bytes 1572872 | tf_op jit(solution)/shard_map/ppermute | solution.py:418
  725.3 108.8 %collective-permute-start.26 = (bf16[4,64,2048]{2,1,0:T(8,128)(2,1)S(1)}, bf16[4,64,2048]{2,1,0:T(8,128)(2,1)S(1)}, u32[]{:S(2)}, u32[]{:S(2)}) collective-permute-start(bf16[4,64,2048]{2,1,0:T(8,128)(2,1)S(1)} %dynamic-slice_bitcast_fusion.4), channel_id=1, source_target_pairs={{0,1},{1,0},{2,3},{3,2},{4,5},{5,4},{6,7},{7,6},{8,9},{9,8},{10,11... | collective-permute-start | bytes 3145736 | tf_op jit(solution)/shard_map/ppermute | solution.py:398
  756.9 98.8 %collective-permute-start.33 = (bf16[4,64,2816]{2,1,0:T(8,128)(2,1)S(1)}, bf16[4,64,2816]{2,1,0:T(8,128)(2,1)S(1)}, u32[]{:S(2)}, u32[]{:S(2)}) collective-permute-start(bf16[4,64,2816]{2,1,0:T(8,128)(2,1)S(1)} %dynamic-slice_bitcast_fusion.1), channel_id=1, source_target_pairs={{0,2},{1,3},{2,0},{3,1},{4,6},{5,7},{6,4},{7,5},{8,10},{9,11},{10,... | collective-permute-start | bytes 4325384 | tf_op jit(solution)/shard_map/ppermute | solution.py:398
  838.0 17.6 %collective-permute-start.28 = (bf16[64,2048]{1,0:T(8,128)(2,1)S(1)}, bf16[64,2048]{1,0:T(8,128)(2,1)S(1)}, u32[]{:S(2)}, u32[]{:S(2)}) collective-permute-start(bf16[64,2048]{1,0:T(8,128)(2,1)S(1)} %get-tuple-element.86), channel_id=1, source_target_pairs={{0,8},{1,9},{2,10},{3,11},{4,12},{5,13},{6,14},{7,15},{8,0},{9,1},... | collective-permute-start | bytes 786440 | tf_op jit(solution)/shard_map/ppermute | solution.py:398
  838.0 17.6 %collective-permute-start.27 = (bf16[64,2048]{1,0:T(8,128)(2,1)S(1)}, bf16[64,2048]{1,0:T(8,128)(2,1)S(1)}, u32[]{:S(2)}, u32[]{:S(2)}) collective-permute-start(bf16[64,2048]{1,0:T(8,128)(2,1)S(1)} %get-tuple-element.84), channel_id=1, source_target_pairs={{0,4},{1,5},{2,6},{3,7},{4,8},{5,9},{6,10},{7,11},{8,12},{9,13},{1... | collective-permute-start | bytes 786440 | tf_op jit(solution)/shard_map/ppermute | solution.py:398
  845.4 27.4 %collective-permute-start.8 = (bf16[4,64,2816]{2,1,0:T(8,128)(2,1)S(1)}, bf16[4,64,2816]{2,1,0:T(8,128)(2,1)S(1)}, u32[]{:S(2)}, u32[]{:S(2)}) collective-permute-start(bf16[4,64,2816]{2,1,0:T(8,128)(2,1)S(1)} %dynamic-slice_bitcast_fusion.2), channel_id=1, source_target_pairs={{0,2},{1,3},{2,0},{3,1},{4,6},{5,7},{6,4},{7,5},{8,10},{9,11},{10,... | collective-permute-start | bytes 4325384 | tf_op jit(solution)/shard_map/ppermute | solution.py:398
  856.3 24.9 %collective-permute-start.36 = (bf16[64,2816]{1,0:T(8,128)(2,1)S(1)}, bf16[64,2816]{1,0:T(8,128)(2,1)S(1)}, u32[]{:S(2)}, u32[]{:S(2)}) collective-permute-start(bf16[64,2816]{1,0:T(8,128)(2,1)S(1)} %get-tuple-element.80), channel_id=1, source_target_pairs={{0,12},{1,13},{2,14},{3,15},{4,0},{5,1},{6,2},{7,3},{8,4},{9,5},{1... | collective-permute-start | bytes 1081352 | tf_op jit(solution)/shard_map/ppermute | solution.py:398
  856.3 53.6 %collective-permute-start.35 = (bf16[64,2816]{1,0:T(8,128)(2,1)S(1)}, bf16[64,2816]{1,0:T(8,128)(2,1)S(1)}, u32[]{:S(2)}, u32[]{:S(2)}) collective-permute-start(bf16[64,2816]{1,0:T(8,128)(2,1)S(1)} %get-tuple-element.81), channel_id=1, source_target_pairs={{0,8},{1,9},{2,10},{3,11},{4,12},{5,13},{6,14},{7,15},{8,0},{9,1},... | collective-permute-start | bytes 1081352 | tf_op jit(solution)/shard_map/ppermute | solution.py:398
  870.9 39.1 %collective-permute-start.34 = (bf16[64,2816]{1,0:T(8,128)(2,1)S(1)}, bf16[64,2816]{1,0:T(8,128)(2,1)S(1)}, u32[]{:S(2)}, u32[]{:S(2)}) collective-permute-start(bf16[64,2816]{1,0:T(8,128)(2,1)S(1)} %get-tuple-element.79), channel_id=1, source_target_pairs={{0,4},{1,5},{2,6},{3,7},{4,8},{5,9},{6,10},{7,11},{8,12},{9,13},{1... | collective-permute-start | bytes 1081352 | tf_op jit(solution)/shard_map/ppermute | solution.py:398
  873.3 36.9 %collective-permute-start.11 = (bf16[64,2816]{1,0:T(8,128)(2,1)S(1)}, bf16[64,2816]{1,0:T(8,128)(2,1)S(1)}, u32[]{:S(2)}, u32[]{:S(2)}) collective-permute-start(bf16[64,2816]{1,0:T(8,128)(2,1)S(1)} %get-tuple-element.75), channel_id=1, source_target_pairs={{0,12},{1,13},{2,14},{3,15},{4,0},{5,1},{6,2},{7,3},{8,4},{9,5},{1... | collective-permute-start | bytes 1081352 | tf_op jit(solution)/shard_map/ppermute | solution.py:398
  881.1 43.0 %collective-permute-start.10 = (bf16[64,2816]{1,0:T(8,128)(2,1)S(1)}, bf16[64,2816]{1,0:T(8,128)(2,1)S(1)}, u32[]{:S(2)}, u32[]{:S(2)}) collective-permute-start(bf16[64,2816]{1,0:T(8,128)(2,1)S(1)} %get-tuple-element.76), channel_id=1, source_target_pairs={{0,8},{1,9},{2,10},{3,11},{4,12},{5,13},{6,14},{7,15},{8,0},{9,1},... | collective-permute-start | bytes 1081352 | tf_op jit(solution)/shard_map/ppermute | solution.py:398
  925.4 87.5 %collective-permute-start.53 = (bf16[64,6272]{1,0:T(8,128)(2,1)}, bf16[64,6272]{1,0:T(8,128)(2,1)}, u32[]{:S(2)}, u32[]{:S(2)}) collective-permute-start(bf16[64,6272]{1,0:T(8,128)(2,1)} %broadcast_select_fusion.1), channel_id=1, source_target_pairs={{0,16},{16,0},{1,17},{17,1},{2,18},{18,2},{3,19},{19,3},{4,20},{20... | collective-permute-start | bytes 2408456 | tf_op jit(solution)/shard_map/ppermute | solution.py:418
  926.5 192.0 %all-reduce.3.cloned.1.call-start = ((), (), s32[]{:S(2)}) async-start(), calls=%async_computation.8 | async-start | bytes 1081344 | tf_op jit(solution)/shard_map/psum | solution.py:573
  (111 other events, 1753.8 us)
Sparse Core Ops, SparseCore 0:
  11.9 8.7 sort.19.cloned.1.call-done
  926.6 78.7 reduce-scatter.3
  1013.0 105.4 all-reduce.2
  (1 shorter events, 0.0 us)
Sparse Core Ops, SparseCore 1:
  11.6 27.5 all-gather.4
  40.5 14.7 all-gather.6
  56.7 39.7 all-gather.8
  98.1 24.9 all-gather.10

commit v2 on v1

--- a/solution.py
+++ b/solution.py
@@ -19,6 +19,7 @@
 VMEM_BYTES = 48 * 1024 * 1024
 
 epsilon = 1e-05
+A, B = (2, 1, 0), (1, 2, 0)
 f32 = jnp.float32
 bf16 = jnp.bfloat16
 
@@ -375,43 +376,253 @@
     return sides
 
 
-def sum_along(block, sides, kept, which):
-    stride = 1
-    for side in sides[which + 1 :]:
-        stride *= side
-    size = sides[which]
-    if size == 1:
-        return block
-    total = sides[0] * sides[1] * sides[2]
-    place = (lax.axis_index("rows") // stride) % size
-    axis = kept.index(which)
-
-    def part(index):
-        return lax.dynamic_index_in_dim(block, index, axis, keepdims=False)
-
-    result = part(place).astype(f32)
-    for step in range(1, size):
-        route = []
-        for device in range(total):
-            own = (device // stride) % size
-            route.append((device, device + ((own + step) % size - own) * stride))
-        arrived = lax.ppermute(part((place + step) % size), "rows", route)
-        result = result + arrived.astype(f32)
-    return result.astype(bf16)
-
-
-def scatter_sum(block, order):
+def at_place(ref, axis, place):
+    return ref.at[(slice(None),) * axis + (place,)]
+
+
+def sum_kernel(sides, plan, counts, *refs):
+    devices = sides[0] * sides[1] * sides[2]
+    arrays, refs = refs[: counts[0]], refs[counts[0] :]
+    blocks_ref, refs = refs[0], refs[1:]
+    outs, refs = refs[: counts[1]], refs[counts[1] :]
+    gathered_ref, arrived_ref, refs = refs[0], refs[1], refs[2:]
+    pieces = len(plan)
+    owns, refs = refs[:pieces], refs[pieces:]
+    lands, refs = [refs[3 * i : 3 * i + 3] for i in range(pieces)], refs[3 * pieces :]
+    send_sems, land_sems, load_sems, trade_send, trade_land, spread_send, spread_land, own_sem = refs
+    most = max(sides) - 1
+
+    me = lax.axis_index("rows")
+    strides = (sides[1] * sides[2], sides[2], 1)
+    places = [(me // strides[d]) % sides[d] for d in range(3)]
+
+    def other(step):
+        return lax.rem(me + step, devices)
+
+    barrier = pltpu.get_barrier_semaphore()
+    for step in range(1, devices):
+        pl.semaphore_signal(
+            barrier, inc=1, device_id={"rows": other(step)}, device_id_type=pl.DeviceIdType.MESH
+        )
+    pl.semaphore_wait(barrier, devices - 1)
+
+    def remote(source, target, send, land, device):
+        return pltpu.make_async_remote_copy(
+            src_ref=source,
+            dst_ref=target,
+            send_sem=send,
+            recv_sem=land,
+            device_id={"rows": device},
+            device_id_type=pl.DeviceIdType.MESH,
+        )
+
+    def source_of(piece):
+        array, first, width, order = plan[piece]
+        return arrays[array].at[:, :, :, :, pl.ds(first, width)]
+
+    def sends(piece, phase):
+        order = plan[piece][3]
+        axis = order[phase]
+        left = [d for d in range(3) if d not in order[:phase]]
+        at = left.index(axis)
+        ref = source_of(piece) if phase == 0 else kept(piece, phase)
+        copies = []
+        for step in range(1, sides[axis]):
+            there = lax.rem(places[axis] + step, sides[axis])
+            device = me + (there - places[axis]) * strides[axis]
+            slot = (piece * 3 + phase) * most + step - 1
+            copies.append(
+                remote(
+                    at_place(ref, at, there),
+                    lands[piece][phase].at[step - 1],
+                    send_sems.at[slot],
+                    land_sems.at[slot],
+                    device,
+                )
+            )
+        return copies
+
+    def kept(piece, phase):
+        order = plan[piece][3]
+        ref = owns[piece]
+        left = [d for d in range(3) if d != order[0]]
+        for axis in order[1:phase]:
+            ref = at_place(ref, left.index(axis), places[axis])
+            left.remove(axis)
+        return ref
+
+    def load(piece):
+        axis = plan[piece][3][0]
+        return pltpu.make_async_copy(
+            at_place(source_of(piece), axis, places[axis]), owns[piece], load_sems.at[piece]
+        )
+
+    def add(piece, phase):
+        target = kept(piece, phase + 1)
+        land = lands[piece][phase]
+        leads = target.shape[:-2]
+        count = 1
+        for size in leads:
+            count *= size
+        rows = 16
+        groups = target.shape[-2] // rows
+
+        def body(index, carry):
+            at = (pl.ds(pl.multiple_of(index % groups * rows, rows), rows), slice(None))
+            lead = index // groups
+            if len(leads) == 2:
+                at = (lead // leads[1], lead % leads[1]) + at
+            elif len(leads) == 1:
+                at = (lead,) + at
+            value = target[at].astype(f32)
+            for step in range(land.shape[0]):
+                value = value + land[(step,) + at].astype(f32)
+            target[at] = value.astype(bf16)
+            return carry
+
+        lax.fori_loop(0, count * groups, body, 0)
+
+    def start(copies):
+        for copy in copies:
+            copy.start()
+
+    def settle(piece, phase):
+        for copy in sends(piece, phase):
+            copy.wait_recv()
+
+    def trades():
+        return [
+            remote(
+                blocks_ref.at[other(step)],
+                arrived_ref.at[me],
+                trade_send.at[step - 1],
+                trade_land.at[step - 1],
+                other(step),
+            )
+            for step in range(1, devices)
+        ]
+
+    def spreads():
+        return [
+            remote(
+                gathered_ref.at[me],
+                gathered_ref.at[me],
+                spread_send.at[step - 1],
+                spread_land.at[step - 1],
+                other(step),
+            )
+            for step in range(1, devices)
+        ]
+
+    def trade_landing(step):
+        back = lax.rem(me + devices - step, devices)
+        return remote(
+            blocks_ref.at[back], arrived_ref.at[back], trade_send.at[step - 1], trade_land.at[step - 1], back
+        )
+
+    def spread_landing(step):
+        back = lax.rem(me + devices - step, devices)
+        return remote(
+            gathered_ref.at[me], gathered_ref.at[back], spread_send.at[step - 1], spread_land.at[step - 1], back
+        )
+
+    groups = [[i for i in range(pieces) if plan[i][3] == order] for order in (A, B)]
+    for rank in range(2):
+        for group in groups:
+            if rank < len(group):
+                start(sends(group[rank], 0))
+                load(group[rank]).start()
+    start(trades())
+    own_block = pltpu.make_async_copy(blocks_ref.at[me], arrived_ref.at[me], own_sem)
+    own_block.start()
+
+    def finish(piece):
+        settle(piece, 2)
+        add(piece, 2)
+        array, first, width, order = plan[piece]
+        if array < counts[1]:
+            outs[array][:, first : first + width] = kept(piece, 3)[...]
+        else:
+            gathered_ref[me] = kept(piece, 3)[...]
+            start(spreads())
+
+    rounds = max(len(group) for group in groups)
+    for turn in range(rounds + 2):
+        for group in groups:
+            if turn < len(group):
+                piece = group[turn]
+                settle(piece, 0)
+                if turn + 2 < len(group):
+                    start(sends(group[turn + 2], 0))
+                    load(group[turn + 2]).start()
+                load(piece).wait()
+                add(piece, 0)
+                start(sends(piece, 1))
+            if 0 <= turn - 1 < len(group):
+                piece = group[turn - 1]
+                settle(piece, 1)
+                add(piece, 1)
+                start(sends(piece, 2))
+            if 0 <= turn - 2 < len(group):
+                finish(group[turn - 2])
+
+    for piece in range(pieces):
+        for phase in range(3):
+            for copy in sends(piece, phase):
+                copy.wait_send()
+    own_block.wait()
+    for copy in trades():
+        copy.wait_send()
+    for copy in spreads():
+        copy.wait_send()
+    for step in range(1, devices):
+        trade_landing(step).wait_recv()
+        spread_landing(step).wait_recv()
+
+
+def sum_and_trade(arrays, plan, extra, blocks):
     devices = lax.axis_size("rows")
     sides = factors(devices)
-    kept = [0, 1, 2]
-    block = block.reshape(*sides, block.shape[0] // devices, block.shape[1])
-    for which in order:
-        if sides[which] == 1:
-            block = block.reshape([s for d, s in enumerate(block.shape) if d != kept.index(which)])
-        else:
-            block = sum_along(block, sides, kept, which)
-        kept.remove(which)
-    return block
+    rows = arrays[0].shape[0] // devices
+    plan = plan + [(len(arrays), 0, extra.shape[1], B)]
+    operands = [array.reshape(*sides, rows, array.shape[1]) for array in (*arrays, extra)]
+    owns, lands = [], []
+    for array, first, width, order in plan:
+        left = [0, 1, 2]
+        for which in order:
+            left.remove(which)
+            shape = tuple(sides[d] for d in left) + (rows, width)
+            if which == order[0]:
+                owns.append(pltpu.VMEM(shape, bf16))
+            lands.append(pltpu.VMEM((max(sides[which] - 1, 1),) + shape, bf16))
+    copies = len(plan) * 3 * (max(sides) - 1)
+    return pl.pallas_call(
+        functools.partial(sum_kernel, tuple(sides), tuple(plan), (len(operands), len(arrays))),
+        in_specs=[pl.BlockSpec(memory_space=pl.ANY)] * (len(operands) + 1),
+        out_specs=[pl.BlockSpec(memory_space=pltpu.VMEM)] * (len(arrays) + 1) + [pl.BlockSpec(memory_space=pl.ANY)],
+        out_shape=[jax.ShapeDtypeStruct((rows, array.shape[1]), bf16) for array in arrays]
+        + [
+            jax.ShapeDtypeStruct((devices, rows, extra.shape[1]), bf16),
+            jax.ShapeDtypeStruct(blocks.shape, blocks.dtype),
+        ],
+        scratch_shapes=[
+            *owns,
+            *lands,
+            pltpu.SemaphoreType.DMA((copies,)),
+            pltpu.SemaphoreType.DMA((copies,)),
+            pltpu.SemaphoreType.DMA((len(plan),)),
+            pltpu.SemaphoreType.DMA((devices - 1,)),
+            pltpu.SemaphoreType.DMA((devices - 1,)),
+            pltpu.SemaphoreType.DMA((devices - 1,)),
+            pltpu.SemaphoreType.DMA((devices - 1,)),
+            pltpu.SemaphoreType.DMA,
+        ],
+        compiler_params=pltpu.CompilerParams(
+            collective_id=0, has_side_effects=True, vmem_limit_bytes=56 * 1024 * 1024
+        ),
+        cost_estimate=pl.CostEstimate(flops=10**9, bytes_accessed=6 * 10**8, transcendentals=0),
+        name="sum_and_trade",
+    )(*operands, blocks)
 
 
 def swap(array):
@@ -453,7 +664,7 @@
     slots = by_owner(order_key % positions).reshape(-1)
     requested = lax.all_to_all(by_owner(grouped), "rows", split_axis=0, concat_axis=0, tiled=True)
     flat_tables = hash_tables.reshape(count_tables * shard_rows, half_width)
-    found_rows = jnp.take(flat_tables, requested, axis=0)
+    found_rows = flat_tables.at[requested].get(mode="promise_in_bounds")
     returned = lax.all_to_all(found_rows, "rows", split_axis=0, concat_axis=0, tiled=True)
 
     gains = both(norm_gains).astype(f32)
@@ -523,25 +734,24 @@
     grad_middle, gain_two_second, grad_joined, grad_branch = feed_back(
         middle_two, gains[1, 1], gate_up_both[1], down_both[1], kept_two, grad_kept
     )
-    gate_up_two = scatter_sum(share(kept_two[0], grad_joined), (2, 1, 0))
-    down_two = scatter_sum(share(grad_branch, kept_two[3]), (1, 2, 0))
+    gate_up_two = share(kept_two[0], grad_joined)
+    down_two = share(grad_branch, kept_two[3])
     grad_low = grad_middle.astype(bf16)
     grad_attended = dot_nt(grad_low, out_both[1]).astype(bf16)
     grad_mixed = jnp.concatenate(causal_attention_back(mixed, grad_attended), axis=1)
-    rest_two = scatter_sum(
-        jnp.concatenate([share(normed_two, grad_mixed), share(attended_two, grad_low)], axis=1), (1, 2, 0)
-    )
+    rest_two = jnp.concatenate([share(normed_two, grad_mixed), share(attended_two, grad_low)], axis=1)
     grad_normed = dot_nt(grad_mixed, qkv_both[1])
     grad_in, gain_two_first = normalize_back(inputs_two, gains[1, 0], inverse_two, grad_normed)
     grad_encoded = jnp.where(valid, 0.0, cotangent_two) + grad_middle + grad_in
+
 
     grad_out = cotangent_one + grad_encoded.astype(bf16).astype(f32)
     grad_kept = jnp.where(valid, grad_out, 0.0)
     grad_middle, gain_one_second, grad_joined, grad_branch = feed_back(
         middle_one, gains[0, 1], gate_up_both[0], down_both[0], kept_one, grad_kept
     )
-    gate_up_one = scatter_sum(share(kept_one[0], grad_joined), (2, 1, 0))
-    down_one = scatter_sum(share(grad_branch, kept_one[3]), (1, 2, 0))
+    gate_up_one = share(kept_one[0], grad_joined)
+    down_one = share(grad_branch, kept_one[3])
     grad_low = grad_middle.astype(bf16)
     grad_attended = dot_nt(grad_low, out_both[0]).astype(bf16)
     grad_queries, grad_keys, grad_values = patch_attention_back(
@@ -553,6 +763,7 @@
     grad_pooled = jnp.where(valid, 0.0, grad_out) + grad_middle + grad_in
     grad_bytes = dot(member_byte, (grad_pooled / counts).astype(bf16))
     grad_bytes = (grad_bytes + dot_nt(grad_pairs, qkv_both[0, :, D:])).astype(bf16)
+
 
     grad_halves = grad_bytes.reshape(L, 2, half_width)
     kept_grad = lax.dynamic_index_in_dim(grad_halves, section, 1, keepdims=False)
@@ -562,23 +773,36 @@
         jnp.concatenate([kept_grad, sent_grad], axis=0),
         jnp.concatenate([sent_grad, kept_grad], axis=0),
     )
+    rest_one = jnp.concatenate(
+        [share(normed_one, grad_queries), share(byte_rows, grad_pairs), share(attended_one, grad_low)], axis=1
+    )
     slot_grads = spread(slots[:, None], own_grad).reshape(devices, -1, half_width)
-    arrived = lax.all_to_all(slot_grads, "rows", split_axis=0, concat_axis=0, tiled=True)
+    words = (flat_bytes[:, None] == jnp.arange(table_rows, dtype=jnp.int32)[None, :]).astype(bf16)
+    table_part = dot_tn(words, own_grad).reshape(D, -1)
+    gain_part = jnp.stack([gain_one_first, gain_one_second, gain_two_first, gain_two_second], axis=1)
+    gain_part = gain_part + swap(gain_part)
+    table_columns = table_part.shape[1]
+    extra = jnp.concatenate([table_part, gain_part], axis=1)
+    extra = jnp.pad(extra, ((0, 0), (0, -extra.shape[1] % 128))).astype(bf16)
+
+    plan = []
+    for array in (0, 3):
+        width = FF // 2
+        plan += [(array, 0, width, A), (array, width, width, A), (array + 1, 0, width, B)]
+        plan += [(array + 2, 0, D, B), (array + 2, D, D, B)]
+    sums = sum_and_trade(
+        [gate_up_two, down_two, rest_two, gate_up_one, down_one, rest_one], plan, extra, slot_grads
+    )
+    gate_up_two, down_two, rest_two, gate_up_one, down_one, rest_one, gathered, arrived = sums
     hash_grad = jax.ops.segment_sum(
         arrived.reshape(-1, half_width).astype(f32),
         requested.reshape(-1),
         num_segments=count_tables * shard_rows,
     ).reshape(count_tables, shard_rows, half_width)
-    words = (flat_bytes[:, None] == jnp.arange(table_rows, dtype=jnp.int32)[None, :]).astype(bf16)
-    byte_table_grad = lax.psum(dot_tn(words, own_grad), "rows")
-
-    rest_one = scatter_sum(
-        jnp.concatenate(
-            [share(normed_one, grad_queries), share(byte_rows, grad_pairs), share(attended_one, grad_low)],
-            axis=1,
-        ),
-        (1, 2, 0),
-    )
+    byte_table_grad = gathered[:, :, :table_columns].reshape(table_rows, half_width).astype(f32)
+    gain_sums = lax.dynamic_index_in_dim(gathered, lax.axis_index("rows"), 0, keepdims=False)
+    gain_sums = gain_sums[:, table_columns : table_columns + 4].T.reshape(2, 2, -1).astype(f32)
+    gains_grad = lax.dynamic_index_in_dim(gain_sums, section, 0, keepdims=True)
 
     sums_one = jnp.concatenate([gate_up_one, down_one, rest_one], axis=1)
     sums_two = jnp.concatenate([gate_up_two, down_two, rest_two], axis=1)
@@ -597,11 +821,6 @@
     qkv_grad = jnp.where(
         first_core, jnp.concatenate(pieces_one, axis=1), jnp.concatenate(pieces_two, axis=1)
     )
-
-    gain_sums = jnp.stack([gain_one_first, gain_one_second, gain_two_first, gain_two_second])
-    gain_sums = lax.psum_scatter(gain_sums, "rows", scatter_dimension=1, tiled=True)
-    gain_sums = (gain_sums + swap(gain_sums)).reshape(2, 2, -1)
-    gains_grad = lax.dynamic_index_in_dim(gain_sums, section, 0, keepdims=True)
 
     return (
         section_out,

time: 1140 us -> 925 us (0.81)
  waiting for transfers between devices: 559 us -> 114 us
  Pallas kernels: 72.9 us -> 431 us
  starting transfers between devices: 93.2 us -> 11.7 us
  local copies, waits for them, and re-layouts: 119 us -> 96.1 us
  other arithmetic: 114 us -> 92.1 us
    pallas_call x0 -> x1, Pallas kernels: none -> 358 us  [sum_and_trade(): pl.pallas_call(functools.partial(sum_kernel, tuple(sides), tuple(plan), (...]
    ppermute x30 -> x0, waiting for transfers between devices: 323 us -> none  [sum_along(): arrived = lax.ppermute(part((place + step) % size), 'rows', route)]
    unnamed x7 -> x4, waiting for transfers between devices: 80.9 us -> 2.25 us
    ppermute x30 -> x0, starting transfers between devices: 52.8 us -> none  [sum_along(): arrived = lax.ppermute(part((place + step) % size), 'rows', route)]
    psum x1 -> x0, waiting for transfers between devices: 41.8 us -> none  [on_device(): byte_table_grad = lax.psum(dot_tn(words, own_grad), 'rows')]
    all_to_all x1 -> x0, starting transfers between devices: 28.8 us -> none  [on_device(): lax.all_to_all(slot_grads, 'rows', split_axis=0, concat_axis=0, tiled=True)]
    dynamic_slice x8 -> x0, local copies, waits for them, and re-layouts: 18.3 us -> none  [part(): return lax.dynamic_index_in_dim(block, index, axis, keepdims=False)]
    convert_element_type x18 -> x2, other arithmetic: 16 us -> 0.19 us  [the longest x1 0.11 us: on_device(): gathered[:, :, :table_columns].reshape(table_rows, half_width).astype(f32)]
  transfers between devices with their start and end apart: 62 -> 29, of which waited for: 19 -> 1; matrix products, arithmetic and copies ran while one was open for 30% -> 32% of each run, Pallas kernels for 6% -> 47%
where the time goes in v2:
time: 925 us; the launch traced here: 914 us
  Pallas kernels  431 us (47%)
  matrix products  134 us (14%)
  waiting for transfers between devices  114 us (12%)
  local copies, waits for them, and re-layouts  96.1 us (10%)
  other arithmetic  92.1 us (10%)
  blocking collectives  17.5 us (2%)
  between operations  17.3 us (2%)
  starting transfers between devices  11.7 us (1%)
    pallas_call x1, Pallas kernels, sum_and_trade(): pl.pallas_call(functools.partial(sum_kernel, tuple(sides), tuple(plan), (...  358 us
    all_to_all x1, waiting for transfers between devices, on_device(): lax.all_to_all(found_rows, 'rows', split_axis=0, concat_axis=0, tiled=True)  112 us
    scatter-add x1, other arithmetic, on_device(): jax.ops.segment_sum(arrived.reshape(-1, half_width).astype(f32), requeste...  58.2 us
    dot_general x11, matrix products, dot(): return jnp.dot(left, right, preferred_element_type=f32)  46.8 us
    dot_general x9, matrix products, dot_nt(): lax.dot_general(left, right, (((1,), (1,)), ((), ())), preferred_element_...  44 us
    dot_general x10, matrix products, dot_tn(): lax.dot_general(left, right, (((0,), (0,)), ((), ())), preferred_element_...  43.2 us
    gather x1, local copies, waits for them, and re-layouts, on_device(): found_rows = flat_tables.at[requested].get(mode='promise_in_bounds')  37.1 us
    pallas_call x1, Pallas kernels, spread(): pl.pallas_call(spread_kernel, grid=(count // tile,), in_specs=[pl.BlockSp...  19 us
  transfers between devices with their start and end apart: 29, of which 1 were waited for; matrix products, arithmetic and copies ran while one was open for 32% of the time, Pallas kernels for 47%

profile of v2, /device:TPU:0, one launch (start us, length us, event | category | flops | bytes accessed | tf_op | source)
XLA Modules:
  0.0 913.8 jit_solution(2443017697508374918)
XLA Ops:
  11.3 9.6 %sort.17.cloned.1.call-done = (s32[3,2048]{1,0:T(4,128)}, s32[3,2048]{1,0:T(4,128)}) async-done(((s32[3,2048]{1,0:T(4,128)}, s32[3,2048]{1,0:T(4,128)}), (s32[3,2048]{1,0:T(4,128)}, s32[3,2048]{1,0:T(4,128)})) %sort.17.cloned.1.call-update) | async-done | bytes 49168 | tf_op jit(solution)/shard_map/sort | solution.py:659
  21.7 15.5 %all_to_all.18 = s32[16,1,384]{2,1,0:T(1,128)S(1)} all-to-all(s32[16,1,384]{2,1,0:T(1,128)S(1)} %all_to_all.15), channel_id=1, replica_groups=mesh['section'=2,'rows'=16] {'rows'}, dimensions={0} | all-to-all | bytes 49152 | tf_op jit(solution)/shard_map/all_to_all | solution.py:665
  37.8 37.1 %gather_fusion = bf16[6144,512]{1,0:T(8,128)(2,1)} fusion(bf16[24576,512]{1,0:T(8,128)(2,1)} %bitcast.220, s32[6144]{0:T(1024)S(1)} %broadcast_clamp_fusion), kind=kCustom, calls=%fused_computation | custom fusion | bytes 12607488 | tf_op jit(solution)/shard_map/gather | solution.py:667
  74.8 4.7 all-to-all-start.1
  83.0 112.0 %all-to-all-done.1 = bf16[16,384,512]{2,1,0:T(8,128)(2,1)} async-done(((bf16[16,384,512]{2,1,0:T(8,128)(2,1)}), bf16[16,384,512]{2,1,0:T(8,128)(2,1)}, u32[]{:S(2)}, u32[]{:S(2)}) %all-to-all-start.1) | async-done | bytes 6291488 | tf_op jit(solution)/shard_map/all_to_all | solution.py:668
  195.0 18.5 %combine_rows.1 = bf16[2048,512]{1,0:T(8,128)(2,1)S(1)} custom-call(s32[1,6144]{1,0:T(1,128)S(1)} %broadcast_in_dim_reshape_reshape.6.slots_ref, s32[2048,1]{1,0:T(8,128)S(1)} %bitcast.216, bf16[6144,512]{1,0:T(8,128)(2,1)} %bitcast.13.rows_ref, bf16[384,512]{1,0:T(8,128)(2,1)S(1)} %pad.9.table_ref), custom_call_target="tpu_custom_call" | custom-call | flops 12884901888 | bytes 9437184 | tf_op jit(solution)/shard_map/combine_rows/pallas_call | solution.py:58
  221.0 3.1 broadcast_in_dim_reshape_reshape.8.slots_ref
  224.1 2.4 fusion.67
  231.6 2.6 fusion.65.query_ref
  234.2 7.4 convolution_convert_fusion.5.key_ref.value_ref
  241.6 6.8 patch_attention.1
  250.4 2.8 multiply_reduce_fusion.7
  255.2 6.2 fusion.4
  261.4 2.5 copy-done.10
  265.9 5.4 fusion.80
  271.5 4.8 fusion.22.query_ref.key_ref.value_ref
  276.3 8.9 causal_attention.1
  288.1 10.6 %fusion.6 = f32[256,5632]{1,0:T(8,128)} fusion(bf16[256,1024]{1,0:T(8,128)(2,1)} %multiply_convert_fusion.6, bf16[2,1024,5632]{2,1,0:T(8,128)(2,1)} %all-gather.9.cloned.1.call-done), kind=kOutput, calls=%fused_computation.10 | convolution fusion | flops 2952790016 | bytes 17825792 | tf_op jit(solution)/shard_map/dot_general | solution.py:28
  298.7 5.8 multiply_convert_fusion.2
  304.6 6.8 multiply_reduce_fusion
  311.8 2.5 fusion.63.grad_ref
  314.3 11.4 %causal_attention_back.1 = (bf16[256,1024]{1,0:T(8,128)(2,1)S(1)}, bf16[256,1024]{1,0:T(8,128)(2,1)S(1)}, bf16[256,1024]{1,0:T(8,128)(2,1)S(1)}) custom-call(bf16[256,3072]{1,0:T(8,128)(2,1)S(1)} %fusion.22.query_ref.key_ref.value_ref, bf16[256,3072]{1,0:T(8,128)(2,1)S(1)} %fusion.22.query_ref.key_ref.value_ref, ...), custom_call_target="tpu_custom_call" | custom-call | flops 4000000000 | bytes 4000000 | tf_op jit(solution)/shard_map/causal_attention_back/pallas_call | solution.py:315
  325.9 5.4 fusion.79
  334.5 2.6 fusion.52
  337.2 5.5 multiply_convert_fusion
  342.7 2.6 fusion.50
  345.3 6.2 multiply_reduce_fusion.1
  352.0 2.5 fusion.64.grad_ref
  354.6 8.4 patch_attention_back.1
  363.0 2.6 multiply_reduce_fusion.3
  369.9 6.6 fusion.23
  378.2 2.8 select_bitcast_fusion
  382.2 2.6 constant_dynamic-slice_fusion.6
  388.9 2.3 copy.87
  391.2 2.7 copy.86
  394.9 3.1 convolution_convert_fusion.7
  398.0 3.1 convolution_convert_fusion.6
  403.8 5.1 convolution_convert_fusion.2
  409.4 4.6 convolution_convert_fusion.4
  416.3 2.7 pad_maximum_fusion
  420.0 19.0 %spread_grads.1 = bf16[6144,512]{1,0:T(8,128)(2,1)} custom-call(s32[6144,1]{1,0:T(8,128)S(1)} %broadcast_in_dim_reshape_reshape.8.slots_ref, bf16[2048,512]{1,0:T(8,128)(2,1)S(1)} %maximum_select_fusion.grads_ref), custom_call_target="tpu_custom_call" | custom-call | flops 12884901888 | bytes 9437184 | tf_op jit(solution)/shard_map/spread_grads/pallas_call | solution.py:88
  443.5 7.5 convolution_convert_fusion
  451.1 7.3 convolution_convert_fusion.1
  458.5 7.2 fusion.31
  465.7 2.3 pad_maximum_fusion.1
  468.0 6.5 copy.79
  474.5 357.8 %sum_and_trade.1 = (bf16[64,2816]{1,0:T(8,128)(2,1)}, bf16[64,1408]{1,0:T(8,128)(2,1)}, bf16[64,2048]{1,0:T(8,128)(2,1)}, bf16[64,2816]{1,0:T(8,128)(2,1)}, bf16...) custom-call(bf16[4,2,2,64,2816]{4,3,2,1,0:T(8,128)(2,1)} %bitcast.23, ...), custom_call_target="tpu_custom_call" | custom-call | flops 1000000000 | bytes 600000000 | tf_op jit(solution)/shard_map/sum_and_trade/pallas_call | solution.py:599
  841.5 58.2 %scatter_custom_fusion = f32[24576,512]{1,0:T(8,128)} fusion(s32[6144]{0:T(1024)} %bitcast.239, f32[]{:T(128)} %constant.125.clone.1, bf16[6144,512]{1,0:T(8,128)(2,1)} %bitcast.227), kind=kCustom, calls=%fused_computation.2 | custom fusion | flops 6291456 | bytes 56623616 | tf_op jit(solution)/shard_map/scatter-add | solution.py:797
  (306 shorter events, 72.0 us)
Async XLA Ops:
  8.0 74.3 %copy-start = (s32[2,256]{1,0:T(2,128)S(1)}, s32[2,256]{1,0:T(2,128)}, u32[]{:S(2)}) copy-start(s32[2,256]{1,0:T(2,128)} %param.14) | copy-start | bytes 6148
  8.0 12.9 %sort.17.cloned.1.call-start = ((), (), s32[]{:S(2)}) async-start(), calls=%async_computation.6 | async-start | bytes 196640 | tf_op jit(solution)/shard_map/sort | solution.py:659
  9.5 222.0 %all-gather.5.cloned.1.call-start = ((), (), s32[]{:S(2)}) async-start(), calls=%async_computation.2 | async-start | bytes 18874368 | tf_op jit(solution)/shard_map/all_gather | solution.py:653
  10.1 240.3 %all-gather.7.cloned.1.call-start = ((), (), s32[]{:S(2)}) async-start(), calls=%async_computation.3 | async-start | bytes 6291456 | tf_op jit(solution)/shard_map/all_gather | solution.py:653
  10.7 244.5 %all-gather.9.cloned.1.call-start = ((), (), s32[]{:S(2)}) async-start(), calls=%async_computation.4 | async-start | bytes 34603008 | tf_op jit(solution)/shard_map/all_gather | solution.py:653
  74.8 120.2 %all-to-all-start.1 = ((bf16[16,384,512]{2,1,0:T(8,128)(2,1)}), bf16[16,384,512]{2,1,0:T(8,128)(2,1)}, u32[]{:S(2)}, u32[]{:S(2)}) async-start(bf16[16,384,512]{2,1,0:T(8,128)(2,1)} %bitcast.222), calls=%async_computation.1 | async-start | bytes 12582912 | tf_op jit(solution)/shard_map/all_to_all | solution.py:668
  79.6 186.3 %all-gather.11.cloned.1.call-start = ((), (), s32[]{:S(2)}) async-start(), calls=%async_computation.5 | async-start | bytes 17301504 | tf_op jit(solution)/shard_map/all_gather | solution.py:653
  81.9 142.2 %collective-permute-start.3 = (bf16[256,1024]{1,0:T(8,128)(2,1)}, bf16[256,1024]{1,0:T(8,128)(2,1)}, u32[]{:S(2)}, u32[]{:S(2)}) collective-permute-start(bf16[256,1024]{1,0:T(8,128)(2,1)} %dynamic-slice_bitcast_fusion.1), channel_id=1, source_target_pairs={{0,16},{16,0},{1,17},{17,1},{2,18},{18,2},{3,19},{19,3},{4,20},{20... | collective-permute-start | bytes 1572872 | tf_op jit(solution)/shard_map/ppermute | solution.py:629
  195.0 22.2 %copy-start.63 = (s32[2]{0:T(128)S(1)}, s32[2]{0:T(128)}, u32[]{:S(2)}) copy-start(s32[2]{0:T(128)} %param.15) | copy-start | bytes 28
  195.0 23.4 %copy-start.60 = (bf16[1,2,1024]{2,1,0:T(2,128)(2,1)S(1)}, bf16[1,2,1024]{2,1,0:T(2,128)(2,1)}, u32[]{:S(2)}) copy-start(bf16[1,2,1024]{2,1,0:T(2,128)(2,1)} %param.18) | copy-start | bytes 12292
  215.9 10.6 %collective-permute-start = (bf16[1024,512]{1,0:T(8,128)(2,1)}, bf16[1024,512]{1,0:T(8,128)(2,1)}, u32[]{:S(2)}, u32[]{:S(2)}) collective-permute-start(bf16[1024,512]{1,0:T(8,128)(2,1)} %dynamic-slice_bitcast_fusion), channel_id=1, source_target_pairs={{0,16},{16,0},{1,17},{17,1},{2,18},{18,2},{3,19},{19,3},{4,20},{20... | collective-permute-start | bytes 3145736 | tf_op jit(solution)/shard_map/ppermute | solution.py:629
  231.4 154.1 %collective-permute-start.15 = (bf16[256,1024]{1,0:T(8,128)(2,1)}, bf16[256,1024]{1,0:T(8,128)(2,1)}, u32[]{:S(2)}, u32[]{:S(2)}) collective-permute-start(bf16[256,1024]{1,0:T(8,128)(2,1)} %multiply_convert_fusion.8), channel_id=1, source_target_pairs={{0,16},{16,0},{1,17},{17,1},{2,18},{18,2},{3,19},{19,3},{4,20},{20... | collective-permute-start | bytes 1572872 | tf_op jit(solution)/shard_map/ppermute | solution.py:629
  248.4 137.3 %collective-permute-start.19 = (bf16[256,1024]{1,0:T(8,128)(2,1)}, bf16[256,1024]{1,0:T(8,128)(2,1)}, u32[]{:S(2)}, u32[]{:S(2)}) collective-permute-start(bf16[256,1024]{1,0:T(8,128)(2,1)} %get-tuple-element.28), channel_id=1, source_target_pairs={{0,16},{16,0},{1,17},{17,1},{2,18},{18,2},{3,19},{19,3},{4,20},{20... | collective-permute-start | bytes 1572872 | tf_op jit(solution)/shard_map/ppermute | solution.py:629
  271.3 60.1 %copy-start.34 = (bf16[256,1024]{1,0:T(8,128)(2,1)}, bf16[256,1024]{1,0:T(8,128)(2,1)S(1)}, u32[]{:S(2)}) copy-start(bf16[256,1024]{1,0:T(8,128)(2,1)S(1)} %get-tuple-element.103) | copy-start | bytes 1572868
  276.3 8.9 copy-start.61
  287.1 11.6 %slice-start.2 = ((s8[11534336]{0:T(1024)(128)(4,1)}), s8[4194304]{0:T(1024)(128)(4,1)S(1)}, s32[]{:S(2)}) async-start(s8[11534336]{0:T(1024)(128)(4,1)} %bitcast.273), calls=%async_computation.10 | async-start | bytes 8388608
  288.1 10.6 %copy-start.51 = (bf16[256,1024]{1,0:T(8,128)(2,1)S(1)}, bf16[256,1024]{1,0:T(8,128)(2,1)}, u32[]{:S(2)}) copy-start(bf16[256,1024]{1,0:T(8,128)(2,1)} %get-tuple-element.55) | copy-start | bytes 1572868
  288.1 10.6 %slice-start.3 = ((s8[11534336]{0:T(1024)(128)(4,1)}), s8[4194304]{0:T(1024)(128)(4,1)S(1)}, s32[]{:S(2)}) async-start(s8[11534336]{0:T(1024)(128)(4,1)} %bitcast.273), calls=%async_computation.11 | async-start | bytes 8388608
  288.1 10.6 %slice-start.4 = ((s8[11534336]{0:T(1024)(128)(4,1)}), s8[3145728]{0:T(1024)(128)(4,1)S(1)}, s32[]{:S(2)}) async-start(s8[11534336]{0:T(1024)(128)(4,1)} %bitcast.273), calls=%async_computation.12 | async-start | bytes 6291456
  311.8 14.0 %copy-start.30 = (bf16[256,1024]{1,0:T(8,128)(2,1)}, bf16[256,1024]{1,0:T(8,128)(2,1)S(1)}, u32[]{:S(2)}) copy-start(bf16[256,1024]{1,0:T(8,128)(2,1)S(1)} %fusion.146) | copy-start | bytes 1572868
  325.8 11.4 %slice-start = ((s8[5767168]{0:T(1024)(128)(4,1)}), s8[4194304]{0:T(1024)(128)(4,1)S(1)}, s32[]{:S(2)}) async-start(s8[5767168]{0:T(1024)(128)(4,1)} %bitcast.228), calls=%async_computation.8 | async-start | bytes 8388608
  325.9 11.2 %slice-start.1 = ((s8[5767168]{0:T(1024)(128)(4,1)}), s8[1572864]{0:T(1024)(128)(4,1)S(1)}, s32[]{:S(2)}) async-start(s8[5767168]{0:T(1024)(128)(4,1)} %bitcast.228), calls=%async_computation.9 | async-start | bytes 3145728
  333.2 61.5 %collective-permute-start.13 = (bf16[256,1024]{1,0:T(8,128)(2,1)}, bf16[256,1024]{1,0:T(8,128)(2,1)}, u32[]{:S(2)}, u32[]{:S(2)}) collective-permute-start(bf16[256,1024]{1,0:T(8,128)(2,1)} %get-tuple-element.52), channel_id=1, source_target_pairs={{0,16},{16,0},{1,17},{17,1},{2,18},{18,2},{3,19},{19,3},{4,20},{20... | collective-permute-start | bytes 1572872 | tf_op jit(solution)/shard_map/ppermute | solution.py:629
  352.0 11.1 %copy-start.32 = (bf16[256,1024]{1,0:T(8,128)(2,1)}, bf16[256,1024]{1,0:T(8,128)(2,1)S(1)}, u32[]{:S(2)}) copy-start(bf16[256,1024]{1,0:T(8,128)(2,1)S(1)} %fusion.147) | copy-start | bytes 1572868
  354.6 8.4 copy-start.14
  365.9 21.0 %collective-permute-start.22 = (f32[1024,4]{0,1:T(4,128)S(1)}, f32[1024,4]{0,1:T(4,128)S(1)}, u32[]{:S(2)}, u32[]{:S(2)}) collective-permute-start(f32[1024,4]{0,1:T(4,128)S(1)} %pad_maximum_fusion.7), channel_id=1, source_target_pairs={{0,16},{16,0},{1,17},{17,1},{2,18},{18,2},{3,19},{19,3},{4,20},{20... | collective-permute-start | bytes 49160 | tf_op jit(solution)/shard_map/ppermute | solution.py:629
  366.7 20.3 %collective-permute-start.16 = (bf16[256,512]{1,0:T(8,128)(2,1)S(1)}, bf16[256,512]{1,0:T(8,128)(2,1)S(1)}, u32[]{:S(2)}, u32[]{:S(2)}) collective-permute-start(bf16[256,512]{1,0:T(8,128)(2,1)S(1)} %get-tuple-element.87), channel_id=1, source_target_pairs={{0,16},{16,0},{1,17},{17,1},{2,18},{18,2},{3,19},{19,3},{4,20},{20... | collective-permute-start | bytes 786440 | tf_op jit(solution)/shard_map/ppermute | solution.py:629
  369.7 8.4 slice-start.5
  369.9 8.2 slice-start.6
  369.9 8.2 slice-start.7
  385.5 8.3 collective-permute-start.20
  385.7 15.8 %collective-permute-start.14 = (bf16[256,1408]{1,0:T(8,128)(2,1)}, bf16[256,1408]{1,0:T(8,128)(2,1)}, u32[]{:S(2)}, u32[]{:S(2)}) collective-permute-start(bf16[256,1408]{1,0:T(8,128)(2,1)} %get-tuple-element.81), channel_id=1, source_target_pairs={{0,16},{16,0},{1,17},{17,1},{2,18},{18,2},{3,19},{19,3},{4,20},{20... | collective-permute-start | bytes 2162696 | tf_op jit(solution)/shard_map/ppermute | solution.py:629
  386.9 14.3 %collective-permute-start.9 = (bf16[256,1024]{1,0:T(8,128)(2,1)}, bf16[256,1024]{1,0:T(8,128)(2,1)}, u32[]{:S(2)}, u32[]{:S(2)}) collective-permute-start(bf16[256,1024]{1,0:T(8,128)(2,1)} %causal_attention.1), channel_id=1, source_target_pairs={{0,16},{16,0},{1,17},{17,1},{2,18},{18,2},{3,19},{19,3},{4,20},{20... | collective-permute-start | bytes 1572872 | tf_op jit(solution)/shard_map/ppermute | solution.py:629
  387.1 7.3 collective-permute-start.10
  393.8 15.4 %collective-permute-start.6 = (bf16[256,1408]{1,0:T(8,128)(2,1)}, bf16[256,1408]{1,0:T(8,128)(2,1)}, u32[]{:S(2)}, u32[]{:S(2)}) collective-permute-start(bf16[256,1408]{1,0:T(8,128)(2,1)} %get-tuple-element.83), channel_id=1, source_target_pairs={{0,16},{16,0},{1,17},{17,1},{2,18},{18,2},{3,19},{19,3},{4,20},{20... | collective-permute-start | bytes 2162696 | tf_op jit(solution)/shard_map/ppermute | solution.py:629
  394.4 14.5 %collective-permute-start.5 = (bf16[256,1024]{1,0:T(8,128)(2,1)}, bf16[256,1024]{1,0:T(8,128)(2,1)S(1)}, u32[]{:S(2)}, u32[]{:S(2)}) collective-permute-start(bf16[256,1024]{1,0:T(8,128)(2,1)} %get-tuple-element.55), channel_id=1, source_target_pairs={{0,16},{16,0},{1,17},{17,1},{2,18},{18,2},{3,19},{19,3},{4,20},{20... | collective-permute-start | bytes 1572872 | tf_op jit(solution)/shard_map/ppermute | solution.py:629
  394.7 19.6 %collective-permute-start.8 = (bf16[256,1536]{1,0:T(8,128)(2,1)}, bf16[256,1536]{1,0:T(8,128)(2,1)S(1)}, u32[]{:S(2)}, u32[]{:S(2)}) collective-permute-start(bf16[256,1536]{1,0:T(8,128)(2,1)} %get-tuple-element.79), channel_id=1, source_target_pairs={{0,16},{16,0},{1,17},{17,1},{2,18},{18,2},{3,19},{19,3},{4,20},{20... | collective-permute-start | bytes 2359304 | tf_op jit(solution)/shard_map/ppermute | solution.py:629
  401.1 12.8 %collective-permute-start.7 = (bf16[256,1024]{1,0:T(8,128)(2,1)S(1)}, bf16[256,1024]{1,0:T(8,128)(2,1)S(1)}, u32[]{:S(2)}, u32[]{:S(2)}) collective-permute-start(bf16[256,1024]{1,0:T(8,128)(2,1)S(1)} %copy-done.50), channel_id=1, source_target_pairs={{0,16},{16,0},{1,17},{17,1},{2,18},{18,2},{3,19},{19,3},{4,20},{20... | collective-permute-start | bytes 1572872 | tf_op jit(solution)/shard_map/ppermute | solution.py:629
  401.5 17.5 %collective-permute-start.21 = (bf16[1024,512]{1,0:T(8,128)(2,1)S(1)}, bf16[1024,512]{1,0:T(8,128)(2,1)S(1)}, u32[]{:S(2)}, u32[]{:S(2)}) collective-permute-start(bf16[1024,512]{1,0:T(8,128)(2,1)S(1)} %bitcast.236), channel_id=1, source_target_pairs={{0,16},{16,0},{1,17},{17,1},{2,18},{18,2},{3,19},{19,3},{4,20},{20... | collective-permute-start | bytes 3145736 | tf_op jit(solution)/shard_map/ppermute | solution.py:629
  408.9 33.1 %collective-permute-start.11 = (bf16[256,1024]{1,0:T(8,128)(2,1)}, bf16[256,1024]{1,0:T(8,128)(2,1)}, u32[]{:S(2)}, u32[]{:S(2)}) collective-permute-start(bf16[256,1024]{1,0:T(8,128)(2,1)} %multiply_convert_fusion.7), channel_id=1, source_target_pairs={{0,16},{16,0},{1,17},{17,1},{2,18},{18,2},{3,19},{19,3},{4,20},{20... | collective-permute-start | bytes 1572872 | tf_op jit(solution)/shard_map/ppermute | solution.py:629
  409.2 49.3 %collective-permute-start.17 = (bf16[1024,1024]{1,0:T(8,128)(2,1)}, bf16[1024,1024]{1,0:T(8,128)(2,1)}, u32[]{:S(2)}, u32[]{:S(2)}) collective-permute-start(bf16[1024,1024]{1,0:T(8,128)(2,1)} %pad_maximum_fusion.6), channel_id=1, source_target_pairs={{0,16},{16,0},{1,17},{17,1},{2,18},{18,2},{3,19},{19,3},{4,20},{20... | collective-permute-start | bytes 6291464 | tf_op jit(solution)/shard_map/ppermute | solution.py:629
  414.0 44.5 %collective-permute-start.18 = (bf16[1024,1024]{1,0:T(8,128)(2,1)}, bf16[1024,1024]{1,0:T(8,128)(2,1)}, u32[]{:S(2)}, u32[]{:S(2)}) collective-permute-start(bf16[1024,1024]{1,0:T(8,128)(2,1)} %get-tuple-element.63), channel_id=1, source_target_pairs={{0,16},{16,0},{1,17},{17,1},{2,18},{18,2},{3,19},{19,3},{4,20},{20... | collective-permute-start | bytes 6291464 | tf_op jit(solution)/shard_map/ppermute | solution.py:629
  414.3 28.9 %collective-permute-start.12 = (bf16[256,2816]{1,0:T(8,128)(2,1)}, bf16[256,2816]{1,0:T(8,128)(2,1)}, u32[]{:S(2)}, u32[]{:S(2)}) collective-permute-start(bf16[256,2816]{1,0:T(8,128)(2,1)} %get-tuple-element.67), channel_id=1, source_target_pairs={{0,16},{16,0},{1,17},{17,1},{2,18},{18,2},{3,19},{19,3},{4,20},{20... | collective-permute-start | bytes 4325384 | tf_op jit(solution)/shard_map/ppermute | solution.py:629
  419.0 32.1 %collective-permute-start.4 = (bf16[256,2816]{1,0:T(8,128)(2,1)}, bf16[256,2816]{1,0:T(8,128)(2,1)}, u32[]{:S(2)}, u32[]{:S(2)}) collective-permute-start(bf16[256,2816]{1,0:T(8,128)(2,1)} %get-tuple-element.69), channel_id=1, source_target_pairs={{0,16},{16,0},{1,17},{17,1},{2,18},{18,2},{3,19},{19,3},{4,20},{20... | collective-permute-start | bytes 4325384 | tf_op jit(solution)/shard_map/ppermute | solution.py:629
  420.0 19.0 %copy-start.59 = (s32[1,8,2,128]{3,1,2,0:T(8,128)S(1)}, s32[1,8,2,128]{3,1,2,0:T(8,128)}, u32[]{:S(2)}) copy-start(s32[1,8,2,128]{3,1,2,0:T(8,128)} %copy.93) | copy-start | bytes 24580
  442.0 9.1 collective-permute-start.2
  443.2 394.4 %collective-permute-start.1 = (bf16[256,1024]{1,0:T(8,128)(2,1)}, bf16[256,1024]{1,0:T(8,128)(2,1)S(1)}, u32[]{:S(2)}, u32[]{:S(2)}) collective-permute-start(bf16[256,1024]{1,0:T(8,128)(2,1)} %get-tuple-element.85), channel_id=1, source_target_pairs={{0,16},{16,0},{1,17},{17,1},{2,18},{18,2},{3,19},{19,3},{4,20},{20... | collective-permute-start | bytes 1572872 | tf_op jit(solution)/shard_map/ppermute | solution.py:629
  837.5 62.7 %collective-permute-start.23 = (bf16[64,6272]{1,0:T(8,128)(2,1)S(1)}, bf16[64,6272]{1,0:T(8,128)(2,1)}, u32[]{:S(2)}, u32[]{:S(2)}) collective-permute-start(bf16[64,6272]{1,0:T(8,128)(2,1)S(1)} %broadcast_select_fusion), channel_id=1, source_target_pairs={{0,16},{16,0},{1,17},{17,1},{2,18},{18,2},{3,19},{19,3},{4,20},{20... | collective-permute-start | bytes 2408456 | tf_op jit(solution)/shard_map/ppermute | solution.py:629
  (54 other events, 212.9 us)
Sparse Core Ops, SparseCore 0:
  11.9 8.7 sort.19.cloned.1.call-done
  (1 shorter events, 0.0 us)
Sparse Core Ops, SparseCore 1:
  11.6 27.5 all-gather.4
  40.5 14.7 all-gather.6
  56.7 39.7 all-gather.8
  98.1 24.9 all-gather.10

commit v3 on v1

--- a/solution.py
+++ b/solution.py
@@ -71,34 +71,6 @@
         ),
         name="combine_rows",
     )(slots, ids, rows, table)
-
-
-def spread_kernel(slots_ref, grads_ref, out_ref):
-    positions = grads_ref.shape[0]
-    places = lax.broadcasted_iota(jnp.int32, (out_ref.shape[0], positions), 1)
-    chosen = (places == slots_ref[...]).astype(f32).astype(bf16)
-    out_ref[...] = dot(chosen, grads_ref[...]).astype(bf16)
-
-
-def spread(slots, grads):
-    count = slots.shape[0]
-    positions, width = grads.shape
-    tile = 256
-    return pl.pallas_call(
-        spread_kernel,
-        grid=(count // tile,),
-        in_specs=[
-            pl.BlockSpec((tile, 1), lambda i: (i, 0)),
-            pl.BlockSpec((positions, width), lambda i: (0, 0)),
-        ],
-        out_specs=pl.BlockSpec((tile, width), lambda i: (i, 0)),
-        out_shape=jax.ShapeDtypeStruct((count, width), bf16),
-        compiler_params=params("arbitrary"),
-        cost_estimate=pl.CostEstimate(
-            flops=2 * positions * count * width, bytes_accessed=3 * count * width, transcendentals=0
-        ),
-        name="spread_grads",
-    )(slots, grads)
 
 
 def head_marks(heads, width):
@@ -195,23 +167,23 @@
     attention_ref,
     grad_ref,
     grad_query_ref,
-    grad_key_ref,
-    grad_value_ref,
+    grad_pair_ref,
 ):
     heads, width = attention_ref.shape[0], query_ref.shape[1]
+    first = pl.multiple_of(pl.program_id(0) * width, width)
     marks = head_marks(heads, width)
     by_patch, by_byte = patch_marks(patch_row_ref, patch_col_ref)
     grads = dot(by_byte, grad_ref[...])
     attention = attention_ref[...]
     grad_attention = per_head(marks, grads * value_ref[...].astype(f32))
     weights = dot_tn(attention.astype(bf16), marks)
-    grad_value_ref[...] = (weights * grads).astype(bf16)
+    grad_pair_ref[:, pl.ds(D + first, width)] = (weights * grads).astype(bf16)
     back, ahead = neighbours(patch_row_ref[...], heads)
     terms = attention * grad_attention
     total = scan_sum(terms, back) + scan_sum(terms, ahead) - terms
     grad_scores = (attention * (grad_attention - total)).astype(bf16)
     spread_scores = dot_tn(grad_scores, marks) * 0.125
-    grad_key_ref[...] = (spread_scores * dot(by_byte, query_ref[...])).astype(bf16)
+    grad_pair_ref[:, pl.ds(first, width)] = (spread_scores * dot(by_byte, query_ref[...])).astype(bf16)
     weighted = (spread_scores * key_ref[...].astype(f32)).astype(bf16)
     grad_query_ref[...] = dot(by_patch, weighted).astype(bf16)
 
@@ -232,11 +204,10 @@
             pl.BlockSpec((HEADS // groups, L), lambda i: (i, 0)),
             patch_block,
         ],
-        out_specs=[patch_block, byte_block, byte_block],
+        out_specs=[patch_block, pl.BlockSpec((L, 2 * D), lambda i: (0, 0))],
         out_shape=[
             jax.ShapeDtypeStruct((P_SIZE, D), bf16),
-            jax.ShapeDtypeStruct((L, D), bf16),
-            jax.ShapeDtypeStruct((L, D), bf16),
+            jax.ShapeDtypeStruct((L, 2 * D), bf16),
         ],
         compiler_params=params("arbitrary"),
         cost_estimate=pl.CostEstimate(flops=6 * 10**9, bytes_accessed=10 * 10**6, transcendentals=0),
@@ -288,7 +259,8 @@
     )(mixed, mixed, mixed)
 
 
-def causal_back_kernel(query_ref, key_ref, value_ref, grad_ref, gq_ref, gk_ref, gv_ref):
+def causal_back_kernel(query_ref, key_ref, value_ref, grad_ref, out_ref):
+    pair = pl.program_id(0) * 2 * HEAD
     queries, keys, values, grads = query_ref[...], key_ref[...], value_ref[...], grad_ref[...]
     masks = pair_masks(queries.shape)
     results = []
@@ -304,8 +276,9 @@
                 dot_tn(attention.astype(bf16), grads),
             )
         )
-    for ref, first, second in zip((gq_ref, gk_ref, gv_ref), results[0], results[1]):
-        ref[...] = jnp.where(masks[0], first, second).astype(bf16)
+    for index, (first, second) in enumerate(zip(results[0], results[1])):
+        columns = pl.ds(pl.multiple_of(index * D + pair, 2 * HEAD), 2 * HEAD)
+        out_ref[:, columns] = jnp.where(masks[0], first, second).astype(bf16)
 
 
 def causal_attention_back(mixed, grad_attended):
@@ -320,8 +293,8 @@
             pl.BlockSpec((P_SIZE, 2 * HEAD), lambda i: (0, i + 2 * pairs)),
             block,
         ],
-        out_specs=[block] * 3,
-        out_shape=[jax.ShapeDtypeStruct((P_SIZE, D), bf16)] * 3,
+        out_specs=pl.BlockSpec((P_SIZE, 3 * D), lambda i: (0, 0)),
+        out_shape=jax.ShapeDtypeStruct((P_SIZE, 3 * D), bf16),
         compiler_params=params("arbitrary"),
         cost_estimate=pl.CostEstimate(flops=4 * 10**9, bytes_accessed=4 * 10**6, transcendentals=10**6),
         name="causal_attention_back",
@@ -364,54 +337,511 @@
     return grad_out + grad_in, grad_gain, grad_joined, grad_branch
 
 
-def factors(count):
-    sides = [1, 1, 1]
-    prime = 2
-    while count > 1:
-        while count % prime == 0:
-            sides[sides.index(min(sides))] *= prime
-            count //= prime
-        prime += 1
-    return sides
-
-
-def sum_along(block, sides, kept, which):
-    stride = 1
-    for side in sides[which + 1 :]:
-        stride *= side
-    size = sides[which]
-    if size == 1:
-        return block
-    total = sides[0] * sides[1] * sides[2]
-    place = (lax.axis_index("rows") // stride) % size
-    axis = kept.index(which)
-
-    def part(index):
-        return lax.dynamic_index_in_dim(block, index, axis, keepdims=False)
-
-    result = part(place).astype(f32)
-    for step in range(1, size):
-        route = []
-        for device in range(total):
-            own = (device // stride) % size
-            route.append((device, device + ((own + step) % size - own) * stride))
-        arrived = lax.ppermute(part((place + step) % size), "rows", route)
-        result = result + arrived.astype(f32)
-    return result.astype(bf16)
-
-
-def scatter_sum(block, order):
+def chip_bits(devices):
+    bits = devices.bit_length() - 1
+    first = tuple(reversed(range(bits)))
+    return bits, {"A": first, "B": (first[1], first[0]) + first[2:], "C": first[2:4] + first[:2] + first[4:]}
+
+
+def at_place(ref, axis, place):
+    return ref.at[(slice(None),) * axis + (place,)]
+
+
+def plan_pieces():
+    ff, half = FF // 2, D // 2
+    pieces = []
+    for layer in (1, 0):
+        pieces += [
+            (layer, "A", [("gate_up", 0, ff)]),
+            (layer, "A", [("gate_up", ff, ff)]),
+            (layer, "B", [("down", 0, ff)]),
+            (layer, "B", [("query", 0, half), ("key", 0, half)]),
+            (layer, "C", [("value", 0, half), ("out", 0, half)]),
+        ]
+    return pieces
+
+
+def backward_kernel(devices, table_rows, *refs):
+    bits, orders = chip_bits(devices)
+    half, ff = D // 2, FF // 2
+    rows = D // devices
+    table_block = table_block_rows(devices, table_rows)
+    plan = plan_pieces()
+    extra = len(plan)
+    pieces = extra + 1
+    names = [piece[1] for piece in plan] + ["C"]
+    widths = [sum(width for _, _, width in piece[2]) for piece in plan] + [half]
+
+    layers, refs = {1: refs[:8], 0: refs[8:16]}, refs[16:]
+    bytes_ref, pairs_ref, grad_ref, slots_ref, ids_ref, gains_ref = refs[:6]
+    sums_ref, theirs_ref, gathered_ref, arrived_ref, staged_ref = refs[6:11]
+    refs = refs[11:]
+    landed, refs = {1: refs[:8], 0: refs[8:16]}, refs[16:]
+    bytes_landed, pairs_landed, refs = refs[0], refs[1], refs[2:]
+    owns, refs = refs[:pieces], refs[pieces:]
+    lands, refs = [refs[bits * i : bits * i + bits] for i in range(pieces)], refs[bits * pieces :]
+    left_ref, right_ref, total_ref, send_ref, extra_ref, own_ref, slot_ref, block_ref = refs[:8]
+    swap_send, swap_land, load_sems, grad_sems, slot_sems, block_sems, refs = *refs[8:14], refs[14:]
+    send_sems, land_sems, trade_send, trade_land, spread_send, spread_land, last_sems = refs
+
+    me = lax.axis_index("rows")
+    section = lax.axis_index("section")
+    partner = 1 - section
+    places = [(me // 2 ** (bits - 1 - d)) % 2 for d in range(bits)]
+    peers = [me + (1 - 2 * places[d]) * 2 ** (bits - 1 - d) for d in range(bits)]
+
+    def other(step):
+        return lax.rem(me + step, devices)
+
+    barrier = pltpu.get_barrier_semaphore()
+    mesh_id = pl.DeviceIdType.MESH
+    pl.semaphore_signal(barrier, inc=1, device_id={"section": partner}, device_id_type=mesh_id)
+    for step in range(1, devices):
+        pl.semaphore_signal(barrier, inc=1, device_id={"rows": other(step)}, device_id_type=mesh_id)
+    pl.semaphore_wait(barrier, devices)
+
+    def remote(source, target, send, land, **device):
+        return pltpu.make_async_remote_copy(
+            src_ref=source, dst_ref=target, send_sem=send, recv_sem=land, device_id=device, device_id_type=mesh_id
+        )
+
+    def part_of(array, index, core):
+        size = array.shape[1]
+        if size == 3 * D:
+            first = index * D + core * half
+        elif size == 2 * D:
+            first = index * D + core * half
+        else:
+            first = core * (size // 2)
+            return array.at[:, pl.ds(pl.multiple_of(first, 128), size // 2)]
+        return array.at[:, pl.ds(pl.multiple_of(first, 128), half)]
+
+    swaps = {}
+
+    def swap_of(key, source, target):
+        slot = len(swaps)
+        swaps[key] = remote(source, target, swap_send.at[slot], swap_land.at[slot], section=partner)
+        swaps[key].start()
+
+    def swap_layer(layer, which):
+        for index in which:
+            array, target = layers[layer][index], landed[layer][index]
+            if index < 4:
+                swap_of((layer, index, 0), array, target)
+            else:
+                wide = array.shape[1] // D if index == 4 else 1
+                for part in range(wide):
+                    there = target.at[:, pl.ds(part * half, half)] if index == 4 else target
+                    swap_of((layer, index, part), part_of(array, part, partner), there)
+
+    ready = set()
+
+    def settled(key):
+        if key not in ready:
+            ready.add(key)
+            swaps[key].wait_recv()
+
+    swap_layer(1, (2, 6, 3, 7))
+    own_rows = own_ref.at[pl.ds(pl.multiple_of(section * L, L), L)]
+    swap_of(("grads",), grad_ref.at[:, pl.ds(pl.multiple_of(partner * half, half), half)], own_rows)
+    own_copy = pltpu.make_async_copy(
+        grad_ref.at[:, pl.ds(pl.multiple_of(section * half, half), half)], own_rows, grad_sems
+    )
+    own_copy.start()
+    swap_layer(1, (0, 1, 4, 5))
+    swap_layer(0, (2, 6, 3, 7, 0, 1, 4, 5))
+    swap_of(("bytes",), bytes_ref, bytes_landed)
+    for part in range(2):
+        swap_of(
+            ("pairs", part), part_of(pairs_ref, part, partner), pairs_landed.at[:, pl.ds(part * half, half)]
+        )
+
+    def jobs_of(piece):
+        layer, _, segments = plan[piece]
+        own, land = layers[layer], landed[layer]
+        result, column = [], 0
+        for kind, first, width in segments:
+            if layer == 0 and kind in ("key", "value"):
+                part = 0 if kind == "key" else 1
+                for chunk in range(4):
+                    depth = pl.ds(chunk % 2 * 512, 512)
+                    if chunk < 2:
+                        left, right = bytes_ref, part_of(pairs_ref, part, section)
+                        keys = []
+                    else:
+                        left, right = bytes_landed, pairs_landed.at[:, pl.ds(part * half, half)]
+                        keys = [("bytes",), ("pairs", part)]
+                    copies = [("left", left.at[depth], 0, 512), ("right", right.at[depth], 0, 512)]
+                    result.append((piece, column, width, chunk, 4, keys, copies))
+            else:
+                index, other_index, part = {
+                    "gate_up": (2, 6, 0),
+                    "down": (3, 7, 0),
+                    "query": (0, 4, 0),
+                    "key": (0, 4, 1),
+                    "value": (0, 4, 2),
+                    "out": (1, 5, 0),
+                }[kind]
+                if other_index == 4:
+                    right = part_of(own[4], part, section)
+                    right_landed = land[4].at[:, pl.ds(part * half, half)]
+                elif kind == "gate_up":
+                    start = pl.multiple_of(section * FF + first, 128)
+                    right = own[6].at[:, pl.ds(start, width)]
+                    right_landed = land[6].at[:, pl.ds(first, width)]
+                else:
+                    right, right_landed = part_of(own[other_index], 0, section), land[other_index]
+                copies = [
+                    ("left", own[index], 0, P_SIZE),
+                    ("left", land[index], P_SIZE, P_SIZE),
+                    ("right", right, 0, P_SIZE),
+                    ("right", right_landed, P_SIZE, P_SIZE),
+                ]
+                keys = [(layer, index, 0), (layer, other_index, part)]
+                result.append((piece, column, width, 0, 1, keys, copies))
+            column += width
+        return result
+
+    groups = [[i for i in range(pieces) if names[i] == name] for name in "ABC"]
+    order_made = []
+    for rank in range(max(len(group) for group in groups)):
+        order_made += [group[rank] for group in groups if rank < len(group)]
+    jobs = [job for piece in order_made if piece != extra for job in jobs_of(piece)]
+
+    def loads(number):
+        piece, column, width, chunk, chunks, keys, copies = jobs[number]
+        slot = number % 2
+        result = []
+        for index, (side, source, first, count) in enumerate(copies):
+            buffer = left_ref if side == "left" else right_ref
+            columns = D if side == "left" else width
+            target = buffer.at[slot, pl.ds(first, count), pl.ds(0, columns)]
+            result.append(pltpu.make_async_copy(source, target, load_sems.at[slot, index]))
+        return result
+
+    def start_loads(number):
+        if number < len(jobs):
+            for key in jobs[number][5]:
+                settled(key)
+            for copy in loads(number):
+                copy.start()
+
+    slots_of = {piece: index % send_ref.shape[0] for index, piece in enumerate(order_made) if piece != extra}
+
+    def sent_part(piece):
+        if piece == extra:
+            return extra_ref
+        return send_ref.at[slots_of[piece]].at[(slice(None),) * bits + (pl.ds(0, widths[piece]),)]
+
+    def store(piece, device, value, column, width):
+        axis = orders[names[piece]][0]
+        at = [(device // 2 ** (bits - 1 - d)) % 2 for d in range(bits)]
+        bit = at.pop(axis)
+        at = tuple(at) + (slice(None), pl.ds(column, width))
+        target = sent_part(piece)
+
+        @pl.when(bit == places[axis])
+        def _():
+            owns[piece][at] = value
+
+        @pl.when(bit != places[axis])
+        def _():
+            target[at] = value
+
+    def run_job(number):
+        piece, column, width, chunk, chunks, keys, copies = jobs[number]
+        slot = number % 2
+        for copy in loads(number):
+            copy.wait()
+        start_loads(number + 1)
+        tile = 128
+
+        def body(index, carry):
+            at = pl.ds(pl.multiple_of(index * tile, tile), tile)
+            value = dot_tn(left_ref[slot, :, at], right_ref[slot, :, pl.ds(0, width)])
+            if chunk > 0:
+                value = value + total_ref[at, :]
+            if chunk < chunks - 1:
+                total_ref[at, :] = value
+            else:
+                for part in range(tile // rows):
+                    block = value[part * rows : (part + 1) * rows].astype(bf16)
+                    store(piece, index * (tile // rows) + part, block, column, width)
+            return carry
+
+        lax.fori_loop(0, D // tile, body, 0)
+
+    def left_of(piece, phase):
+        order = orders[names[piece]]
+        return [d for d in range(bits) if d not in order[:phase]]
+
+    def kept(piece, phase):
+        order = orders[names[piece]]
+        ref = owns[piece]
+        for step in range(1, phase):
+            ref = at_place(ref, left_of(piece, step).index(order[step]), places[order[step]])
+        return ref
+
+    def send(piece, phase):
+        axis = orders[names[piece]][phase]
+        if phase == 0:
+            source = sent_part(piece)
+        else:
+            source = at_place(kept(piece, phase), left_of(piece, phase).index(axis), 1 - places[axis])
+        slot = piece * bits + phase
+        return remote(source, lands[piece][phase], send_sems.at[slot], land_sems.at[slot], rows=peers[axis])
+
+    made = [0, 0]
+    sent = set()
+
+    def make(piece):
+        if piece == extra:
+            make_extra()
+        else:
+            index = order_made.index(piece)
+            count = send_ref.shape[0]
+            earlier = [p for p in order_made[:index] if p != extra and slots_of[p] == slots_of[piece]]
+            if earlier and (earlier[-1], 0) not in sent:
+                sent.add((earlier[-1], 0))
+                send(earlier[-1], 0).wait_send()
+            while made[0] < len(jobs) and jobs[made[0]][0] == piece:
+                run_job(made[0])
+                made[0] += 1
+        send(piece, 0).start()
+
+    def make_extra():
+        tile = table_block
+        first_gain = table_rows // 16 * 16
+        positions = M * L
+
+        def body(index, carry):
+            words = index * tile + lax.broadcasted_iota(jnp.int32, (tile, positions), 0)
+            chosen = (words == ids_ref[...]).astype(f32).astype(bf16)
+            value = dot(chosen, own_ref[...])
+            row = index * tile + lax.broadcasted_iota(jnp.int32, (tile, half), 0)
+            gains = jnp.concatenate([gains_ref[...]] * (tile // 16), axis=0)
+            inside = (row >= first_gain) & (row < first_gain + 16)
+            value = value + jnp.where(inside, gains, 0.0)
+            store(extra, index, value.astype(bf16), 0, half)
+            return carry
+
+        lax.fori_loop(0, devices, body, 0)
+
+    def add(piece, phase):
+        target = kept(piece, phase + 1)
+        land = lands[piece][phase]
+        leads = len(target.shape) - 2
+        count = 16
+        groups_in = target.shape[-2] // count
+
+        def body(index, carry):
+            at = (pl.ds(pl.multiple_of(index % groups_in * count, count), count), slice(None))
+            lead = index // groups_in
+            at = tuple((lead // 2 ** (leads - 1 - d)) % 2 for d in range(leads)) + at
+            target[at] = (target[at].astype(f32) + land[at].astype(f32)).astype(bf16)
+            return carry
+
+        lax.fori_loop(0, 2**leads * groups_in, body, 0)
+
+    block_rows = block_ref.shape[1]
+    block_slots = block_ref.shape[0]
+
+    def slot_copy(step):
+        return pltpu.make_async_copy(
+            slots_ref.at[pl.ds(pl.multiple_of(other(step) * block_rows, 16), block_rows)],
+            slot_ref.at[step % 2],
+            slot_sems.at[step % 2],
+        )
+
+    def block_copy(step):
+        target = staged_ref.at[step] if step else arrived_ref.at[me]
+        slot = (step - 1) % devices % block_slots
+        return pltpu.make_async_copy(block_ref.at[slot], target, block_sems.at[slot])
+
+    def trade(step):
+        return remote(
+            staged_ref.at[step], arrived_ref.at[me], trade_send.at[step - 1], trade_land.at[step - 1], rows=other(step)
+        )
+
+    def trade_landing(step):
+        back = lax.rem(me + devices - step, devices)
+        return remote(
+            staged_ref.at[step], arrived_ref.at[back], trade_send.at[step - 1], trade_land.at[step - 1], rows=back
+        )
+
+    def make_blocks():
+        own_copy.wait()
+        settled(("grads",))
+        steps = list(range(1, devices)) + [0]
+        slot_copy(steps[0]).start()
+        behind = block_slots - 1
+
+        def pass_on(step):
+            block_copy(step).wait()
+            if step:
+                trade(step).start()
+
+        for index, step in enumerate(steps):
+            if index + 1 < devices:
+                slot_copy(steps[index + 1]).start()
+            slot_copy(step).wait()
+            if index >= behind:
+                pass_on(steps[index - behind])
+            where = lax.broadcasted_iota(jnp.int32, (block_rows, M * L), 1)
+            chosen = (where == slot_ref[step % 2]).astype(f32).astype(bf16)
+            block_ref[index % block_slots] = dot(chosen, own_ref[...]).astype(bf16)
+            block_copy(step).start()
+        for step in steps[devices - behind :]:
+            pass_on(step)
+
+    def spreads():
+        return [
+            remote(
+                gathered_ref.at[me],
+                gathered_ref.at[me],
+                spread_send.at[step - 1],
+                spread_land.at[step - 1],
+                rows=other(step),
+            )
+            for step in range(1, devices)
+        ]
+
+    def spread_landing(step):
+        back = lax.rem(me + devices - step, devices)
+        return remote(
+            gathered_ref.at[me], gathered_ref.at[back], spread_send.at[step - 1], spread_land.at[step - 1], rows=back
+        )
+
+    def finish(piece):
+        if piece == extra:
+            gathered_ref[me] = kept(piece, bits)[...]
+            for copy in spreads():
+                copy.start()
+        else:
+            layer = plan[piece][0]
+            first = sum(widths[p] for p in range(piece) if plan[p][0] == layer)
+            sums_ref[layer, :, first : first + widths[piece]] = kept(piece, bits)[...]
+
+    start_loads(0)
+    for group in groups:
+        make(group[0])
+    make_blocks()
+    for group in groups:
+        if len(group) > 1:
+            make(group[1])
+    rounds = max(len(group) for group in groups)
+    for turn in range(rounds + bits - 1):
+        for phase in range(bits):
+            for group in groups:
+                if not 0 <= turn - phase < len(group):
+                    continue
+                piece = group[turn - phase]
+                send(piece, phase).wait_recv()
+                if phase == 0 and turn + 2 < len(group):
+                    make(group[turn + 2])
+                add(piece, phase)
+                if phase + 1 < bits:
+                    send(piece, phase + 1).start()
+                else:
+                    finish(piece)
+
+    last = remote(sums_ref.at[partner], theirs_ref, last_sems.at[0], last_sems.at[1], section=partner)
+    last.start()
+    for piece in range(pieces):
+        for phase in range(bits):
+            if (piece, phase) not in sent:
+                send(piece, phase).wait_send()
+    for key, copy in swaps.items():
+        copy.wait_send()
+        settled(key)
+    for step in range(1, devices):
+        trade(step).wait_send()
+    for copy in spreads():
+        copy.wait_send()
+    for step in range(1, devices):
+        trade_landing(step).wait_recv()
+        spread_landing(step).wait_recv()
+    last.wait()
+
+
+def table_block_rows(devices, table_rows):
+    return -(-(table_rows + 12) // (16 * devices)) * 16
+
+
+def backward_sums(layer_two, layer_one, byte_rows, grad_pairs, grad_bytes, slots, ids, gains, table_rows):
     devices = lax.axis_size("rows")
-    sides = factors(devices)
-    kept = [0, 1, 2]
-    block = block.reshape(*sides, block.shape[0] // devices, block.shape[1])
-    for which in order:
-        if sides[which] == 1:
-            block = block.reshape([s for d, s in enumerate(block.shape) if d != kept.index(which)])
-        else:
-            block = sum_along(block, sides, kept, which)
-        kept.remove(which)
-    return block
+    bits, orders = chip_bits(devices)
+    rows = D // devices
+    plan = plan_pieces()
+    table_block = table_block_rows(devices, table_rows)
+    half, ff = D // 2, FF // 2
+    block_rows = slots.shape[0] // devices
+    widths = [sum(width for _, _, width in piece[2]) for piece in plan]
+    shapes = [(rows, width) for width in widths] + [(table_block, half)]
+    owns, lands = [], []
+    for shape in shapes:
+        owns.append(pltpu.VMEM((2,) * (bits - 1) + shape, bf16))
+        lands += [pltpu.VMEM((2,) * (bits - 1 - phase) + shape, bf16) for phase in range(bits)]
+    total = sum(widths) // 2
+    landed = []
+    for layer in (layer_two, layer_one):
+        for index, array in enumerate(layer):
+            shape = array.shape if index < 4 else (array.shape[0], array.shape[1] // 2)
+            landed.append(jax.ShapeDtypeStruct(shape, bf16))
+    landed += [
+        jax.ShapeDtypeStruct(byte_rows.shape, bf16),
+        jax.ShapeDtypeStruct((grad_pairs.shape[0], grad_pairs.shape[1] // 2), bf16),
+    ]
+    swaps = 2 * 7 + 3 + 1 + 4
+    copies = len(shapes) * bits
+    any_space = pl.BlockSpec(memory_space=pl.ANY)
+    vmem = pl.BlockSpec(memory_space=pltpu.VMEM)
+    blocks = jax.ShapeDtypeStruct((devices, block_rows, half), bf16)
+    dma = pltpu.SemaphoreType.DMA
+    results = pl.pallas_call(
+        functools.partial(backward_kernel, devices, table_rows),
+        in_specs=[any_space] * 20 + [vmem] * 2,
+        out_specs=[vmem, any_space, vmem] + [any_space] * (2 + len(landed)),
+        out_shape=[
+            jax.ShapeDtypeStruct((2, rows, total), bf16),
+            jax.ShapeDtypeStruct((rows, total), bf16),
+            jax.ShapeDtypeStruct((devices, table_block, half), bf16),
+            blocks,
+            blocks,
+            *landed,
+        ],
+        scratch_shapes=[
+            *owns,
+            *lands,
+            pltpu.VMEM((2, 2 * P_SIZE, D), bf16),
+            pltpu.VMEM((2, 2 * P_SIZE, ff), bf16),
+            pltpu.VMEM((D, half), f32),
+            pltpu.VMEM((4,) + (2,) * (bits - 1) + (rows, ff), bf16),
+            pltpu.VMEM((2,) * (bits - 1) + (table_block, half), bf16),
+            pltpu.VMEM((M * L, half), bf16),
+            pltpu.VMEM((2, block_rows, 1), jnp.int32),
+            pltpu.VMEM((3, block_rows, half), bf16),
+            dma((swaps,)),
+            dma((swaps,)),
+            dma((2, 4)),
+            dma,
+            dma((2,)),
+            dma((3,)),
+            dma((copies,)),
+            dma((copies,)),
+            dma((devices - 1,)),
+            dma((devices - 1,)),
+            dma((devices - 1,)),
+            dma((devices - 1,)),
+            dma((2,)),
+        ],
+        compiler_params=pltpu.CompilerParams(
+            collective_id=0, has_side_effects=True, vmem_limit_bytes=60 * 1024 * 1024
+        ),
+        cost_estimate=pl.CostEstimate(flops=5 * 10**10, bytes_accessed=6 * 10**8, transcendentals=0),
+        name="backward_sums",
+    )(*layer_two, *layer_one, byte_rows, grad_pairs, grad_bytes, slots, ids, gains)
+    return results[:4]
 
 
 def swap(array):
@@ -453,7 +883,7 @@
     slots = by_owner(order_key % positions).reshape(-1)
     requested = lax.all_to_all(by_owner(grouped), "rows", split_axis=0, concat_axis=0, tiled=True)
     flat_tables = hash_tables.reshape(count_tables * shard_rows, half_width)
-    found_rows = jnp.take(flat_tables, requested, axis=0)
+    found_rows = flat_tables.at[requested].get(mode="promise_in_bounds")
     returned = lax.all_to_all(found_rows, "rows", split_axis=0, concat_axis=0, tiled=True)
 
     gains = both(norm_gains).astype(f32)
@@ -511,97 +941,77 @@
         first_core, jnp.stack([kept_out, sent_out]), jnp.stack([sent_out, kept_out])
     )[None]
 
-    def share(left, right):
-        width = right.shape[1] // 2
-        mine = lax.dynamic_slice_in_dim(right, section * width, width, axis=1)
-        theirs = lax.dynamic_slice_in_dim(right, (1 - section) * width, width, axis=1)
-        lefts = jnp.concatenate([left, swap(left)], axis=0)
-        rights = jnp.concatenate([mine, swap(theirs)], axis=0)
-        return dot_tn(lefts, rights).astype(bf16)
-
     grad_kept = jnp.where(valid, cotangent_two, 0.0)
     grad_middle, gain_two_second, grad_joined, grad_branch = feed_back(
         middle_two, gains[1, 1], gate_up_both[1], down_both[1], kept_two, grad_kept
     )
-    gate_up_two = scatter_sum(share(kept_two[0], grad_joined), (2, 1, 0))
-    down_two = scatter_sum(share(grad_branch, kept_two[3]), (1, 2, 0))
     grad_low = grad_middle.astype(bf16)
+    factors_two = [normed_two, attended_two, kept_two[0], grad_branch, None, grad_low, grad_joined, kept_two[3]]
     grad_attended = dot_nt(grad_low, out_both[1]).astype(bf16)
-    grad_mixed = jnp.concatenate(causal_attention_back(mixed, grad_attended), axis=1)
-    rest_two = scatter_sum(
-        jnp.concatenate([share(normed_two, grad_mixed), share(attended_two, grad_low)], axis=1), (1, 2, 0)
-    )
+    grad_mixed = causal_attention_back(mixed, grad_attended)
     grad_normed = dot_nt(grad_mixed, qkv_both[1])
     grad_in, gain_two_first = normalize_back(inputs_two, gains[1, 0], inverse_two, grad_normed)
     grad_encoded = jnp.where(valid, 0.0, cotangent_two) + grad_middle + grad_in
+
 
     grad_out = cotangent_one + grad_encoded.astype(bf16).astype(f32)
     grad_kept = jnp.where(valid, grad_out, 0.0)
     grad_middle, gain_one_second, grad_joined, grad_branch = feed_back(
         middle_one, gains[0, 1], gate_up_both[0], down_both[0], kept_one, grad_kept
     )
-    gate_up_one = scatter_sum(share(kept_one[0], grad_joined), (2, 1, 0))
-    down_one = scatter_sum(share(grad_branch, kept_one[3]), (1, 2, 0))
     grad_low = grad_middle.astype(bf16)
+    factors_one = [normed_one, attended_one, kept_one[0], grad_branch, None, grad_low, grad_joined, kept_one[3]]
     grad_attended = dot_nt(grad_low, out_both[0]).astype(bf16)
-    grad_queries, grad_keys, grad_values = patch_attention_back(
+    grad_queries, grad_pairs = patch_attention_back(
         patch_row, patch_col, queries_one, byte_pairs, attention_one, grad_attended
     )
-    grad_pairs = jnp.concatenate([grad_keys, grad_values], axis=1)
     grad_normed = dot_nt(grad_queries, qkv_both[0, :, :D])
     grad_in, gain_one_first = normalize_back(pooled, gains[0, 0], inverse_one, grad_normed)
     grad_pooled = jnp.where(valid, 0.0, grad_out) + grad_middle + grad_in
     grad_bytes = dot(member_byte, (grad_pooled / counts).astype(bf16))
     grad_bytes = (grad_bytes + dot_nt(grad_pairs, qkv_both[0, :, D:])).astype(bf16)
 
-    grad_halves = grad_bytes.reshape(L, 2, half_width)
-    kept_grad = lax.dynamic_index_in_dim(grad_halves, section, 1, keepdims=False)
-    sent_grad = swap(lax.dynamic_index_in_dim(grad_halves, 1 - section, 1, keepdims=False))
-    own_grad = jnp.where(
-        first_core,
-        jnp.concatenate([kept_grad, sent_grad], axis=0),
-        jnp.concatenate([sent_grad, kept_grad], axis=0),
+
+    factors_two[4], factors_one[4] = grad_mixed, grad_queries
+    gain_part = jnp.stack([gain_one_first, gain_one_second, gain_two_first, gain_two_second])
+    gain_part = jnp.pad(gain_part.reshape(8, half_width), ((8, 0), (0, 0)))
+    sums, theirs, gathered, arrived = backward_sums(
+        factors_two,
+        factors_one,
+        byte_rows,
+        grad_pairs,
+        grad_bytes,
+        slots[:, None],
+        flat_bytes[None, :],
+        gain_part,
+        table_rows,
     )
-    slot_grads = spread(slots[:, None], own_grad).reshape(devices, -1, half_width)
-    arrived = lax.all_to_all(slot_grads, "rows", split_axis=0, concat_axis=0, tiled=True)
     hash_grad = jax.ops.segment_sum(
         arrived.reshape(-1, half_width).astype(f32),
         requested.reshape(-1),
         num_segments=count_tables * shard_rows,
     ).reshape(count_tables, shard_rows, half_width)
-    words = (flat_bytes[:, None] == jnp.arange(table_rows, dtype=jnp.int32)[None, :]).astype(bf16)
-    byte_table_grad = lax.psum(dot_tn(words, own_grad), "rows")
-
-    rest_one = scatter_sum(
-        jnp.concatenate(
-            [share(normed_one, grad_queries), share(byte_rows, grad_pairs), share(attended_one, grad_low)],
-            axis=1,
-        ),
-        (1, 2, 0),
-    )
-
-    sums_one = jnp.concatenate([gate_up_one, down_one, rest_one], axis=1)
-    sums_two = jnp.concatenate([gate_up_two, down_two, rest_two], axis=1)
-    kept_sums = jnp.where(first_core, sums_one, sums_two)
-    sent_sums = swap(jnp.where(first_core, sums_two, sums_one))
-    lower = jnp.where(first_core, kept_sums, sent_sums).astype(f32)
-    upper = jnp.where(first_core, sent_sums, kept_sums).astype(f32)
-    half_ff = FF // 2
+    gathered = gathered.reshape(-1, half_width)
+    byte_table_grad = gathered[:table_rows].astype(f32)
+    first_gain = table_rows // 16 * 16 + 8
+    gain_sums = gathered[first_gain : first_gain + 8].reshape(2, 2, D)
+    gain_sums = (gain_sums.astype(f32) + swap(gain_sums).astype(f32)).reshape(2, 2, devices, -1)
+    gains_grad = lax.dynamic_index_in_dim(gain_sums, section, 0, keepdims=True)
+    gains_grad = lax.dynamic_index_in_dim(gains_grad, lax.axis_index("rows"), 2, keepdims=False)
+
+    mine = lax.dynamic_index_in_dim(sums, section, 0, keepdims=False)
+    lower = jnp.where(first_core, mine, theirs).astype(f32)
+    upper = jnp.where(first_core, theirs, mine).astype(f32)
+    half, half_ff = D // 2, FF // 2
     gate_up_grad = jnp.concatenate([lower[:, :FF], upper[:, :FF]], axis=1)
     down_grad = jnp.concatenate([lower[:, FF : FF + half_ff], upper[:, FF : FF + half_ff]], axis=1).T
     low_rest, high_rest = lower[:, FF + half_ff :], upper[:, FF + half_ff :]
-    half = D // 2
-    out_grad = jnp.concatenate([low_rest[:, -half:], high_rest[:, -half:]], axis=1)
-    pieces_one = [low_rest[:, :half], high_rest[:, :half], low_rest[:, half : 3 * half], high_rest[:, half : 3 * half]]
-    pieces_two = [low_rest[:, : 3 * half], high_rest[:, : 3 * half]]
-    qkv_grad = jnp.where(
-        first_core, jnp.concatenate(pieces_one, axis=1), jnp.concatenate(pieces_two, axis=1)
-    )
-
-    gain_sums = jnp.stack([gain_one_first, gain_one_second, gain_two_first, gain_two_second])
-    gain_sums = lax.psum_scatter(gain_sums, "rows", scatter_dimension=1, tiled=True)
-    gain_sums = (gain_sums + swap(gain_sums)).reshape(2, 2, -1)
-    gains_grad = lax.dynamic_index_in_dim(gain_sums, section, 0, keepdims=True)
+    columns = []
+    for index in range(4):
+        part = slice(index * half, (index + 1) * half)
+        columns.append(jnp.concatenate([low_rest[:, part], high_rest[:, part]], axis=1))
+    qkv_grad = jnp.concatenate(columns[:3], axis=1)
+    out_grad = columns[3]
 
     return (
         section_out,

time: 1140 us -> 826 us (0.72)
  waiting for transfers between devices: 559 us -> 113 us
  Pallas kernels: 72.9 us -> 413 us
  starting transfers between devices: 93.2 us -> 5.5 us
  local copies, waits for them, and re-layouts: 119 us -> 71.2 us
  matrix products: 135 us -> 96.3 us
  other arithmetic: 114 us -> 80.7 us
    pallas_call x1, Pallas kernels: 18.8 us -> 360 us  [backward_sums(): pl.pallas_call(functools.partial(backward_kernel, devices, table_rows), i...]
    ppermute x30 -> x0, waiting for transfers between devices: 323 us -> none  [sum_along(): arrived = lax.ppermute(part((place + step) % size), 'rows', route)]
    unnamed x7 -> x4, waiting for transfers between devices: 80.9 us -> 2.25 us
    ppermute x30 -> x0, starting transfers between devices: 52.8 us -> none  [sum_along(): arrived = lax.ppermute(part((place + step) % size), 'rows', route)]
    psum x1 -> x0, waiting for transfers between devices: 41.8 us -> none  [on_device(): byte_table_grad = lax.psum(dot_tn(words, own_grad), 'rows')]
    dot_general x10 -> x0, matrix products: 40.4 us -> none  [dot_tn(): lax.dot_general(left, right, (((0,), (0,)), ((), ())), preferred_element_...]
    all_to_all x1 -> x0, starting transfers between devices: 28.8 us -> none  [on_device(): lax.all_to_all(slot_grads, 'rows', split_axis=0, concat_axis=0, tiled=True)]
    dynamic_slice x17 -> x1, local copies, waits for them, and re-layouts: 29.1 us -> 0.57 us  [on_device(): lax.dynamic_index_in_dim(gains_grad, lax.axis_index('rows'), 2, keepdims=...]
  transfers between devices with their start and end apart: 62 -> 9, of which waited for: 19 -> 1; matrix products, arithmetic and copies ran while one was open for 30% -> 17% of each run, Pallas kernels for 6% -> 3%
where the time goes in v3:
time: 826 us; the launch traced here: 815 us
  Pallas kernels  413 us (50%)
  waiting for transfers between devices  113 us (14%)
  matrix products  96.3 us (12%)
  other arithmetic  80.7 us (10%)
  local copies, waits for them, and re-layouts  71.2 us (9%)
  blocking collectives  17.8 us (2%)
  between operations  17 us (2%)
    pallas_call x1, Pallas kernels, backward_sums(): pl.pallas_call(functools.partial(backward_kernel, devices, table_rows), i...  360 us
    all_to_all x1, waiting for transfers between devices, on_device(): lax.all_to_all(found_rows, 'rows', split_axis=0, concat_axis=0, tiled=True)  111 us
    scatter-add x1, other arithmetic, on_device(): jax.ops.segment_sum(arrived.reshape(-1, half_width).astype(f32), requeste...  58.4 us
    dot_general x11, matrix products, dot(): return jnp.dot(left, right, preferred_element_type=f32)  50.1 us
    dot_general x9, matrix products, dot_nt(): lax.dot_general(left, right, (((1,), (1,)), ((), ())), preferred_element_...  46.2 us
    gather x1, local copies, waits for them, and re-layouts, on_device(): found_rows = flat_tables.at[requested].get(mode='promise_in_bounds')  37.1 us
    pallas_call x1, Pallas kernels, combine(): pl.pallas_call(combine_kernel, grid=(positions // tile,), in_specs=[pl.Bl...  18.5 us
  transfers between devices with their start and end apart: 9, of which 1 were waited for; matrix products, arithmetic and copies ran while one was open for 17% of the time, Pallas kernels for 3%

profile of v3, /device:TPU:0, one launch (start us, length us, event | category | flops | bytes accessed | tf_op | source)
XLA Modules:
  0.0 814.7 jit_solution(13789451417615854253)
XLA Ops:
  11.3 9.6 %sort.17.cloned.1.call-done = (s32[3,2048]{1,0:T(4,128)}, s32[3,2048]{1,0:T(4,128)}) async-done(((s32[3,2048]{1,0:T(4,128)}, s32[3,2048]{1,0:T(4,128)}), (s32[3,2048]{1,0:T(4,128)}, s32[3,2048]{1,0:T(4,128)})) %sort.17.cloned.1.call-update) | async-done | bytes 49168 | tf_op jit(solution)/shard_map/sort | solution.py:878
  21.7 15.5 %all_to_all.18 = s32[16,1,384]{2,1,0:T(1,128)S(1)} all-to-all(s32[16,1,384]{2,1,0:T(1,128)S(1)} %all_to_all.15), channel_id=1, replica_groups=mesh['section'=2,'rows'=16] {'rows'}, dimensions={0} | all-to-all | bytes 49152 | tf_op jit(solution)/shard_map/all_to_all | solution.py:884
  37.8 37.1 %gather_fusion = bf16[6144,512]{1,0:T(8,128)(2,1)} fusion(bf16[24576,512]{1,0:T(8,128)(2,1)} %bitcast.200, s32[6144]{0:T(1024)S(1)} %broadcast_clamp_fusion), kind=kCustom, calls=%fused_computation | custom fusion | bytes 12607488 | tf_op jit(solution)/shard_map/gather | solution.py:886
  74.8 4.7 all-to-all-start.1
  84.1 110.9 %all-to-all-done.1 = bf16[16,384,512]{2,1,0:T(8,128)(2,1)} async-done(((bf16[16,384,512]{2,1,0:T(8,128)(2,1)}), bf16[16,384,512]{2,1,0:T(8,128)(2,1)}, u32[]{:S(2)}, u32[]{:S(2)}) %all-to-all-start.1) | async-done | bytes 6291488 | tf_op jit(solution)/shard_map/all_to_all | solution.py:887
  195.7 18.5 %combine_rows.1 = bf16[2048,512]{1,0:T(8,128)(2,1)S(1)} custom-call(s32[1,6144]{1,0:T(1,128)S(1)} %copy-done.2, s32[2048,1]{1,0:T(8,128)S(1)} %bitcast.196, bf16[6144,512]{1,0:T(8,128)(2,1)} %bitcast.13.rows_ref, bf16[384,512]{1,0:T(8,128)(2,1)S(1)} %pad.8.table_ref), custom_call_target="tpu_custom_call" | custom-call | flops 12884901888 | bytes 9437184 | tf_op jit(solution)/shard_map/combine_rows/pallas_call | solution.py:57
  214.2 1.0 dynamic-slice_bitcast_fusion
  215.8 1.2 dynamic_slice.33
  217.0 2.3 all_gather.15
  220.0 4.6 broadcast_in_dim_reshape_reshape.8.refs_19_
  224.7 2.2 fusion.32
  226.9 1.6 bitcast_select_fusion.1
  228.4 1.8 pad_maximum_fusion.2.refs_16_
  230.2 1.7 multiply_reduce_fusion.8
  232.0 1.5 multiply_convert_fusion.8.refs_8_
  233.5 2.5 fusion.30.query_ref
  236.0 7.0 convolution_convert_fusion.key_ref.value_ref
  243.0 6.0 patch_attention.1
  249.0 1.9 copy-done.6
  251.0 2.8 multiply_reduce_fusion.7
  253.8 1.0 copy-done.8
  255.8 6.4 fusion.4
  262.2 2.4 copy-done.14
  264.6 1.9 multiply_convert_fusion.5.refs_15_
  266.6 5.1 fusion.44
  271.9 4.8 fusion.13.query_ref.key_ref.value_ref
  276.7 8.0 causal_attention.1.refs_1_
  285.7 10.6 %fusion.6 = f32[256,5632]{1,0:T(8,128)} fusion(bf16[256,1024]{1,0:T(8,128)(2,1)S(1)} %multiply_convert_fusion.6.refs_2_, bf16[2,1024,5632]{2,1,0:T(8,128)(2,1)} %all-gather.9.cloned.1.call-done), kind=kOutput, calls=%fused_computation.10 | convolution fusion | flops 2952790016 | bytes 17825792 | tf_op jit(solution)/shard_map/dot_general | solution.py:27
  296.4 5.7 multiply_convert_fusion.3
  302.1 7.3 multiply_reduce_fusion
  310.7 2.3 fusion.28.grad_ref
  313.0 11.2 %causal_attention_back.1.refs_4_ = bf16[256,3072]{1,0:T(8,128)(2,1)S(1)} custom-call(bf16[256,3072]{1,0:T(8,128)(2,1)S(1)} %fusion.13.query_ref.key_ref.value_ref, bf16[256,3072]{1,0:T(8,128)(2,1)S(1)} %fusion.13.query_ref.key_ref.value_ref, bf16[256,3072]{1,0:T(8,128)(2,1)S(1)} %fusion.13.query_ref.key_ref.value_ref, bf16[256,1024]{1,0:T(8,128)(2,1)S(1)} %fusion.28.grad_ref), custom_call_target="tpu_custom_call" | custom-call | flops 4000000000 | bytes 4000000 | tf_op jit(solution)/shard_map/causal_attention_back/pallas_call | solution.py:287
  324.3 5.4 fusion.43
  330.7 5.5 multiply_convert_fusion.1
  336.2 1.1 copy-done.33
  337.8 2.7 pad_maximum_fusion
  340.5 7.2 multiply_reduce_fusion.1
  348.9 9.0 %patch_attention_back.1 = (bf16[256,1024]{1,0:T(8,128)(2,1)S(1)}, bf16[1024,2048]{1,0:T(8,128)(2,1)}) custom-call(s32[1,1024]{1,0:T(1,128)S(1)} %bitcast.199, s32[1024,1]{1,0:T(8,128)S(1)} %copy.31.patch_col_ref, bf16[256,1024]{1,0:T(8,128)(2,1)S(1)} %fusion.30.query_ref, bf16[1024,2048]{1,0:T(8,128)(2,1)} %copy-done.6, bf16[1024,2048]{1,0:T(8,128)(2,1)} %copy-done.6, ...), custom_call_target="tpu_custom_call" | custom-call | flops 6000000000 | bytes 10000000 | tf_op jit(solution)/shard_map/patch_attention_back/pallas_call | solution.py:195
  357.9 3.9 multiply_reduce_fusion.2
  362.5 8.2 %fusion.14 = f32[1024,1024]{1,0:T(8,128)S(1)} fusion(bf16[1024,2048]{1,0:T(8,128)(2,1)} %get-tuple-element.23.refs_17_, bf16[2,1024,3072]{2,1,0:T(8,128)(2,1)} %all-gather.5.cloned.1.call-done), kind=kOutput, calls=%fused_computation.24 | convolution fusion | flops 4294967296 | bytes 12582912 | tf_op jit(solution)/shard_map/dot_general | solution.py:31
  370.8 4.0 add_convert_fusion.refs_18_
  374.8 360.4 %backward_sums.1 = (bf16[2,64,6272]{2,1,0:T(8,128)(2,1)}, bf16[64,6272]{1,0:T(8,128)(2,1)}, bf16[16,32,512]{2,1,0:T(8,128)(2,1)}, bf16[16,384,512]{2,1,0:T(8,128...) custom-call(bf16[256,1024]{1,0:T(8,128)(2,1)} %copy-done.36, ...), custom_call_target="tpu_custom_call" | custom-call | flops 49999998976 | bytes 600000000 | tf_op jit(solution)/shard_map/backward_sums/pallas_call | solution.py:801
  735.2 1.6 fusion.48
  738.8 4.4 select_bitcast_fusion
  743.2 0.9 maximum_bitcast_fusion.1
  744.1 1.2 maximum_bitcast_fusion
  746.7 58.4 %scatter_custom_fusion = f32[24576,512]{1,0:T(8,128)} fusion(s32[6144]{0:T(1024)} %bitcast.210, f32[]{:T(128)} %constant.134.clone.1, bf16[6144,512]{1,0:T(8,128)(2,1)} %bitcast.203), kind=kCustom, calls=%fused_computation.2 | custom fusion | flops 6291456 | bytes 56623616 | tf_op jit(solution)/shard_map/scatter-add | solution.py:989
  805.7 1.1 maximum_select_fusion
  (202 shorter events, 21.7 us)
Async XLA Ops:
  8.0 73.9 %copy-start = (s32[2,256]{1,0:T(2,128)S(1)}, s32[2,256]{1,0:T(2,128)}, u32[]{:S(2)}) copy-start(s32[2,256]{1,0:T(2,128)} %param.14) | copy-start | bytes 6148
  8.0 12.9 %sort.17.cloned.1.call-start = ((), (), s32[]{:S(2)}) async-start(), calls=%async_computation.6 | async-start | bytes 196640 | tf_op jit(solution)/shard_map/sort | solution.py:878
  9.5 223.9 %all-gather.5.cloned.1.call-start = ((), (), s32[]{:S(2)}) async-start(), calls=%async_computation.2 | async-start | bytes 18874368 | tf_op jit(solution)/shard_map/all_gather | solution.py:872
  10.1 240.8 %all-gather.7.cloned.1.call-start = ((), (), s32[]{:S(2)}) async-start(), calls=%async_computation.3 | async-start | bytes 6291456 | tf_op jit(solution)/shard_map/all_gather | solution.py:872
  10.7 244.3 %all-gather.9.cloned.1.call-start = ((), (), s32[]{:S(2)}) async-start(), calls=%async_computation.4 | async-start | bytes 34603008 | tf_op jit(solution)/shard_map/all_gather | solution.py:872
  74.8 120.1 %all-to-all-start.1 = ((bf16[16,384,512]{2,1,0:T(8,128)(2,1)}), bf16[16,384,512]{2,1,0:T(8,128)(2,1)}, u32[]{:S(2)}, u32[]{:S(2)}) async-start(bf16[16,384,512]{2,1,0:T(8,128)(2,1)} %bitcast.202), calls=%async_computation.1 | async-start | bytes 12582912 | tf_op jit(solution)/shard_map/all_to_all | solution.py:887
  79.6 187.0 %all-gather.11.cloned.1.call-start = ((), (), s32[]{:S(2)}) async-start(), calls=%async_computation.5 | async-start | bytes 17301504 | tf_op jit(solution)/shard_map/all_gather | solution.py:872
  81.9 142.8 %collective-permute-start.2 = (bf16[256,1024]{1,0:T(8,128)(2,1)}, bf16[256,1024]{1,0:T(8,128)(2,1)}, u32[]{:S(2)}, u32[]{:S(2)}) collective-permute-start(bf16[256,1024]{1,0:T(8,128)(2,1)} %dynamic-slice_bitcast_fusion.1), channel_id=1, source_target_pairs={{0,16},{16,0},{1,17},{17,1},{2,18},{18,2},{3,19},{19,3},{4,20},{20... | collective-permute-start | bytes 1572872 | tf_op jit(solution)/shard_map/ppermute | solution.py:848
  82.3 131.9 %copy-start.48 = (s32[1,1,2,1024]{3,1,2,0:T(1,128)}, s32[1,1,2,1024]{3,1,2,0:T(1,128)S(1)}, u32[]{:S(2)}) copy-start(s32[1,1,2,1024]{3,1,2,0:T(1,128)S(1)} %copy.35) | copy-start | bytes 24580
  83.4 111.5 %copy-start.44 = (s32[16,3,128]{2,1,0:T(4,128)}, s32[16,3,128]{2,1,0:T(4,128)S(1)}, u32[]{:S(2)}) copy-start(s32[16,3,128]{2,1,0:T(4,128)S(1)} %fusion.61) | copy-start | bytes 73732
  195.7 19.6 %copy-start.52 = (s32[2]{0:T(128)S(1)}, s32[2]{0:T(128)}, u32[]{:S(2)}) copy-start(s32[2]{0:T(128)} %slice_reduce_fusion) | copy-start | bytes 28
  215.3 11.6 %collective-permute-start = (bf16[1024,512]{1,0:T(8,128)(2,1)}, bf16[1024,512]{1,0:T(8,128)(2,1)}, u32[]{:S(2)}, u32[]{:S(2)}) collective-permute-start(bf16[1024,512]{1,0:T(8,128)(2,1)} %dynamic-slice_bitcast_fusion), channel_id=1, source_target_pairs={{0,16},{16,0},{1,17},{17,1},{2,18},{18,2},{3,19},{19,3},{4,20},{20... | collective-permute-start | bytes 3145736 | tf_op jit(solution)/shard_map/ppermute | solution.py:848
  226.9 82.6 %copy-start.17 = (bf16[256,1024]{1,0:T(8,128)(2,1)}, bf16[256,1024]{1,0:T(8,128)(2,1)S(1)}, u32[]{:S(2)}) copy-start(bf16[256,1024]{1,0:T(8,128)(2,1)S(1)} %get-tuple-element.40) | copy-start | bytes 1572868
  232.0 4.0 copy-start.22
  233.5 9.5 %copy-start.38 = (bf16[256,1024]{1,0:T(8,128)(2,1)}, bf16[256,1024]{1,0:T(8,128)(2,1)S(1)}, u32[]{:S(2)}) copy-start(bf16[256,1024]{1,0:T(8,128)(2,1)S(1)} %multiply_convert_fusion.8.refs_8_) | copy-start | bytes 1572868
  251.0 4.0 copy-start.3
  271.6 13.0 %copy-start.26 = (bf16[256,1024]{1,0:T(8,128)(2,1)}, bf16[256,1024]{1,0:T(8,128)(2,1)S(1)}, u32[]{:S(2)}) copy-start(bf16[256,1024]{1,0:T(8,128)(2,1)S(1)} %get-tuple-element.67) | copy-start | bytes 1572868
  271.9 4.8 copy-start.36
  276.7 8.0 copy-start.53
  285.5 44.2 %copy-start.12 = (f32[256,1024]{1,0:T(8,128)}, f32[256,1024]{1,0:T(8,128)S(1)}, u32[]{:S(2)}) copy-start(f32[256,1024]{1,0:T(8,128)S(1)} %get-tuple-element.69) | copy-start | bytes 3145732
  285.5 10.9 %slice-start.2 = ((s8[11534336]{0:T(1024)(128)(4,1)}), s8[4194304]{0:T(1024)(128)(4,1)S(1)}, s32[]{:S(2)}) async-start(s8[11534336]{0:T(1024)(128)(4,1)} %bitcast.240), calls=%async_computation.10 | async-start | bytes 8388608
  285.7 10.7 %copy-start.40 = (bf16[256,1024]{1,0:T(8,128)(2,1)}, bf16[256,1024]{1,0:T(8,128)(2,1)S(1)}, u32[]{:S(2)}) copy-start(bf16[256,1024]{1,0:T(8,128)(2,1)S(1)} %multiply_convert_fusion.6.refs_2_) | copy-start | bytes 1572868
  285.7 10.7 %copy-start.37 = (bf16[256,1024]{1,0:T(8,128)(2,1)S(1)}, bf16[256,1024]{1,0:T(8,128)(2,1)}, u32[]{:S(2)}) copy-start(bf16[256,1024]{1,0:T(8,128)(2,1)} %get-tuple-element.39.refs_3_) | copy-start | bytes 1572868
  285.7 10.7 %slice-start.3 = ((s8[11534336]{0:T(1024)(128)(4,1)}), s8[4194304]{0:T(1024)(128)(4,1)S(1)}, s32[]{:S(2)}) async-start(s8[11534336]{0:T(1024)(128)(4,1)} %bitcast.240), calls=%async_computation.11 | async-start | bytes 8388608
  285.7 10.7 %slice-start.4 = ((s8[11534336]{0:T(1024)(128)(4,1)}), s8[3145728]{0:T(1024)(128)(4,1)S(1)}, s32[]{:S(2)}) async-start(s8[11534336]{0:T(1024)(128)(4,1)} %bitcast.240), calls=%async_computation.12 | async-start | bytes 6291456
  302.1 7.3 copy-start.29
  302.1 7.3 copy-start.31
  313.0 11.2 %copy-start.27 = (bf16[256,1024]{1,0:T(8,128)(2,1)S(1)}, bf16[256,1024]{1,0:T(8,128)(2,1)}, u32[]{:S(2)}) copy-start(bf16[256,1024]{1,0:T(8,128)(2,1)} %copy-done.26) | copy-start | bytes 1572868
  313.0 17.6 %slice-start = ((s8[5767168]{0:T(1024)(128)(4,1)}), s8[4194304]{0:T(1024)(128)(4,1)S(1)}, s32[]{:S(2)}) async-start(s8[5767168]{0:T(1024)(128)(4,1)} %bitcast.204), calls=%async_computation.8 | async-start | bytes 8388608
  324.2 5.4 copy-start.7
  324.2 5.5 copy-start.18
  324.2 5.5 copy-start.25
  324.3 6.4 slice-start.1
  330.6 5.6 copy-start.43
  330.6 17.1 %copy-start.15 = (bf16[256,1024]{1,0:T(8,128)(2,1)}, bf16[256,1024]{1,0:T(8,128)(2,1)S(1)}, u32[]{:S(2)}) copy-start(bf16[256,1024]{1,0:T(8,128)(2,1)S(1)} %get-tuple-element.38) | copy-start | bytes 1572868
  330.7 7.1 copy-start.30
  330.7 7.1 copy-start.32
  340.5 7.7 copy-start.54
  348.2 9.8 %copy-start.42 = (bf16[256,1024]{1,0:T(8,128)(2,1)}, bf16[256,1024]{1,0:T(8,128)(2,1)S(1)}, u32[]{:S(2)}) copy-start(bf16[256,1024]{1,0:T(8,128)(2,1)S(1)} %fusion.66.refs_13_) | copy-start | bytes 1572868
  357.9 12.8 %copy-start.4 = (bf16[256,1024]{1,0:T(8,128)(2,1)}, bf16[256,1024]{1,0:T(8,128)(2,1)S(1)}, u32[]{:S(2)}) copy-start(bf16[256,1024]{1,0:T(8,128)(2,1)S(1)} %get-tuple-element.22.refs_12_) | copy-start | bytes 1572868
  362.5 8.2 %copy-start.11 = (f32[256,1024]{1,0:T(8,128)S(1)}, f32[256,1024]{1,0:T(8,128)}, u32[]{:S(2)}) copy-start(f32[256,1024]{1,0:T(8,128)} %copy-done.8) | copy-start | bytes 3145732
  362.5 8.2 %copy-start.16 = (bf16[256,1024]{1,0:T(8,128)(2,1)S(1)}, bf16[256,1024]{1,0:T(8,128)(2,1)}, u32[]{:S(2)}) copy-start(bf16[256,1024]{1,0:T(8,128)(2,1)} %copy-done.15) | copy-start | bytes 1572868
  362.5 8.2 %copy-start.20 = (f32[256,1024]{1,0:T(8,128)S(1)}, f32[256,1024]{1,0:T(8,128)}, u32[]{:S(2)}) copy-start(f32[256,1024]{1,0:T(8,128)} %copy-done.19) | copy-start | bytes 3145732
  362.5 8.3 %copy-start.35 = (f32[256,1024]{1,0:T(8,128)S(1)}, f32[256,1024]{1,0:T(8,128)}, u32[]{:S(2)}) copy-start(f32[256,1024]{1,0:T(8,128)} %get-tuple-element.73) | copy-start | bytes 3145732
  743.2 62.6 %collective-permute-start.1 = (bf16[256,1024]{1,0:T(8,128)(2,1)S(1)}, bf16[256,1024]{1,0:T(8,128)(2,1)S(1)}, u32[]{:S(2)}, u32[]{:S(2)}) collective-permute-start(bf16[256,1024]{1,0:T(8,128)(2,1)S(1)} %get-tuple-element.55), channel_id=1, source_target_pairs={{0,16},{16,0},{1,17},{17,1},{2,18},{18,2},{3,19},{19,3},{4,20},{20... | collective-permute-start | bytes 1572872 | tf_op jit(solution)/shard_map/ppermute | solution.py:848
  745.4 59.7 %copy-start.50 = (f32[64,3072]{1,0:T(8,128)}, f32[64,3072]{1,0:T(8,128)S(1)}, u32[]{:S(2)}) copy-start(f32[64,3072]{1,0:T(8,128)S(1)} %get-tuple-element.53) | copy-start | bytes 2359300
  745.4 59.7 %collective-permute-start.3 = (bf16[2,2,1024]{2,1,0:T(2,128)(2,1)S(1)}, bf16[2,2,1024]{2,1,0:T(2,128)(2,1)S(1)}, u32[]{:S(2)}, u32[]{:S(2)}) collective-permute-start(bf16[2,2,1024]{2,1,0:T(2,128)(2,1)S(1)} %reshape.272), channel_id=1, source_target_pairs={{0,16},{16,0},{1,17},{17,1},{2,18},{18,2},{3,19},{19,3},{4,20},{20... | collective-permute-start | bytes 24584 | tf_op jit(solution)/shard_map/ppermute | solution.py:848
  746.7 60.2 %copy-start.1 = (s32[2,256]{1,0:T(2,128)S(1)}, s32[2,256]{1,0:T(2,128)}, u32[]{:S(2)}) copy-start(s32[2,256]{1,0:T(2,128)} %param.14) | copy-start | bytes 6148
  (23 other events, 43.0 us)
Sparse Core Ops, SparseCore 0:
  11.9 8.7 sort.19.cloned.1.call-done
  (1 shorter events, 0.0 us)
Sparse Core Ops, SparseCore 1:
  11.6 27.5 all-gather.4
  40.5 14.7 all-gather.6
  56.7 39.7 all-gather.8
  98.1 24.9 all-gather.10

commit v4 on v3

--- a/solution.py
+++ b/solution.py
@@ -17,6 +17,7 @@
 P_SIZE = 256
 GROUP = 512
 VMEM_BYTES = 48 * 1024 * 1024
+SORT_TURN = 3
 
 epsilon = 1e-05
 f32 = jnp.float32
@@ -39,38 +40,232 @@
     return pltpu.CompilerParams(vmem_limit_bytes=VMEM_BYTES, dimension_semantics=semantics)
 
 
-def combine_kernel(slots_ref, ids_ref, rows_ref, table_ref, out_ref):
-    tile = out_ref.shape[0]
-    first = pl.program_id(0) * tile
-    places = first + lax.broadcasted_iota(jnp.int32, (tile, slots_ref.shape[1]), 0)
-    chosen = (places == slots_ref[...]).astype(f32).astype(bf16)
-    words = lax.broadcasted_iota(jnp.int32, (tile, table_ref.shape[0]), 1)
-    word = (words == ids_ref[...]).astype(f32).astype(bf16)
-    total = dot(chosen, rows_ref[...]) + dot(word, table_ref[...])
-    out_ref[...] = total.astype(bf16)
-
-
-def combine(slots, ids, rows, table):
-    count, width = rows.shape
-    positions = ids.shape[0]
-    tile = 256
+def as_column(row):
+    shape = (row.shape[1], row.shape[1])
+    same = lax.broadcasted_iota(jnp.int32, shape, 0) == lax.broadcasted_iota(jnp.int32, shape, 1)
+    return jnp.sum(jnp.where(same, jnp.broadcast_to(row, shape), 0), axis=1, keepdims=True)
+
+
+def gather_kernel(devices, *refs):
+    requests_ref, tables_ref, slots_ref, ids_ref, bytes_ref = refs[:5]
+    weights, refs = refs[5:9], refs[9:]
+    out_ref, requested_ref = refs[:2]
+    layers, refs = refs[2:6], refs[6:]
+    held_ref, staged_ref, landed_ref, part_ref, total_ref, mine_ref, theirs_ref = refs[:7]
+    load_sems, ask_send, ask_land, send_sems, land_sems, last_sems = refs[7:13]
+    weight_send, weight_land = refs[13:]
+    count_tables, shard_rows, half = tables_ref.shape
+    each = requests_ref.shape[2]
+    bits = devices.bit_length() - 1
+
+    me = lax.axis_index("rows")
+    section = lax.axis_index("section")
+    partner = 1 - section
+    mesh_id = pl.DeviceIdType.MESH
+    places = [(me // 2**d) % 2 for d in range(bits)]
+
+    def across(step):
+        device = me
+        for d in range(bits):
+            if step // 2**d % 2:
+                device = device + (1 - 2 * places[d]) * 2**d
+        return device
+
+    steps = [0]
+    for d in range(bits):
+        steps = list(range(2**d, 2 ** (d + 1))) + steps
+
+    def load(table):
+        return pltpu.make_async_copy(tables_ref.at[table], held_ref.at[table], load_sems.at[table])
+
+    for table in range(count_tables):
+        load(table).start()
+
+    barrier = pltpu.get_barrier_semaphore()
+    pl.semaphore_signal(barrier, inc=1, device_id={"section": partner}, device_id_type=mesh_id)
+    for step in range(1, devices):
+        pl.semaphore_signal(barrier, inc=1, device_id={"rows": across(step)}, device_id_type=mesh_id)
+    pl.semaphore_wait(barrier, devices)
+
+    def remote(source, target, send, land, **device):
+        return pltpu.make_async_remote_copy(
+            src_ref=source, dst_ref=target, send_sem=send, recv_sem=land, device_id=device, device_id_type=mesh_id
+        )
+
+    def ask(step):
+        return remote(
+            requests_ref.at[across(step)],
+            requested_ref.at[me],
+            ask_send.at[step - 1],
+            ask_land.at[step - 1],
+            rows=across(step),
+        )
+
+    def asked(step):
+        return remote(
+            requests_ref.at[across(step)],
+            requested_ref.at[across(step)],
+            ask_send.at[step - 1],
+            ask_land.at[step - 1],
+            rows=across(step),
+        )
+
+    for step in range(1, devices):
+        ask(step).start()
+    requested_ref[me] = requests_ref[me]
+
+    def shared(index):
+        return remote(
+            weights[index],
+            layers[index],
+            weight_send.at[index],
+            weight_land.at[index],
+            section=partner,
+        )
+
+    tile = 512
+    def own_row(index, carry):
+        at = pl.ds(pl.multiple_of(index * tile, tile), tile)
+        words = lax.broadcasted_iota(jnp.int32, (tile, bytes_ref.shape[0]), 1)
+        word = (words == ids_ref[at, :]).astype(f32).astype(bf16)
+        total_ref[at, :] = dot(word, bytes_ref[...])
+        return carry
+
+    lax.fori_loop(0, M * L // tile, own_row, 0)
+    for step in range(1, devices):
+        asked(step).wait_recv()
+
+    groups = 4
+    size = devices // groups
+
+    def send(position, table):
+        step = steps[position]
+        slot = position * count_tables + table
+        return remote(
+            staged_ref.at[table, position],
+            landed_ref.at[table, position],
+            send_sems.at[slot],
+            land_sems.at[slot],
+            rows=across(step),
+        )
+
+    def find(table, group):
+        positions = range(group * size, (group + 1) * size)
+        ids = jnp.concatenate(
+            [as_column(requested_ref[across(steps[p]), table : table + 1, :]) for p in positions], axis=0
+        )
+        depth = 1024
+        part_ref[...] = jnp.zeros_like(part_ref)
+
+        def body(index, carry):
+            first = pl.multiple_of(index * depth, depth)
+            places_in = first + lax.broadcasted_iota(jnp.int32, (size * each, depth), 1)
+            chosen = (places_in == ids).astype(f32).astype(bf16)
+            part_ref[...] += dot(chosen, held_ref[table, pl.ds(first, depth), :])
+            return carry
+
+        lax.fori_loop(0, shard_rows // depth, body, 0)
+        for index, position in enumerate(positions):
+            block = part_ref[index * each : (index + 1) * each, :].astype(bf16)
+            if steps[position]:
+                staged_ref[table, position] = block
+                send(position, table).start()
+            else:
+                landed_ref[table, position] = block
+
+    def combine(table, group):
+        positions = range(group * size, (group + 1) * size)
+        for position in positions:
+            if steps[position]:
+                send(position, table).wait_recv()
+        rows = landed_ref[table, group * size : (group + 1) * size].reshape(size * each, half)
+        slots = jnp.concatenate(
+            [slots_ref[across(steps[p]), table : table + 1, :] for p in positions], axis=1
+        )
+
+        def body(index, carry):
+            at = pl.ds(pl.multiple_of(index * tile, tile), tile)
+            places_in = index * tile + lax.broadcasted_iota(jnp.int32, (tile, size * each), 0)
+            chosen = (places_in == slots).astype(f32).astype(bf16)
+            total_ref[at, :] += dot(chosen, rows)
+            return carry
+
+        lax.fori_loop(0, M * L // tile, body, 0)
+
+    for index in range(len(weights)):
+        shared(index).start()
+    far, near = (0, 1), (2, 3)
+    for table in range(count_tables):
+        load(table).wait()
+        for group in far:
+            find(table, group)
+    for table in range(count_tables):
+        for group in near:
+            find(table, group)
+    for table in range(count_tables):
+        for group in near:
+            combine(table, group)
+    for table in range(count_tables):
+        for group in far:
+            combine(table, group)
+
+    theirs_ref[...] = total_ref[pl.ds(pl.multiple_of(partner * L, L), L), :].astype(bf16)
+    mine = out_ref.at[:, pl.ds(pl.multiple_of(section * half, half), half)]
+    last = remote(theirs_ref, mine, last_sems.at[0], last_sems.at[1], section=partner)
+    last.start()
+    mine_ref[...] = total_ref[pl.ds(pl.multiple_of(section * L, L), L), :].astype(bf16)
+    own = pltpu.make_async_copy(mine_ref, mine, last_sems.at[2])
+    own.start()
+    for step in range(1, devices):
+        ask(step).wait_send()
+    for position in range(devices):
+        for table in range(count_tables):
+            if steps[position]:
+                send(position, table).wait_send()
+    for index in range(len(weights)):
+        shared(index).wait()
+    own.wait()
+    last.wait()
+
+
+def gather_rows(requests, tables, slots, ids, table, weights):
+    devices, count_tables, each = requests.shape
+    half = tables.shape[2]
+    vmem = pl.BlockSpec(memory_space=pltpu.VMEM)
+    any_space = pl.BlockSpec(memory_space=pl.ANY)
+    dma = pltpu.SemaphoreType.DMA
+    blocks = (count_tables, devices, each, half)
     return pl.pallas_call(
-        combine_kernel,
-        grid=(positions // tile,),
-        in_specs=[
-            pl.BlockSpec((1, count), lambda i: (0, 0)),
-            pl.BlockSpec((tile, 1), lambda i: (i, 0)),
-            pl.BlockSpec((count, width), lambda i: (0, 0)),
-            pl.BlockSpec(table.shape, lambda i: (0, 0)),
+        functools.partial(gather_kernel, devices),
+        in_specs=[vmem, any_space, vmem, vmem, vmem] + [any_space] * len(weights),
+        out_specs=[vmem, vmem] + [any_space] * len(weights),
+        out_shape=[
+            jax.ShapeDtypeStruct((L, 2 * half), bf16),
+            jax.ShapeDtypeStruct(requests.shape, jnp.int32),
+            *[jax.ShapeDtypeStruct(weight.shape, weight.dtype) for weight in weights],
         ],
-        out_specs=pl.BlockSpec((tile, width), lambda i: (i, 0)),
-        out_shape=jax.ShapeDtypeStruct((positions, width), bf16),
-        compiler_params=params("arbitrary"),
-        cost_estimate=pl.CostEstimate(
-            flops=2 * positions * count * width, bytes_accessed=12 * count * width // 4, transcendentals=0
+        scratch_shapes=[
+            pltpu.VMEM(tables.shape, bf16),
+            pltpu.VMEM(blocks, bf16),
+            pltpu.VMEM(blocks, bf16),
+            pltpu.VMEM((devices // 4 * each, half), f32),
+            pltpu.VMEM((M * L, half), f32),
+            pltpu.VMEM((L, half), bf16),
+            pltpu.VMEM((L, half), bf16),
+            dma((count_tables,)),
+            dma((devices - 1,)),
+            dma((devices - 1,)),
+            dma((devices * count_tables,)),
+            dma((devices * count_tables,)),
+            dma((3,)),
+            *[dma((len(weights),))] * 2,
+        ],
+        compiler_params=pltpu.CompilerParams(
+            collective_id=1, has_side_effects=True, vmem_limit_bytes=56 * 1024 * 1024
         ),
-        name="combine_rows",
-    )(slots, ids, rows, table)
+        cost_estimate=pl.CostEstimate(flops=5 * 10**10, bytes_accessed=4 * 10**8, transcendentals=0),
+        name="gather_rows",
+    )(requests, tables, slots, ids, table, *weights)
 
 
 def head_marks(heads, width):
@@ -361,7 +556,7 @@
     return pieces
 
 
-def backward_kernel(devices, table_rows, *refs):
+def backward_kernel(devices, table_rows, count_tables, *refs):
     bits, orders = chip_bits(devices)
     half, ff = D // 2, FF // 2
     rows = D // devices
@@ -373,15 +568,15 @@
     widths = [sum(width for _, _, width in piece[2]) for piece in plan] + [half]
 
     layers, refs = {1: refs[:8], 0: refs[8:16]}, refs[16:]
-    bytes_ref, pairs_ref, grad_ref, slots_ref, ids_ref, gains_ref = refs[:6]
-    sums_ref, theirs_ref, gathered_ref, arrived_ref, staged_ref = refs[6:11]
-    refs = refs[11:]
+    bytes_ref, pairs_ref, grad_ref, slots_ref, places_ref, ids_ref, gains_ref = refs[:7]
+    sums_ref, theirs_ref, gathered_ref, sorted_ref, arrived_ref, staged_ref = refs[7:13]
+    refs = refs[13:]
     landed, refs = {1: refs[:8], 0: refs[8:16]}, refs[16:]
     bytes_landed, pairs_landed, refs = refs[0], refs[1], refs[2:]
     owns, refs = refs[:pieces], refs[pieces:]
     lands, refs = [refs[bits * i : bits * i + bits] for i in range(pieces)], refs[bits * pieces :]
-    left_ref, right_ref, total_ref, send_ref, extra_ref, own_ref, slot_ref, block_ref = refs[:8]
-    swap_send, swap_land, load_sems, grad_sems, slot_sems, block_sems, refs = *refs[8:14], refs[14:]
+    left_ref, right_ref, total_ref, send_ref, extra_ref, own_ref, table_ref, tile_ref, block_ref = refs[:9]
+    swap_send, swap_land, load_sems, grad_sems, table_sem, tile_sems, block_sems, refs = *refs[9:16], refs[16:]
     send_sems, land_sems, trade_send, trade_land, spread_send, spread_land, last_sems = refs
 
     me = lax.axis_index("rows")
@@ -646,13 +841,6 @@
     block_rows = block_ref.shape[1]
     block_slots = block_ref.shape[0]
 
-    def slot_copy(step):
-        return pltpu.make_async_copy(
-            slots_ref.at[pl.ds(pl.multiple_of(other(step) * block_rows, 16), block_rows)],
-            slot_ref.at[step % 2],
-            slot_sems.at[step % 2],
-        )
-
     def block_copy(step):
         target = staged_ref.at[step] if step else arrived_ref.at[me]
         slot = (step - 1) % devices % block_slots
@@ -669,30 +857,63 @@
             staged_ref.at[step], arrived_ref.at[back], trade_send.at[step - 1], trade_land.at[step - 1], rows=back
         )
 
+    own_block = block_copy(0)
+
     def make_blocks():
         own_copy.wait()
         settled(("grads",))
         steps = list(range(1, devices)) + [0]
-        slot_copy(steps[0]).start()
         behind = block_slots - 1
 
         def pass_on(step):
-            block_copy(step).wait()
             if step:
+                block_copy(step).wait()
                 trade(step).start()
 
         for index, step in enumerate(steps):
-            if index + 1 < devices:
-                slot_copy(steps[index + 1]).start()
-            slot_copy(step).wait()
             if index >= behind:
                 pass_on(steps[index - behind])
-            where = lax.broadcasted_iota(jnp.int32, (block_rows, M * L), 1)
-            chosen = (where == slot_ref[step % 2]).astype(f32).astype(bf16)
-            block_ref[index % block_slots] = dot(chosen, own_ref[...]).astype(bf16)
+            each = block_rows // count_tables
+            where = lax.broadcasted_iota(jnp.int32, (each, M * L), 1)
+            for table in range(count_tables):
+                slot = as_column(slots_ref[other(step), table : table + 1, :])
+                chosen = (where == slot).astype(f32).astype(bf16)
+                part = pl.ds(table * each, each)
+                block_ref[index % block_slots, part] = dot(chosen, own_ref[...]).astype(bf16)
             block_copy(step).start()
         for step in steps[devices - behind :]:
             pass_on(step)
+
+
+    def tile_copy(table, index):
+        tile = tile_ref.shape[1]
+        return pltpu.make_async_copy(
+            tile_ref.at[index % 2],
+            sorted_ref.at[table, pl.ds(pl.multiple_of(index * tile, tile), tile)],
+            tile_sems.at[index % 2],
+        )
+
+    def sort_rows(table):
+        if table == 0:
+            own_block.wait()
+            for step in range(1, devices):
+                trade_landing(step).wait_recv()
+        each = block_rows // count_tables
+        copy = pltpu.make_async_copy(arrived_ref.at[:, pl.ds(table * each, each)], table_ref, table_sem)
+        copy.start()
+        copy.wait()
+        tile = tile_ref.shape[1]
+        for index in range(M * L // tile):
+            if index >= 2:
+                tile_copy(table, index - 2).wait()
+            place = lax.broadcasted_iota(jnp.int32, (tile, M * L), 1)
+            wanted = as_column(places_ref[table, :, index * tile : (index + 1) * tile])
+            chosen = (place == wanted).astype(f32).astype(bf16)
+            rows_in = table_ref[...].reshape(M * L, half)
+            tile_ref[index % 2] = dot(chosen, rows_in).astype(bf16)
+            tile_copy(table, index).start()
+        for index in range(M * L // tile - 2, M * L // tile):
+            tile_copy(table, index).wait()
 
     def spreads():
         return [
@@ -744,6 +965,8 @@
                     send(piece, phase + 1).start()
                 else:
                     finish(piece)
+        if 0 <= turn - SORT_TURN < count_tables:
+            sort_rows(turn - SORT_TURN)
 
     last = remote(sums_ref.at[partner], theirs_ref, last_sems.at[0], last_sems.at[1], section=partner)
     last.start()
@@ -759,23 +982,63 @@
     for copy in spreads():
         copy.wait_send()
     for step in range(1, devices):
-        trade_landing(step).wait_recv()
         spread_landing(step).wait_recv()
     last.wait()
 
 
+def place_kernel(starts_ref, ids_ref, rows_ref, out_ref):
+    table, tile = pl.program_id(0), pl.program_id(1)
+    height, window = out_ref.shape[1], 256
+    at = table * (pl.num_programs(1) + 1) + tile
+    places = tile * height + lax.broadcasted_iota(jnp.int32, (height, window), 0)
+    out_ref[...] = jnp.zeros(out_ref.shape, f32)
+
+    def body(index, carry):
+        part = pl.ds(pl.multiple_of(index * window, window), window)
+        chosen = (places == ids_ref[0, :, part]).astype(f32).astype(bf16)
+        out_ref[0] += dot(chosen, rows_ref[0, part, :])
+        return carry
+
+    lax.fori_loop(starts_ref[at] // window, (starts_ref[at + 1] + window - 1) // window, body, 0)
+
+
+def place_rows(ids, rows, shard_rows):
+    count_tables, count, width = rows.shape
+    height = 1024
+    tiles = shard_rows // height
+    edges = jnp.arange(tiles + 1, dtype=jnp.int32) * height
+    starts = jnp.sum((ids[:, None, :] < edges[None, :, None]).astype(jnp.int32), axis=2).reshape(-1)
+    return pl.pallas_call(
+        place_kernel,
+        grid_spec=pltpu.PrefetchScalarGridSpec(
+            num_scalar_prefetch=1,
+            grid=(count_tables, tiles),
+            in_specs=[
+                pl.BlockSpec((1, 1, count), lambda i, j, starts: (i, 0, 0)),
+                pl.BlockSpec((1, count, width), lambda i, j, starts: (i, 0, 0)),
+            ],
+            out_specs=pl.BlockSpec((1, height, width), lambda i, j, starts: (i, j, 0)),
+        ),
+        out_shape=jax.ShapeDtypeStruct((count_tables, shard_rows, width), f32),
+        compiler_params=params("arbitrary", "arbitrary"),
+        cost_estimate=pl.CostEstimate(flops=10**10, bytes_accessed=6 * 10**7, transcendentals=0),
+        name="place_rows",
+    )(starts, ids[:, None, :], rows)
+
+
 def table_block_rows(devices, table_rows):
     return -(-(table_rows + 12) // (16 * devices)) * 16
 
 
-def backward_sums(layer_two, layer_one, byte_rows, grad_pairs, grad_bytes, slots, ids, gains, table_rows):
+def backward_sums(layer_two, layer_one, byte_rows, grad_pairs, grad_bytes, slots, places, ids, gains, table_rows):
     devices = lax.axis_size("rows")
     bits, orders = chip_bits(devices)
     rows = D // devices
     plan = plan_pieces()
     table_block = table_block_rows(devices, table_rows)
     half, ff = D // 2, FF // 2
-    block_rows = slots.shape[0] // devices
+    count_tables, each = slots.shape[1:]
+    block_rows = count_tables * each
     widths = [sum(width for _, _, width in piece[2]) for piece in plan]
     shapes = [(rows, width) for width in widths] + [(table_block, half)]
     owns, lands = [], []
@@ -799,13 +1062,14 @@
     blocks = jax.ShapeDtypeStruct((devices, block_rows, half), bf16)
     dma = pltpu.SemaphoreType.DMA
     results = pl.pallas_call(
-        functools.partial(backward_kernel, devices, table_rows),
-        in_specs=[any_space] * 20 + [vmem] * 2,
-        out_specs=[vmem, any_space, vmem] + [any_space] * (2 + len(landed)),
+        functools.partial(backward_kernel, devices, table_rows, count_tables),
+        in_specs=[any_space] * 19 + [vmem] * 4,
+        out_specs=[vmem, any_space, vmem] + [any_space] * (3 + len(landed)),
         out_shape=[
             jax.ShapeDtypeStruct((2, rows, total), bf16),
             jax.ShapeDtypeStruct((rows, total), bf16),
             jax.ShapeDtypeStruct((devices, table_block, half), bf16),
+            jax.ShapeDtypeStruct((count_tables, M * L, half), bf16),
             blocks,
             blocks,
             *landed,
@@ -819,11 +1083,13 @@
             pltpu.VMEM((4,) + (2,) * (bits - 1) + (rows, ff), bf16),
             pltpu.VMEM((2,) * (bits - 1) + (table_block, half), bf16),
             pltpu.VMEM((M * L, half), bf16),
-            pltpu.VMEM((2, block_rows, 1), jnp.int32),
+            pltpu.VMEM((devices, each, half), bf16),
+            pltpu.VMEM((2, 256, half), bf16),
             pltpu.VMEM((3, block_rows, half), bf16),
             dma((swaps,)),
             dma((swaps,)),
             dma((2, 4)),
+            dma,
             dma,
             dma((2,)),
             dma((3,)),
@@ -840,7 +1106,7 @@
         ),
         cost_estimate=pl.CostEstimate(flops=5 * 10**10, bytes_accessed=6 * 10**8, transcendentals=0),
         name="backward_sums",
-    )(*layer_two, *layer_one, byte_rows, grad_pairs, grad_bytes, slots, ids, gains)
+    )(*layer_two, *layer_one, byte_rows, grad_pairs, grad_bytes, slots, places, ids, gains)
     return results[:4]
 
 
@@ -873,22 +1139,28 @@
 
     flat_ids = hash_ids.reshape(positions, count_tables).T
     owners = flat_ids // shard_rows
-    local_rows = flat_ids % shard_rows + jnp.arange(count_tables, dtype=jnp.int32)[:, None] * shard_rows
     order_key = owners * positions + jnp.arange(positions, dtype=jnp.int32)[None, :]
-    order_key, grouped = lax.sort((order_key, local_rows), dimension=1, num_keys=1)
+    order_key, grouped = lax.sort((order_key, flat_ids % shard_rows), dimension=1, num_keys=1)
 
     def by_owner(array):
-        return array.reshape(count_tables, devices, -1).transpose(1, 0, 2).reshape(devices, -1)
-
-    slots = by_owner(order_key % positions).reshape(-1)
-    requested = lax.all_to_all(by_owner(grouped), "rows", split_axis=0, concat_axis=0, tiled=True)
-    flat_tables = hash_tables.reshape(count_tables * shard_rows, half_width)
-    found_rows = flat_tables.at[requested].get(mode="promise_in_bounds")
-    returned = lax.all_to_all(found_rows, "rows", split_axis=0, concat_axis=0, tiled=True)
+        return array.reshape(count_tables, devices, -1).transpose(1, 0, 2)
+
+    byte_of_slot = order_key % positions
+    numbers = jnp.arange(positions, dtype=jnp.int32)[None, :]
+    flat_bytes = byte_ids.reshape(positions)
+    table_rows = byte_table.shape[0]
+    padded = jnp.pad(byte_table, ((0, -table_rows % 128), (0, 0)))
+    slots = by_owner(byte_of_slot)
+    weights = [w_qkv[0], w_out[0], w_gate_up[0], w_down[0]]
+    byte_rows, requested, *other_weights = gather_rows(
+        by_owner(grouped), hash_tables, slots, flat_bytes[:, None], padded, weights
+    )
+    table_ids = requested.transpose(1, 0, 2).reshape(count_tables, -1)
+    id_key = lax.sort(table_ids * positions + numbers, dimension=1)
+    sorted_ids = id_key // positions
+    places = (id_key % positions)[:, None, :]
 
     gains = both(norm_gains).astype(f32)
-    qkv_both, out_both = both(w_qkv), both(w_out)
-    gate_up_both, down_both = both(w_gate_up), both(w_down)
 
     lengths = lax.dynamic_index_in_dim(patch_lengths, section, 0, keepdims=False)
     row_length = lax.dynamic_index_in_dim(row_lengths, section, 0, keepdims=False)
@@ -907,90 +1179,80 @@
     cotangent_one = jnp.where(first_core, own_cotangent, sent_cotangent).astype(f32)
     cotangent_two = jnp.where(first_core, sent_cotangent, own_cotangent).astype(f32)
 
-    flat_bytes = byte_ids.reshape(positions)
-    table_rows = byte_table.shape[0]
-    padded = jnp.pad(byte_table, ((0, -table_rows % 128), (0, 0)))
-    own_half = combine(
-        slots[None, :], flat_bytes[:, None], returned.reshape(-1, half_width), padded
-    ).reshape(M, L, half_width)
-    kept_half = lax.dynamic_index_in_dim(own_half, section, 0, keepdims=False)
-    sent_half = swap(lax.dynamic_index_in_dim(own_half, 1 - section, 0, keepdims=False))
-    byte_rows = jnp.concatenate(
-        [jnp.where(first_core, kept_half, sent_half), jnp.where(first_core, sent_half, kept_half)], axis=1
+    def both_layers(one, two):
+        pooled = dot(member, byte_rows) / counts
+        normed_one, inverse_one = normalize(pooled, gains[0, 0])
+        queries_one = dot(normed_one, one[0][:, :D]).astype(bf16)
+        byte_pairs = dot(byte_rows, one[0][:, D:]).astype(bf16)
+        attention_one, attended_one = patch_attention(patch_row, patch_col, queries_one, byte_pairs)
+        middle_one = pooled + dot(attended_one, one[1])
+        result_one, kept_one = feed_forward(middle_one, gains[0, 1], one[2], one[3])
+        encoded = jnp.where(valid, result_one, pooled).astype(bf16)
+
+        inputs_two = encoded.astype(f32)
+        normed_two, inverse_two = normalize(inputs_two, gains[1, 0])
+        mixed = dot(normed_two, two[0]).astype(bf16)
+        attended_two = causal_attention(mixed)
+        middle_two = inputs_two + dot(attended_two, two[1])
+        result_two, kept_two = feed_forward(middle_two, gains[1, 1], two[2], two[3])
+        final = jnp.where(valid, result_two, inputs_two).astype(bf16)
+        grad_kept = jnp.where(valid, cotangent_two, 0.0)
+        grad_middle, gain_two_second, grad_joined, grad_branch = feed_back(
+            middle_two, gains[1, 1], two[2], two[3], kept_two, grad_kept
+        )
+        grad_low = grad_middle.astype(bf16)
+        factors_two = [normed_two, attended_two, kept_two[0], grad_branch, None, grad_low, grad_joined, kept_two[3]]
+        grad_attended = dot_nt(grad_low, two[1]).astype(bf16)
+        grad_mixed = causal_attention_back(mixed, grad_attended)
+        grad_normed = dot_nt(grad_mixed, two[0])
+        grad_in, gain_two_first = normalize_back(inputs_two, gains[1, 0], inverse_two, grad_normed)
+        grad_encoded = jnp.where(valid, 0.0, cotangent_two) + grad_middle + grad_in
+
+
+        grad_out = cotangent_one + grad_encoded.astype(bf16).astype(f32)
+        grad_kept = jnp.where(valid, grad_out, 0.0)
+        grad_middle, gain_one_second, grad_joined, grad_branch = feed_back(
+            middle_one, gains[0, 1], one[2], one[3], kept_one, grad_kept
+        )
+        grad_low = grad_middle.astype(bf16)
+        factors_one = [normed_one, attended_one, kept_one[0], grad_branch, None, grad_low, grad_joined, kept_one[3]]
+        grad_attended = dot_nt(grad_low, one[1]).astype(bf16)
+        grad_queries, grad_pairs = patch_attention_back(
+            patch_row, patch_col, queries_one, byte_pairs, attention_one, grad_attended
+        )
+        grad_normed = dot_nt(grad_queries, one[0][:, :D])
+        grad_in, gain_one_first = normalize_back(pooled, gains[0, 0], inverse_one, grad_normed)
+        grad_pooled = jnp.where(valid, 0.0, grad_out) + grad_middle + grad_in
+        grad_bytes = dot(member_byte, (grad_pooled / counts).astype(bf16))
+        grad_bytes = (grad_bytes + dot_nt(grad_pairs, one[0][:, D:])).astype(bf16)
+
+        factors_two[4], factors_one[4] = grad_mixed, grad_queries
+        gain_part = jnp.stack([gain_one_first, gain_one_second, gain_two_first, gain_two_second])
+        return encoded, final, factors_two, factors_one, grad_pairs, grad_bytes, gain_part
+
+    encoded, final, factors_two, factors_one, grad_pairs, grad_bytes, gain_part = lax.cond(
+        first_core, both_layers, lambda one, two: both_layers(two, one), weights, other_weights
     )
-
-    pooled = dot(member, byte_rows) / counts
-    normed_one, inverse_one = normalize(pooled, gains[0, 0])
-    queries_one = dot(normed_one, qkv_both[0, :, :D]).astype(bf16)
-    byte_pairs = dot(byte_rows, qkv_both[0, :, D:]).astype(bf16)
-    attention_one, attended_one = patch_attention(patch_row, patch_col, queries_one, byte_pairs)
-    middle_one = pooled + dot(attended_one, out_both[0])
-    result_one, kept_one = feed_forward(middle_one, gains[0, 1], gate_up_both[0], down_both[0])
-    encoded = jnp.where(valid, result_one, pooled).astype(bf16)
-
-    inputs_two = encoded.astype(f32)
-    normed_two, inverse_two = normalize(inputs_two, gains[1, 0])
-    mixed = dot(normed_two, qkv_both[1]).astype(bf16)
-    attended_two = causal_attention(mixed)
-    middle_two = inputs_two + dot(attended_two, out_both[1])
-    result_two, kept_two = feed_forward(middle_two, gains[1, 1], gate_up_both[1], down_both[1])
-    final = jnp.where(valid, result_two, inputs_two).astype(bf16)
     sent_out = swap(jnp.where(first_core, final, encoded))
     kept_out = jnp.where(first_core, encoded, final)
     section_out = jnp.where(
         first_core, jnp.stack([kept_out, sent_out]), jnp.stack([sent_out, kept_out])
     )[None]
 
-    grad_kept = jnp.where(valid, cotangent_two, 0.0)
-    grad_middle, gain_two_second, grad_joined, grad_branch = feed_back(
-        middle_two, gains[1, 1], gate_up_both[1], down_both[1], kept_two, grad_kept
-    )
-    grad_low = grad_middle.astype(bf16)
-    factors_two = [normed_two, attended_two, kept_two[0], grad_branch, None, grad_low, grad_joined, kept_two[3]]
-    grad_attended = dot_nt(grad_low, out_both[1]).astype(bf16)
-    grad_mixed = causal_attention_back(mixed, grad_attended)
-    grad_normed = dot_nt(grad_mixed, qkv_both[1])
-    grad_in, gain_two_first = normalize_back(inputs_two, gains[1, 0], inverse_two, grad_normed)
-    grad_encoded = jnp.where(valid, 0.0, cotangent_two) + grad_middle + grad_in
-
-
-    grad_out = cotangent_one + grad_encoded.astype(bf16).astype(f32)
-    grad_kept = jnp.where(valid, grad_out, 0.0)
-    grad_middle, gain_one_second, grad_joined, grad_branch = feed_back(
-        middle_one, gains[0, 1], gate_up_both[0], down_both[0], kept_one, grad_kept
-    )
-    grad_low = grad_middle.astype(bf16)
-    factors_one = [normed_one, attended_one, kept_one[0], grad_branch, None, grad_low, grad_joined, kept_one[3]]
-    grad_attended = dot_nt(grad_low, out_both[0]).astype(bf16)
-    grad_queries, grad_pairs = patch_attention_back(
-        patch_row, patch_col, queries_one, byte_pairs, attention_one, grad_attended
-    )
-    grad_normed = dot_nt(grad_queries, qkv_both[0, :, :D])
-    grad_in, gain_one_first = normalize_back(pooled, gains[0, 0], inverse_one, grad_normed)
-    grad_pooled = jnp.where(valid, 0.0, grad_out) + grad_middle + grad_in
-    grad_bytes = dot(member_byte, (grad_pooled / counts).astype(bf16))
-    grad_bytes = (grad_bytes + dot_nt(grad_pairs, qkv_both[0, :, D:])).astype(bf16)
-
-
-    factors_two[4], factors_one[4] = grad_mixed, grad_queries
-    gain_part = jnp.stack([gain_one_first, gain_one_second, gain_two_first, gain_two_second])
     gain_part = jnp.pad(gain_part.reshape(8, half_width), ((8, 0), (0, 0)))
-    sums, theirs, gathered, arrived = backward_sums(
+    sums, theirs, gathered, sorted_rows = backward_sums(
         factors_two,
         factors_one,
         byte_rows,
         grad_pairs,
         grad_bytes,
-        slots[:, None],
+        slots,
+        places,
         flat_bytes[None, :],
         gain_part,
         table_rows,
     )
-    hash_grad = jax.ops.segment_sum(
-        arrived.reshape(-1, half_width).astype(f32),
-        requested.reshape(-1),
-        num_segments=count_tables * shard_rows,
-    ).reshape(count_tables, shard_rows, half_width)
+    hash_grad = place_rows(sorted_ids, sorted_rows, shard_rows)
     gathered = gathered.reshape(-1, half_width)
     byte_table_grad = gathered[:table_rows].astype(f32)
     first_gain = table_rows // 16 * 16 + 8

time: 826 us -> 757 us (0.916)
  Pallas kernels: 413 us -> 563 us
  waiting for transfers between devices: 113 us -> 0.01 us
  other arithmetic: 80.7 us -> 36.6 us
  local copies, waits for them, and re-layouts: 71.2 us -> 30.5 us
  blocking collectives: 17.8 us -> 1.86 us
  loops' own time: 0 us -> 9.72 us
  matrix products: 96.3 us -> 88 us
    pallas_call x2 -> x3, Pallas kernels: 379 us -> 532 us  [the longest x1 342 us: backward_sums(): pl.pallas_call(functools.partial(backward_kernel, devices, table_rows, co...]
    all_to_all x1 -> x0, waiting for transfers between devices: 111 us -> none  [on_device(): lax.all_to_all(found_rows, 'rows', split_axis=0, concat_axis=0, tiled=True)]
    scatter-add x1 -> x0, other arithmetic: 58.4 us -> none  [on_device(): jax.ops.segment_sum(arrived.reshape(-1, half_width).astype(f32), requeste...]
    gather x1 -> x0, local copies, waits for them, and re-layouts: 37.1 us -> none  [on_device(): found_rows = flat_tables.at[requested].get(mode='promise_in_bounds')]
    all_to_all x1 -> x0, blocking collectives: 15.5 us -> none  [on_device(): lax.all_to_all(by_owner(grouped), 'rows', split_axis=0, concat_axis=0, ti...]
    unnamed x0 -> x1, loops' own time: none -> 9.72 us
  transfers between devices with their start and end apart: 9 -> 3, of which waited for: 1 -> 0; matrix products, arithmetic and copies ran while one was open for 17% -> 3% of each run, Pallas kernels for 3% -> 25%
where the time goes in v4:
time: 757 us; the launch traced here: 745 us
  Pallas kernels  563 us (74%)
  matrix products  88 us (12%)
  other arithmetic  36.6 us (5%)
  local copies, waits for them, and re-layouts  30.5 us (4%)
  between operations  14.4 us (2%)
  loops' own time  9.72 us (1%)
    pallas_call x1, Pallas kernels, backward_sums(): pl.pallas_call(functools.partial(backward_kernel, devices, table_rows, co...  342 us
    pallas_call x1, Pallas kernels, gather_rows(): pl.pallas_call(functools.partial(gather_kernel, devices), in_specs=[vmem,...  156 us
    dot_general x9, matrix products, dot_nt(): lax.dot_general(left, right, (((1,), (1,)), ((), ())), preferred_element_...  45.7 us
    dot_general x11, matrix products, dot(): return jnp.dot(left, right, preferred_element_type=f32)  42.3 us
    pallas_call x1, Pallas kernels, place_rows(): pl.pallas_call(place_kernel, grid_spec=pltpu.PrefetchScalarGridSpec(num_s...  33.8 us
  transfers between devices with their start and end apart: 3, of which 0 were waited for; matrix products, arithmetic and copies ran while one was open for 3% of the time, Pallas kernels for 25%

profile of v4, /device:TPU:0, one launch (start us, length us, event | category | flops | bytes accessed | tf_op | source)
XLA Modules:
  0.0 744.9 jit_solution(8853616261513292358)
XLA Ops:
  7.3 2.0 dynamic-slice_bitcast_fusion
  12.8 0.9 fusion.70
  13.7 1.0 fusion.71
  15.4 1.3 copy.56
  18.7 1.6 sort.25.cloned.1.call-done
  20.3 1.4 fusion.79.refs_2_.refs_19_
  21.7 155.7 %gather_rows.1 = (bf16[1024,1024]{1,0:T(8,128)(2,1)}, s32[16,3,128]{2,1,0:T(4,128)}, bf16[1024,3072]{1,0:T(8,128)(2,1)}, bf16[1024,1024]{1,0:T(8,128)(2,1)}, bf1...) custom-call(s32[16,3,128]{2,1,0:T(4,128)} %bitcast.260, bf16[3,8192,512]{2,1,0:T(8,128)(2,1)} %refs_1_.1, ...), custom_call_target="tpu_custom_call" | custom-call | flops 49999998976 | bytes 400000000 | tf_op jit(solution)/shard_map/gather_rows/pallas_call | solution.py:238
  177.5 1.4 bitcast_add_fusion.2
  179.0 1.9 all_gather.3
  180.9 6.1 sort.27.cloned.1.call-done
  187.0 0.8 add_select_fusion
  189.0 2.3 fusion.75
  191.3 153.7 %conditional.3 = (bf16[256,1024]{1,0:T(8,128)(2,1)}, bf16[256,1024]{1,0:T(8,128)(2,1)}, bf16[256,3072]{1,0:T(8,128)(2,1)}, bf16[256,1024]{1,0:T(8,128)(2,1)}, bf...) conditional(s32[]{:T(128)} %convert_element_type.276, ...), branch_computations={%region_4.17_spmd, %region_17.30_spmd} | conditional | flops 49896669184 | bytes 539752384
  204.2 6.1 convolution_convert_fusion.5.key_ref.value_ref
  210.6 2.2 copy-done.2
  212.7 6.0 patch_attention.3
  219.8 6.4 fusion.90
  226.2 2.5 multiply_convert_fusion.6
  229.2 5.8 fusion.60
  235.1 1.2 fusion.53
  237.1 4.6 convolution_convert_fusion.4.query_ref.key_ref.value_ref
  241.7 8.0 %causal_attention.3 = bf16[256,1024]{1,0:T(8,128)(2,1)S(1)} custom-call(bf16[256,3072]{1,0:T(8,128)(2,1)S(1)} %convolution_convert_fusion.4.query_ref.key_ref.value_ref, bf16[256,3072]{1,0:T(8,128)(2,1)S(1)} %convolution_convert_fusion.4.query_ref.key_ref.value_ref, bf16[256,3072]{1,0:T(8,128)(2,1)S(1)} %convolution_convert_fusion.4.query_ref.key_ref.value_ref), custom_call_target="tpu_custom_call" | custom-call | flops 2000000000 | bytes 2000000 | tf_op jit(solution)/shard_map/cond/branch_1_fun/causal_attention/pallas_call | solution.py:441
  249.7 2.0 multiply_reduce_fusion.15
  251.9 6.3 fusion.91
  258.4 7.3 add_multiply_fusion.3
  265.8 7.3 multiply_reduce_fusion.10
  274.3 11.4 %causal_attention_back.3 = bf16[256,3072]{1,0:T(8,128)(2,1)S(1)} custom-call(bf16[256,3072]{1,0:T(8,128)(2,1)S(1)} %convolution_convert_fusion.4.query_ref.key_ref.value_ref, bf16[256,3072]{1,0:T(8,128)(2,1)S(1)} %convolution_convert_fusion.4.query_ref.key_ref.value_ref, bf16[256,3072]{1,0:T(8,128)(2,1)S(1)} %convolution_convert_fusion.4.query_ref.key_ref.value_ref, ...), custom_call_target="tpu_custom_call" | custom-call | flops 4000000000 | bytes 4000000 | tf_op jit(solution)/shard_map/cond/branch_1_fun/causal_attention_back/pallas_call | solution.py:482
  285.7 5.5 fusion.59
  291.2 2.9 select_convert_fusion.2
  294.2 7.1 add_multiply_fusion.2
  301.2 1.7 maximum_convert_fusion.3
  303.0 6.1 multiply_reduce_fusion.11
  309.2 1.7 fusion.69
  312.5 5.9 patch_attention_back.3
  318.4 8.3 %fusion.36 = f32[1024,1024]{0,1:T(8,128)S(1)} fusion(bf16[1024,2048]{1,0:T(8,128)(2,1)S(1)} %get-tuple-element.500, bf16[1024,3072]{1,0:T(8,128)(2,1)} %get-tuple-element.186), kind=kOutput, calls=%fused_computation.89 | convolution fusion | flops 4294967296 | bytes 12582912 | tf_op jit(solution)/shard_map/cond/branch_1_fun/dot_general | solution.py:32
  326.8 2.7 multiply_reduce_fusion.9
  329.5 3.0 fusion.35
  332.5 2.9 copy.53
  335.4 3.5 multiply_convert_fusion.5
  338.9 5.8 fusion.52
  344.9 342.0 %backward_sums.1 = (bf16[2,64,6272]{2,1,0:T(8,128)(2,1)}, bf16[64,6272]{1,0:T(8,128)(2,1)}, bf16[16,32,512]{2,1,0:T(8,128)(2,1)}, bf16[3,2048,512]{2,1,0:T(8,128...) custom-call(bf16[256,1024]{1,0:T(8,128)(2,1)} %get-tuple-element.276, ...), custom_call_target="tpu_custom_call" | custom-call | flops 49999998976 | bytes 600000000 | tf_op jit(solution)/shard_map/backward_sums/pallas_call | solution.py:1064
  686.9 1.6 fusion.73
  690.1 0.9 slice_convert_fusion
  694.1 2.2 select_bitcast_fusion
  696.5 1.9 maximum_bitcast_fusion.1
  698.4 1.2 maximum_bitcast_fusion
  699.6 33.8 %place_rows.1 = f32[3,8192,512]{2,1,0:T(8,128)} custom-call(s32[27]{0:T(128)S(1)} %reshape.290.starts_ref, s32[3,1,2048]{2,1,0:T(1,128)S(1)} %broadcast_in_dim.115.ids_ref, bf16[3,2048,512]{2,1,0:T(8,128)(2,1)} %get-tuple-element.272.rows_ref), custom_call_target="tpu_custom_call" | custom-call | flops 10000000000 | bytes 60000000 | tf_op jit(solution)/shard_map/place_rows/pallas_call | solution.py:1011
  735.5 2.3 maximum_select_fusion
  (166 shorter events, 24.2 us)
Async XLA Ops:
  7.2 9.6 %copy-start.68 = (s32[2]{0:T(128)S(1)}, s32[2]{0:T(128)}, u32[]{:S(2)}) copy-start(s32[2]{0:T(128)} %param.17) | copy-start | bytes 28
  7.2 10.1 %copy-start.63 = (bf16[260,512]{1,0:T(8,128)(2,1)S(1)}, bf16[260,512]{1,0:T(8,128)(2,1)}, u32[]{:S(2)}) copy-start(bf16[260,512]{1,0:T(8,128)(2,1)} %param.18) | copy-start | bytes 798724
  7.2 14.5 %copy-start.24 = (bf16[1,1024,1024]{2,1,0:T(8,128)(2,1)S(1)}, bf16[1,1024,1024]{2,1,0:T(8,128)(2,1)}, u32[]{:S(2)}) copy-start(bf16[1,1024,1024]{2,1,0:T(8,128)(2,1)} %param.22) | copy-start | bytes 6291460
  7.2 13.1 %sort.25.cloned.1.call-start = ((), (), s32[]{:S(2)}) async-start(), calls=%async_computation | async-start | bytes 196640 | tf_op jit(solution)/shard_map/sort | solution.py:1143
  9.3 179.7 %collective-permute-start = (bf16[256,1024]{1,0:T(8,128)(2,1)}, bf16[256,1024]{1,0:T(8,128)(2,1)}, u32[]{:S(2)}, u32[]{:S(2)}) collective-permute-start(bf16[256,1024]{1,0:T(8,128)(2,1)} %dynamic-slice_bitcast_fusion), channel_id=1, source_target_pairs={{0,16},{16,0},{1,17},{17,1},{2,18},{18,2},{3,19},{19,3},{4,20},{20... | collective-permute-start | bytes 1572872 | tf_op jit(solution)/shard_map/ppermute | solution.py:1114
  11.2 175.8 %sort.27.cloned.1.call-start = ((), (), s32[]{:S(2)}) async-start(), calls=%async_computation.1 | async-start | bytes 98336 | tf_op jit(solution)/shard_map/sort | solution.py:1159
  15.4 6.3 copy-start.65
  21.7 157.3 %copy-start.66 = (bf16[1,2,1024]{2,1,0:T(2,128)(2,1)S(1)}, bf16[1,2,1024]{2,1,0:T(2,128)(2,1)}, u32[]{:S(2)}) copy-start(bf16[1,2,1024]{2,1,0:T(2,128)(2,1)} %param.20) | copy-start | bytes 12292
  21.7 167.2 %copy-start.48 = (bf16[1,2,256,1024]{3,2,1,0:T(8,128)(2,1)S(1)}, bf16[1,2,256,1024]{3,2,1,0:T(8,128)(2,1)}, u32[]{:S(2)}) copy-start(bf16[1,2,256,1024]{3,2,1,0:T(8,128)(2,1)} %param.25) | copy-start | bytes 3145732
  177.5 13.8 %copy-start.51 = (bf16[256,1024]{1,0:T(8,128)(2,1)S(1)}, bf16[256,1024]{1,0:T(8,128)(2,1)}, u32[]{:S(2)}) copy-start(bf16[256,1024]{1,0:T(8,128)(2,1)} %fusion.70) | copy-start | bytes 1572868
  188.9 2.3 copy-start.76
  200.1 3.4 copy-start.67
  210.5 2.2 copy-start.2
  212.7 6.1 copy-start.18
  212.7 6.1 copy-start.26
  218.8 1.0 copy-start.42
  219.6 9.6 %copy-start.10 = (f32[256,1024]{1,0:T(8,128)}, f32[256,1024]{1,0:T(8,128)S(1)}, u32[]{:S(2)}) copy-start(f32[256,1024]{1,0:T(8,128)S(1)} %get-tuple-element.451) | copy-start | bytes 3145732 | tf_op jit(solution)/shard_map/conditional.1
  219.8 6.4 copy-start.32
  226.2 3.0 copy-start.7
  241.7 8.0 %copy-start.30 = (bf16[1024,1024]{1,0:T(8,128)(2,1)S(1)}, bf16[1024,1024]{1,0:T(8,128)(2,1)}, u32[]{:S(2)}) copy-start(bf16[1024,1024]{1,0:T(8,128)(2,1)} %get-tuple-element.193) | copy-start | bytes 6291460 | tf_op jit(solution)/shard_map/conditional.1
  249.7 2.1 copy-start.44
  251.9 6.3 copy-start.34
  258.2 7.4 copy-start.5
  258.3 7.3 copy-start.53
  265.8 7.3 copy-start.40
  285.7 5.5 copy-start.72
  285.7 5.5 copy-start.13
  291.2 11.8 %slice-start = ((s8[11534336]{0:T(1024)(128)(4,1)}), s8[4194304]{0:T(1024)(128)(4,1)S(1)}, s32[]{:S(2)}) async-start(s8[11534336]{0:T(1024)(128)(4,1)} %bitcast.188), calls=%async_computation.4 | async-start | bytes 8388608 | tf_op jit(solution)/shard_map/conditional.1
  294.2 7.1 copy-start.62
  294.2 8.8 %slice-start.1 = ((s8[11534336]{0:T(1024)(128)(4,1)}), s8[4194304]{0:T(1024)(128)(4,1)S(1)}, s32[]{:S(2)}) async-start(s8[11534336]{0:T(1024)(128)(4,1)} %bitcast.188), calls=%async_computation.5 | async-start | bytes 8388608 | tf_op jit(solution)/shard_map/conditional.1
  294.2 8.8 %slice-start.2 = ((s8[11534336]{0:T(1024)(128)(4,1)}), s8[3145728]{0:T(1024)(128)(4,1)S(1)}, s32[]{:S(2)}) async-start(s8[11534336]{0:T(1024)(128)(4,1)} %bitcast.188), calls=%async_computation.6 | async-start | bytes 6291456 | tf_op jit(solution)/shard_map/conditional.1
  301.2 1.8 copy-start.11
  303.0 6.1 copy-start.22
  309.1 1.9 copy-start.27
  309.2 3.3 copy-start.3
  311.1 7.3 copy-start.59
  318.4 8.4 %copy-start.70 = (bf16[1024,2048]{1,0:T(8,128)(2,1)}, bf16[1024,2048]{1,0:T(8,128)(2,1)S(1)}, u32[]{:S(2)}) copy-start(bf16[1024,2048]{1,0:T(8,128)(2,1)S(1)} %get-tuple-element.500) | copy-start | bytes 12582916 | tf_op jit(solution)/shard_map/conditional.1
  318.4 8.4 %copy-start.74 = (bf16[256,1024]{1,0:T(8,128)(2,1)}, bf16[256,1024]{1,0:T(8,128)(2,1)S(1)}, u32[]{:S(2)}) copy-start(bf16[256,1024]{1,0:T(8,128)(2,1)S(1)} %get-tuple-element.499) | copy-start | bytes 1572868 | tf_op jit(solution)/shard_map/conditional.1
  318.4 8.4 %copy-start.19 = (f32[256,1024]{1,0:T(8,128)S(1)}, f32[256,1024]{1,0:T(8,128)}, u32[]{:S(2)}) copy-start(f32[256,1024]{1,0:T(8,128)} %copy-done.17) | copy-start | bytes 3145732 | tf_op jit(solution)/shard_map/conditional.1
  326.7 2.8 copy-start.23
  326.7 2.8 copy-start.36
  326.8 2.8 copy-start.38
  338.9 5.8 copy-start.47
  688.5 1.6 copy-start.64
  693.7 41.1 %collective-permute-start.2 = (bf16[2,2,1024]{2,1,0:T(2,128)(2,1)S(1)}, bf16[2,2,1024]{2,1,0:T(2,128)(2,1)S(1)}, u32[]{:S(2)}, u32[]{:S(2)}) collective-permute-start(bf16[2,2,1024]{2,1,0:T(2,128)(2,1)S(1)} %reshape.291), channel_id=1, source_target_pairs={{0,16},{16,0},{1,17},{17,1},{2,18},{18,2},{3,19},{19,3},{4,20},{20... | collective-permute-start | bytes 24584 | tf_op jit(solution)/shard_map/ppermute | solution.py:1114
  696.4 39.1 %collective-permute-start.1 = (bf16[256,1024]{1,0:T(8,128)(2,1)}, bf16[256,1024]{1,0:T(8,128)(2,1)}, u32[]{:S(2)}, u32[]{:S(2)}) collective-permute-start(bf16[256,1024]{1,0:T(8,128)(2,1)} %get-tuple-element.469), channel_id=1, source_target_pairs={{0,16},{16,0},{1,17},{17,1},{2,18},{18,2},{3,19},{19,3},{4,20},{20... | collective-permute-start | bytes 1572872 | tf_op jit(solution)/shard_map/ppermute | solution.py:1114
  699.6 34.5 %copy-start.60 = (f32[64,512]{1,0:T(8,128)S(1)}, f32[64,512]{1,0:T(8,128)}, u32[]{:S(2)}) copy-start(f32[64,512]{1,0:T(8,128)} %get-tuple-element.462) | copy-start | bytes 393220
  699.6 35.9 %copy-start.45 = (bf16[1,1,256,1024]{3,2,1,0:T(8,128)(2,1)S(1)}, bf16[1,1,256,1024]{3,2,1,0:T(8,128)(2,1)}, u32[]{:S(2)}) copy-start(bf16[1,1,256,1024]{3,2,1,0:T(8,128)(2,1)} %get-tuple-element.468) | copy-start | bytes 1572868
  (4 other events, 3.4 us)
Sparse Core Ops, SparseCore 0:
  11.3 8.6 sort.29.cloned.1.call-done
  179.1 7.6 sort.31.cloned.1.call-done
  (2 shorter events, 0.0 us)

commit v5 on v4

--- a/solution.py
+++ b/solution.py
@@ -17,6 +17,7 @@
 P_SIZE = 256
 GROUP = 512
 VMEM_BYTES = 48 * 1024 * 1024
+FAR_FIRST = (4, 12, 8, 5, 11, 7, 9, 6, 10, 3, 13, 2, 14, 1, 15)
 SORT_TURN = 3
 
 epsilon = 1e-05
@@ -511,25 +512,153 @@
     return grad_inputs, grad_gain
 
 
+def feed_kernel(
+    hidden_ref, gain_ref, w_gate_ref, w_up_ref, w_down_ref, out_ref, normed_ref, gate_ref, up_ref, inner_ref
+):
+    @pl.when(pl.program_id(0) == 0)
+    def _():
+        hidden = hidden_ref[...]
+        normed_ref[...] = normalize(hidden, gain_ref[...])[0]
+        out_ref[...] = hidden
+
+    gate, up = dot(normed_ref[...], w_gate_ref[...]), dot(normed_ref[...], w_up_ref[...])
+    inner = (gate * jax.nn.sigmoid(gate) * up).astype(bf16)
+    gate_ref[...] = gate.astype(bf16)
+    up_ref[...] = up.astype(bf16)
+    inner_ref[...] = inner
+    out_ref[...] += dot(inner, w_down_ref[...])
+
+
+def feed_specs():
+    tile = FF // 2
+    tiles = FF // tile
+    whole = pl.BlockSpec((P_SIZE, D), lambda j: (0, 0))
+    row = pl.BlockSpec((1, D), lambda j: (0, 0))
+    gate = pl.BlockSpec((D, tile), lambda j: (0, j))
+    up = pl.BlockSpec((D, tile), lambda j: (0, j + tiles))
+    down = pl.BlockSpec((tile, D), lambda j: (j, 0))
+    part = pl.BlockSpec((P_SIZE, tile), lambda j: (0, j))
+    return tiles, whole, row, gate, up, down, part
+
+
 def feed_forward(hidden, gain, w_gate_up, w_down):
-    normed, inverse = normalize(hidden, gain)
-    joined = dot(normed, w_gate_up)
-    inner = (jax.nn.silu(joined[:, :FF]) * joined[:, FF:]).astype(bf16)
-    return hidden + dot(inner, w_down), (normed, inverse, joined, inner)
+    tiles, whole, row, gate, up, down, part = feed_specs()
+    narrow = jax.ShapeDtypeStruct((P_SIZE, FF), bf16)
+    out, normed, gates, ups, inner = pl.pallas_call(
+        feed_kernel,
+        grid=(tiles,),
+        in_specs=[whole, row, gate, up, down],
+        out_specs=[whole, whole, part, part, part],
+        out_shape=[
+            jax.ShapeDtypeStruct((P_SIZE, D), f32),
+            jax.ShapeDtypeStruct((P_SIZE, D), bf16),
+            narrow,
+            narrow,
+            narrow,
+        ],
+        compiler_params=params("arbitrary"),
+        cost_estimate=pl.CostEstimate(flops=6 * P_SIZE * D * FF, bytes_accessed=24 * 10**6, transcendentals=P_SIZE * FF),
+        name="feed_forward",
+    )(hidden, gain[None, :], w_gate_up, w_gate_up, w_down)
+    return out, (normed, gates, ups, inner)
+
+
+def feed_back_kernel(
+    grad_ref,
+    hidden_ref,
+    gain_ref,
+    gate_ref,
+    up_ref,
+    w_gate_ref,
+    w_up_ref,
+    w_down_ref,
+    out_ref,
+    low_ref,
+    branch_ref,
+    joined_ref,
+    grad_gain_ref,
+    total_ref,
+):
+    step = pl.program_id(0)
+    tile = gate_ref.shape[1]
+
+    @pl.when(step == 0)
+    def _():
+        branch_ref[...] = grad_ref[...].astype(bf16)
+        total_ref[...] = jnp.zeros_like(total_ref)
+
+    grad_inner = dot_nt(branch_ref[...], w_down_ref[...])
+    gate, up = gate_ref[...].astype(f32), up_ref[...].astype(f32)
+    sigmoid = jax.nn.sigmoid(gate)
+    grad_gate = (grad_inner * up * sigmoid * (1.0 + gate * (1.0 - sigmoid))).astype(bf16)
+    grad_up = (grad_inner * gate * sigmoid).astype(bf16)
+    joined_ref[:, pl.ds(pl.multiple_of(step * tile, 128), tile)] = grad_gate
+    joined_ref[:, pl.ds(pl.multiple_of(FF + step * tile, 128), tile)] = grad_up
+    total_ref[...] += dot_nt(grad_gate, w_gate_ref[...]) + dot_nt(grad_up, w_up_ref[...])
+
+    @pl.when(step == pl.num_programs(0) - 1)
+    def _():
+        hidden = hidden_ref[...]
+        inverse = lax.rsqrt(jnp.mean(hidden * hidden, axis=-1, keepdims=True) + epsilon)
+        grad_in, grad_gain = normalize_back(hidden, gain_ref[...], inverse, total_ref[...])
+        result = grad_ref[...] + grad_in
+        out_ref[...] = result
+        low_ref[...] = result.astype(bf16)
+        grad_gain_ref[...] = grad_gain[None, :]
 
 
 def feed_back(hidden, gain, w_gate_up, w_down, kept, grad_out):
-    normed, inverse, joined, inner = kept
-    gate, up = joined[:, :FF], joined[:, FF:]
-    sigmoid = jax.nn.sigmoid(gate)
-    grad_branch = grad_out.astype(bf16)
-    grad_inner = dot_nt(grad_branch, w_down)
-    grad_gate = grad_inner * up * sigmoid * (1.0 + gate * (1.0 - sigmoid))
-    grad_up = grad_inner * gate * sigmoid
-    grad_joined = jnp.concatenate([grad_gate, grad_up], axis=1).astype(bf16)
-    grad_normed = dot_nt(grad_joined, w_gate_up)
-    grad_in, grad_gain = normalize_back(hidden, gain, inverse, grad_normed)
-    return grad_out + grad_in, grad_gain, grad_joined, grad_branch
+    normed, gates, ups, inner = kept
+    tiles, whole, row, gate, up, down, part = feed_specs()
+    out, low, branch, joined, grad_gain = pl.pallas_call(
+        feed_back_kernel,
+        grid=(tiles,),
+        in_specs=[whole, whole, row, part, part, gate, up, down],
+        out_specs=[whole, whole, whole, pl.BlockSpec((P_SIZE, 2 * FF), lambda j: (0, 0)), row],
+        out_shape=[
+            jax.ShapeDtypeStruct((P_SIZE, D), f32),
+            jax.ShapeDtypeStruct((P_SIZE, D), bf16),
+            jax.ShapeDtypeStruct((P_SIZE, D), bf16),
+            jax.ShapeDtypeStruct((P_SIZE, 2 * FF), bf16),
+            jax.ShapeDtypeStruct((1, D), f32),
+        ],
+        scratch_shapes=[pltpu.VMEM((P_SIZE, D), f32)],
+        compiler_params=params("arbitrary"),
+        cost_estimate=pl.CostEstimate(flops=6 * P_SIZE * D * FF, bytes_accessed=24 * 10**6, transcendentals=P_SIZE * FF),
+        name="feed_back",
+    )(grad_out, hidden, gain[None, :], gates, ups, w_gate_up, w_gate_up, w_down)
+    return out, low, grad_gain[0], joined, branch
+
+
+def byte_grad_kernel(patch_col_ref, grad_ref, keys_ref, values_ref, w_key_ref, w_value_ref, out_ref):
+    tile = out_ref.shape[0]
+    owner = lax.broadcasted_iota(jnp.int32, (tile, P_SIZE), 1)
+    member = (owner == patch_col_ref[...]).astype(f32).astype(bf16)
+    total = dot(member, grad_ref[...]) + dot_nt(keys_ref[...], w_key_ref[...])
+    out_ref[...] = (total + dot_nt(values_ref[...], w_value_ref[...])).astype(bf16)
+
+
+def byte_grads(patch_col, grad_patches, grad_pairs, w_qkv):
+    tile = 256
+    part = lambda column: pl.BlockSpec((tile, D), lambda i: (i, column))
+    weight = lambda column: pl.BlockSpec((D, D), lambda i: (0, column))
+    return pl.pallas_call(
+        byte_grad_kernel,
+        grid=(L // tile,),
+        in_specs=[
+            pl.BlockSpec((tile, 1), lambda i: (i, 0)),
+            pl.BlockSpec((P_SIZE, D), lambda i: (0, 0)),
+            part(0),
+            part(1),
+            weight(1),
+            weight(2),
+        ],
+        out_specs=pl.BlockSpec((tile, D), lambda i: (i, 0)),
+        out_shape=jax.ShapeDtypeStruct((L, D), bf16),
+        compiler_params=params("arbitrary"),
+        cost_estimate=pl.CostEstimate(flops=5 * L * D * D, bytes_accessed=11 * 10**6, transcendentals=0),
+        name="byte_grads",
+    )(patch_col, grad_patches, grad_pairs, grad_pairs, w_qkv, w_qkv)
 
 
 def chip_bits(devices):
@@ -840,10 +969,11 @@
 
     block_rows = block_ref.shape[1]
     block_slots = block_ref.shape[0]
+    block_steps = [*(FAR_FIRST if devices == 16 else range(1, devices)), 0]
 
     def block_copy(step):
         target = staged_ref.at[step] if step else arrived_ref.at[me]
-        slot = (step - 1) % devices % block_slots
+        slot = block_steps.index(step) % block_slots
         return pltpu.make_async_copy(block_ref.at[slot], target, block_sems.at[slot])
 
     def trade(step):
@@ -862,7 +992,7 @@
     def make_blocks():
         own_copy.wait()
         settled(("grads",))
-        steps = list(range(1, devices)) + [0]
+        steps = block_steps
         behind = block_slots - 1
 
         def pass_on(step):
@@ -1155,11 +1285,6 @@
     byte_rows, requested, *other_weights = gather_rows(
         by_owner(grouped), hash_tables, slots, flat_bytes[:, None], padded, weights
     )
-    table_ids = requested.transpose(1, 0, 2).reshape(count_tables, -1)
-    id_key = lax.sort(table_ids * positions + numbers, dimension=1)
-    sorted_ids = id_key // positions
-    places = (id_key % positions)[:, None, :]
-
     gains = both(norm_gains).astype(f32)
 
     lengths = lax.dynamic_index_in_dim(patch_lengths, section, 0, keepdims=False)
@@ -1170,7 +1295,6 @@
     patch_row, patch_col = byte_patch[None, :], byte_patch[:, None]
     patches = jnp.arange(P_SIZE, dtype=jnp.int32)
     member = (patches[:, None] == patch_row).astype(bf16)
-    member_byte = (patches[None, :] == patch_col).astype(bf16)
     counts = lengths.astype(f32)[:, None]
     valid = (patches < row_length)[:, None]
 
@@ -1197,10 +1321,9 @@
         result_two, kept_two = feed_forward(middle_two, gains[1, 1], two[2], two[3])
         final = jnp.where(valid, result_two, inputs_two).astype(bf16)
         grad_kept = jnp.where(valid, cotangent_two, 0.0)
-        grad_middle, gain_two_second, grad_joined, grad_branch = feed_back(
+        grad_middle, grad_low, gain_two_second, grad_joined, grad_branch = feed_back(
             middle_two, gains[1, 1], two[2], two[3], kept_two, grad_kept
         )
-        grad_low = grad_middle.astype(bf16)
         factors_two = [normed_two, attended_two, kept_two[0], grad_branch, None, grad_low, grad_joined, kept_two[3]]
         grad_attended = dot_nt(grad_low, two[1]).astype(bf16)
         grad_mixed = causal_attention_back(mixed, grad_attended)
@@ -1211,10 +1334,9 @@
 
         grad_out = cotangent_one + grad_encoded.astype(bf16).astype(f32)
         grad_kept = jnp.where(valid, grad_out, 0.0)
-        grad_middle, gain_one_second, grad_joined, grad_branch = feed_back(
+        grad_middle, grad_low, gain_one_second, grad_joined, grad_branch = feed_back(
             middle_one, gains[0, 1], one[2], one[3], kept_one, grad_kept
         )
-        grad_low = grad_middle.astype(bf16)
         factors_one = [normed_one, attended_one, kept_one[0], grad_branch, None, grad_low, grad_joined, kept_one[3]]
         grad_attended = dot_nt(grad_low, one[1]).astype(bf16)
         grad_queries, grad_pairs = patch_attention_back(
@@ -1223,16 +1345,21 @@
         grad_normed = dot_nt(grad_queries, one[0][:, :D])
         grad_in, gain_one_first = normalize_back(pooled, gains[0, 0], inverse_one, grad_normed)
         grad_pooled = jnp.where(valid, 0.0, grad_out) + grad_middle + grad_in
-        grad_bytes = dot(member_byte, (grad_pooled / counts).astype(bf16))
-        grad_bytes = (grad_bytes + dot_nt(grad_pairs, one[0][:, D:])).astype(bf16)
+        grad_bytes = byte_grads(patch_col, (grad_pooled / counts).astype(bf16), grad_pairs, one[0])
+
+        table_ids = requested.transpose(1, 0, 2).reshape(count_tables, -1)
+        id_key = lax.sort(table_ids * positions + numbers, dimension=1)
+        sorted_ids = id_key // positions
+        places = (id_key % positions)[:, None, :]
 
         factors_two[4], factors_one[4] = grad_mixed, grad_queries
         gain_part = jnp.stack([gain_one_first, gain_one_second, gain_two_first, gain_two_second])
-        return encoded, final, factors_two, factors_one, grad_pairs, grad_bytes, gain_part
-
-    encoded, final, factors_two, factors_one, grad_pairs, grad_bytes, gain_part = lax.cond(
+        return encoded, final, factors_two, factors_one, grad_pairs, grad_bytes, gain_part, sorted_ids, places
+
+    results = lax.cond(
         first_core, both_layers, lambda one, two: both_layers(two, one), weights, other_weights
     )
+    encoded, final, factors_two, factors_one, grad_pairs, grad_bytes, gain_part, sorted_ids, places = results
     sent_out = swap(jnp.where(first_core, final, encoded))
     kept_out = jnp.where(first_core, encoded, final)
     section_out = jnp.where(

time: 757 us -> 719 us (0.950)
  matrix products: 88 us -> 30.4 us
  Pallas kernels: 563 us -> 612 us
  other arithmetic: 36.6 us -> 19.4 us
  local copies, waits for them, and re-layouts: 30.5 us -> 20.8 us
    pallas_call x0 -> x5, Pallas kernels: none -> 54.9 us  [the longest x2 24.9 us: feed_back(): pl.pallas_call(feed_back_kernel, grid=(tiles,), in_specs=[whole, whole, r...]
    dot_general x9 -> x4, matrix products: 45.7 us -> 13.2 us  [dot_nt(): lax.dot_general(left, right, (((1,), (1,)), ((), ())), preferred_element_...]
    dot_general x11 -> x6, matrix products: 42.3 us -> 17.1 us  [dot(): return jnp.dot(left, right, preferred_element_type=f32)]
    convert_element_type x9 -> x2, other arithmetic: 14.1 us -> 0.67 us  [the longest x1 0.5 us: both_layers(): (grad_pooled / counts).astype(bf16)]
    pallas_call x1, Pallas kernels: 342 us -> 333 us  [backward_sums(): pl.pallas_call(functools.partial(backward_kernel, devices, table_rows, co...]
  transfers between devices with their start and end apart: 3 -> 3, of which waited for: 0 -> 0; matrix products, arithmetic and copies ran while one was open for 3% -> 2% of each run, Pallas kernels for 25% -> 27%
where the time goes in v5:
time: 719 us; the launch traced here: 709 us
  Pallas kernels  612 us (85%)
  matrix products  30.4 us (4%)
  local copies, waits for them, and re-layouts  20.8 us (3%)
  other arithmetic  19.4 us (3%)
  between operations  14.4 us (2%)
  loops' own time  8.5 us (1%)
    pallas_call x1, Pallas kernels, backward_sums(): pl.pallas_call(functools.partial(backward_kernel, devices, table_rows, co...  333 us
    pallas_call x1, Pallas kernels, gather_rows(): pl.pallas_call(functools.partial(gather_kernel, devices), in_specs=[vmem,...  156 us
    pallas_call x1, Pallas kernels, place_rows(): pl.pallas_call(place_kernel, grid_spec=pltpu.PrefetchScalarGridSpec(num_s...  35.9 us
    pallas_call x2, Pallas kernels, feed_back(): pl.pallas_call(feed_back_kernel, grid=(tiles,), in_specs=[whole, whole, r...  24.9 us
    pallas_call x2, Pallas kernels, feed_forward(): pl.pallas_call(feed_kernel, grid=(tiles,), in_specs=[whole, row, gate, up...  20.9 us
    dot_general x6, matrix products, dot(): return jnp.dot(left, right, preferred_element_type=f32)  17.1 us
  transfers between devices with their start and end apart: 3, of which 0 were waited for; matrix products, arithmetic and copies ran while one was open for 2% of the time, Pallas kernels for 27%

profile of v5, /device:TPU:0, one launch (start us, length us, event | category | flops | bytes accessed | tf_op | source)
XLA Modules:
  0.0 708.8 jit_solution(505477043685774052)
XLA Ops:
  7.3 1.1 dynamic-slice_bitcast_fusion
  8.9 0.8 copy.42
  12.0 0.7 copy.43
  12.7 1.3 copy.44
  15.3 1.8 all_gather.3
  17.1 0.8 pad.10.refs_4_
  18.4 1.6 sort.35.cloned.1.call-done
  20.0 1.4 fusion.64.refs_2_.refs_19_
  21.4 155.6 %gather_rows.1 = (bf16[1024,1024]{1,0:T(8,128)(2,1)}, s32[16,3,128]{2,1,0:T(4,128)S(1)}, bf16[1024,3072]{1,0:T(8,128)(2,1)}, bf16[1024,1024]{1,0:T(8,128)(2,1)},...) custom-call(s32[16,3,128]{2,1,0:T(4,128)} %bitcast.205, bf16[3,8192,512]{2,1,0:T(8,128)(2,1)} %refs_1_.1, ...), custom_call_target="tpu_custom_call" | custom-call | flops 49999998976 | bytes 400000000 | tf_op jit(solution)/shard_map/gather_rows/pallas_call | solution.py:239
  177.1 1.5 fusion.60
  178.6 136.7 %conditional.3 = (bf16[256,1024]{1,0:T(8,128)(2,1)S(1)}, bf16[256,1024]{1,0:T(8,128)(2,1)S(1)}, bf16[256,1024]{1,0:T(8,128)(2,1)}, bf16[256,1024]{1,0:T(8,128)(2...) conditional(s32[]{:T(128)} %convert_element_type.145, ...), branch_computations={%region_4.12_spmd, %region_12.20_spmd} | conditional | flops 50378838016 | bytes 360850560
  187.2 2.5 multiply_reduce_fusion.5
  189.8 0.8 copy-done.16
  190.6 7.6 %fusion.30.key_ref.value_ref = bf16[1024,2048]{1,0:T(8,128)(2,1)} fusion(bf16[1024,1024]{1,0:T(8,128)(2,1)} %get-tuple-element.180, bf16[1024,3072]{1,0:T(8,128)(2,1)S(1)} %copy-done.16), kind=kOutput, calls=%fused_computation.59 | convolution fusion | flops 4297064448 | bytes 10485760 | tf_op jit(solution)/shard_map/cond/branch_1_fun/dot_general | solution.py:29
  198.4 0.7 fusion.41.query_ref
  199.5 2.2 copy-done.6
  201.6 6.0 patch_attention.3
  207.7 0.7 convolution_add_fusion.1.hidden_ref
  208.5 10.3 %feed_forward.6 = (f32[256,1024]{1,0:T(8,128)S(1)}, bf16[256,1024]{1,0:T(8,128)(2,1)}, bf16[256,2816]{1,0:T(8,128)(2,1)S(1)}, bf16[256,2816]{1,0:T(8,128)(2,1)S(1)}, bf16[256,2816]{1,0:T(8,128)(2,1)}) custom-call(f32[256,1024]{1,0:T(8,128)S(1)} %convolution_add_fusion.1.hidden_ref, f32[1,1024]{1,0:T(1,128)S(1)} %get-tuple-element.453.gain_ref, ...), custom_call_target="tpu_custom_call" | custom-call | flops 4429185024 | bytes 24000000 | tf_op jit(solution)/shard_map/cond/branch_1_fun/feed_forward/pallas_call | solution.py:547
  219.4 4.8 convolution_convert_fusion.3.query_ref.key_ref.value_ref
  224.2 8.0 %causal_attention.3 = bf16[256,1024]{1,0:T(8,128)(2,1)S(1)} custom-call(bf16[256,3072]{1,0:T(8,128)(2,1)S(1)} %convolution_convert_fusion.3.query_ref.key_ref.value_ref, bf16[256,3072]{1,0:T(8,128)(2,1)S(1)} %convolution_convert_fusion.3.query_ref.key_ref.value_ref, bf16[256,3072]{1,0:T(8,128)(2,1)S(1)} %convolution_convert_fusion.3.query_ref.key_ref.value_ref), custom_call_target="tpu_custom_call" | custom-call | flops 2000000000 | bytes 2000000 | tf_op jit(solution)/shard_map/cond/branch_1_fun/causal_attention/pallas_call | solution.py:442
  232.2 0.7 convert_add_fusion.2.hidden_ref
  233.0 10.6 %feed_forward.7 = (f32[256,1024]{1,0:T(8,128)S(1)}, bf16[256,1024]{1,0:T(8,128)(2,1)}, bf16[256,2816]{1,0:T(8,128)(2,1)S(1)}, bf16[256,2816]{1,0:T(8,128)(2,1)S(1)}, bf16[256,2816]{1,0:T(8,128)(2,1)}) custom-call(f32[256,1024]{1,0:T(8,128)S(1)} %convert_add_fusion.2.hidden_ref, f32[1,1024]{1,0:T(1,128)S(1)} %get-tuple-element.451.gain_ref, ...), custom_call_target="tpu_custom_call" | custom-call | flops 4429185024 | bytes 24000000 | tf_op jit(solution)/shard_map/cond/branch_1_fun/feed_forward/pallas_call | solution.py:547
  243.6 12.2 %feed_back.6 = (f32[256,1024]{1,0:T(8,128)S(1)}, bf16[256,1024]{1,0:T(8,128)(2,1)S(1)}, bf16[256,1024]{1,0:T(8,128)(2,1)}, bf16[256,5632]{1,0:T(8,128)(2,1)}, f32[1,1024]{1,0:T(1,128)S(1)}) custom-call(f32[256,1024]{1,0:T(8,128)S(1)} %get-tuple-element.455.grad_ref, f32[256,1024]{1,0:T(8,128)S(1)} %convert_add_fusion.2.hidden_ref, ...), custom_call_target="tpu_custom_call" | custom-call | flops 4429185024 | bytes 24000000 | tf_op jit(solution)/shard_map/cond/branch_1_fun/feed_back/pallas_call | solution.py:613
  255.8 2.6 convolution_convert_fusion.5.grad_ref
  258.4 11.0 %causal_attention_back.3 = bf16[256,3072]{1,0:T(8,128)(2,1)S(1)} custom-call(bf16[256,3072]{1,0:T(8,128)(2,1)S(1)} %copy-done.3, bf16[256,3072]{1,0:T(8,128)(2,1)S(1)} %copy-done.3, bf16[256,3072]{1,0:T(8,128)(2,1)S(1)} %copy-done.3, bf16[256,1024]{1,0:T(8,128)(2,1)S(1)} %convolution_convert_fusion.5.grad_ref), custom_call_target="tpu_custom_call" | custom-call | flops 4000000000 | bytes 4000000 | tf_op jit(solution)/shard_map/cond/branch_1_fun/causal_attention_back/pallas_call | solution.py:483
  269.5 5.4 fusion.50
  275.4 12.6 %feed_back.7 = (f32[256,1024]{1,0:T(8,128)S(1)}, bf16[256,1024]{1,0:T(8,128)(2,1)S(1)}, bf16[256,1024]{1,0:T(8,128)(2,1)}, bf16[256,5632]{1,0:T(8,128)(2,1)}, f32[1,1024]{1,0:T(1,128)S(1)}) custom-call(f32[256,1024]{1,0:T(8,128)S(1)} %get-tuple-element.432.grad_ref, f32[256,1024]{1,0:T(8,128)S(1)} %convolution_add_fusion.1.hidden_ref, ...), custom_call_target="tpu_custom_call" | custom-call | flops 4429185024 | bytes 24000000 | tf_op jit(solution)/shard_map/cond/branch_1_fun/feed_back/pallas_call | solution.py:613
  288.1 2.5 convolution_convert_fusion.4.grad_ref
  290.6 7.9 %patch_attention_back.3 = (bf16[256,1024]{1,0:T(8,128)(2,1)S(1)}, bf16[1024,2048]{1,0:T(8,128)(2,1)}) custom-call(s32[1,1024]{1,0:T(1,128)S(1)} %bitcast.175, s32[1024,1]{1,0:T(8,128)S(1)} %copy.34.patch_col_ref, bf16[256,1024]{1,0:T(8,128)(2,1)S(1)} %fusion.41.query_ref, bf16[1024,2048]{1,0:T(8,128)(2,1)S(1)} %copy-done.7, ...), custom_call_target="tpu_custom_call" | custom-call | flops 6000000000 | bytes 10000000 | tf_op jit(solution)/shard_map/cond/branch_1_fun/patch_attention_back/pallas_call | solution.py:391
  298.5 2.7 multiply_reduce_fusion.3
  302.0 1.7 copy-done.9
  303.7 9.1 %byte_grads.3 = bf16[1024,1024]{1,0:T(8,128)(2,1)} custom-call(s32[1024,1]{1,0:T(8,128)S(1)} %copy.34.patch_col_ref, bf16[256,1024]{1,0:T(8,128)(2,1)S(1)} %divide_convert_fusion.1.grad_ref, bf16[1024,2048]{1,0:T(8,128)(2,1)S(1)} %copy-done.9, bf16[1024,2048]{1,0:T(8,128)(2,1)S(1)} %copy-done.9, bf16[1024,3072]{1,0:T(8,128)(2,1)} %get-tuple-element.185.w_key_ref.w_value_ref, ...), custom_call_target="tpu_custom_call" | custom-call | flops 5368709120 | bytes 11000000 | tf_op jit(solution)/shard_map/cond/branch_1_fun/byte_grads/pallas_call | solution.py:645
  312.8 1.4 fusion.54
  314.3 0.8 copy.41
  315.3 333.2 %backward_sums.1 = (bf16[2,64,6272]{2,1,0:T(8,128)(2,1)}, bf16[64,6272]{1,0:T(8,128)(2,1)}, bf16[16,32,512]{2,1,0:T(8,128)(2,1)}, bf16[3,2048,512]{2,1,0:T(8,128...) custom-call(bf16[256,1024]{1,0:T(8,128)(2,1)} %get-tuple-element.302, ...), custom_call_target="tpu_custom_call" | custom-call | flops 49999998976 | bytes 600000000 | tf_op jit(solution)/shard_map/backward_sums/pallas_call | solution.py:1194
  648.5 1.6 fusion.58
  650.1 0.8 slice.133
  651.0 0.8 slice.134
  651.7 0.9 slice.132
  653.3 0.9 slice_convert_fusion
  657.3 1.1 convert_reduce_fusion.1
  658.6 1.1 select_bitcast_fusion
  659.9 0.9 maximum_bitcast_fusion.1
  660.8 1.2 maximum_bitcast_fusion
  662.0 35.9 %place_rows.1 = f32[3,8192,512]{2,1,0:T(8,128)} custom-call(s32[27]{0:T(128)S(1)} %reshape.241.starts_ref, s32[3,1,2048]{2,1,0:T(1,128)S(1)} %copy-done.46, bf16[3,2048,512]{2,1,0:T(8,128)(2,1)} %get-tuple-element.298.rows_ref), custom_call_target="tpu_custom_call" | custom-call | flops 10000000000 | bytes 60000000 | tf_op jit(solution)/shard_map/place_rows/pallas_call | solution.py:1141
  698.6 0.7 maximum_bitcast_fusion.2
  700.7 1.1 maximum_select_fusion
  (136 shorter events, 14.2 us)
Async XLA Ops:
  7.2 6.9 copy-start.54
  7.2 8.1 %copy-start.48 = (bf16[1,2,1024]{2,1,0:T(2,128)(2,1)S(1)}, bf16[1,2,1024]{2,1,0:T(2,128)(2,1)}, u32[]{:S(2)}) copy-start(bf16[1,2,1024]{2,1,0:T(2,128)(2,1)} %param.20) | copy-start | bytes 12292
  7.2 9.9 %copy-start.43 = (bf16[260,512]{1,0:T(8,128)(2,1)S(1)}, bf16[260,512]{1,0:T(8,128)(2,1)}, u32[]{:S(2)}) copy-start(bf16[260,512]{1,0:T(8,128)(2,1)} %param.18) | copy-start | bytes 798724
  7.2 12.8 %sort.35.cloned.1.call-start = ((), (), s32[]{:S(2)}) async-start(), calls=%async_computation.2 | async-start | bytes 196640 | tf_op jit(solution)/shard_map/sort | solution.py:1273
  8.4 168.7 %collective-permute-start = (bf16[256,1024]{1,0:T(8,128)(2,1)S(1)}, bf16[256,1024]{1,0:T(8,128)(2,1)S(1)}, u32[]{:S(2)}, u32[]{:S(2)}) collective-permute-start(bf16[256,1024]{1,0:T(8,128)(2,1)S(1)} %dynamic-slice_bitcast_fusion), channel_id=1, source_target_pairs={{0,16},{16,0},{1,17},{17,1},{2,18},{18,2},{3,19},{19,3},{4,20},{20... | collective-permute-start | bytes 1572872 | tf_op jit(solution)/shard_map/ppermute | solution.py:1244
  12.7 164.4 %copy-start.47 = (s32[1,1,2,1024]{3,1,2,0:T(1,128)}, s32[1,1,2,1024]{3,1,2,0:T(1,128)S(1)}, u32[]{:S(2)}) copy-start(s32[1,1,2,1024]{3,1,2,0:T(1,128)S(1)} %copy.43) | copy-start | bytes 24580
  21.4 155.7 %copy-start.38 = (bf16[1,2,256,1024]{3,2,1,0:T(8,128)(2,1)S(1)}, bf16[1,2,256,1024]{3,2,1,0:T(8,128)(2,1)}, u32[]{:S(2)}) copy-start(bf16[1,2,256,1024]{3,2,1,0:T(8,128)(2,1)} %param.25) | copy-start | bytes 3145732
  186.4 126.4 %sort.33.cloned.1.call-start = ((), (), s32[]{:S(2)}) async-start(), calls=%async_computation.1 | async-start | bytes 98336 | tf_op jit(solution)/shard_map/cond/branch_1_fun/sort | solution.py:1351
  187.2 3.4 copy-start.16
  189.8 17.9 %copy-start.21 = (f32[256,1024]{1,0:T(8,128)}, f32[256,1024]{1,0:T(8,128)S(1)}, u32[]{:S(2)}) copy-start(f32[256,1024]{1,0:T(8,128)S(1)} %get-tuple-element.457) | copy-start | bytes 3145732 | tf_op jit(solution)/shard_map/conditional.1
  198.4 0.8 copy-start.42
  199.4 2.2 copy-start.6
  201.6 6.0 copy-start.25
  207.7 0.8 copy-start.30
  208.5 10.3 %copy-start.15 = (f32[256,1024]{1,0:T(8,128)S(1)}, f32[256,1024]{1,0:T(8,128)}, u32[]{:S(2)}) copy-start(f32[256,1024]{1,0:T(8,128)} %get-tuple-element.196) | copy-start | bytes 3145732 | tf_op jit(solution)/shard_map/conditional.1
  208.5 10.3 %copy-start.22 = (f32[256,1024]{1,0:T(8,128)S(1)}, f32[256,1024]{1,0:T(8,128)}, u32[]{:S(2)}) copy-start(f32[256,1024]{1,0:T(8,128)} %copy-done.21) | copy-start | bytes 3145732 | tf_op jit(solution)/shard_map/conditional.1
  219.2 82.1 %copy-start.10 = (bf16[256,1024]{1,0:T(8,128)(2,1)}, bf16[256,1024]{1,0:T(8,128)(2,1)S(1)}, u32[]{:S(2)}) copy-start(bf16[256,1024]{1,0:T(8,128)(2,1)S(1)} %get-tuple-element.496) | copy-start | bytes 1572868 | tf_op jit(solution)/shard_map/conditional.1
  219.4 4.8 copy-start.40
  224.2 8.0 %copy-start.2 = (bf16[256,3072]{1,0:T(8,128)(2,1)}, bf16[256,3072]{1,0:T(8,128)(2,1)S(1)}, u32[]{:S(2)}) copy-start(bf16[256,3072]{1,0:T(8,128)(2,1)S(1)} %convolution_convert_fusion.3.query_ref.key_ref.value_ref) | copy-start | bytes 4718596 | tf_op jit(solution)/shard_map/conditional.1
  224.2 8.0 %copy-start.27 = (bf16[1024,1024]{1,0:T(8,128)(2,1)S(1)}, bf16[1024,1024]{1,0:T(8,128)(2,1)}, u32[]{:S(2)}) copy-start(bf16[1024,1024]{1,0:T(8,128)(2,1)} %get-tuple-element.192) | copy-start | bytes 6291460 | tf_op jit(solution)/shard_map/conditional.1
  232.2 0.8 copy-start.34
  255.8 13.6 %copy-start.51 = (bf16[256,1024]{1,0:T(8,128)(2,1)}, bf16[256,1024]{1,0:T(8,128)(2,1)S(1)}, u32[]{:S(2)}) copy-start(bf16[256,1024]{1,0:T(8,128)(2,1)S(1)} %get-tuple-element.501) | copy-start | bytes 1572868 | tf_op jit(solution)/shard_map/conditional.1
  255.8 2.6 copy-start.3
  269.4 5.4 copy-start.56
  269.4 5.4 copy-start.13
  275.4 15.2 %copy-start.7 = (bf16[1024,2048]{1,0:T(8,128)(2,1)S(1)}, bf16[1024,2048]{1,0:T(8,128)(2,1)}, u32[]{:S(2)}) copy-start(bf16[1024,2048]{1,0:T(8,128)(2,1)} %fusion.30.key_ref.value_ref) | copy-start | bytes 12582916 | tf_op jit(solution)/shard_map/conditional.1
  288.1 10.4 %copy-start.53 = (bf16[256,1024]{1,0:T(8,128)(2,1)}, bf16[256,1024]{1,0:T(8,128)(2,1)S(1)}, u32[]{:S(2)}) copy-start(bf16[256,1024]{1,0:T(8,128)(2,1)S(1)} %get-tuple-element.508) | copy-start | bytes 1572868 | tf_op jit(solution)/shard_map/conditional.1
  290.6 7.9 %copy-start.23 = (f32[256,1024]{1,0:T(8,128)S(1)}, f32[256,1024]{1,0:T(8,128)}, u32[]{:S(2)}) copy-start(f32[256,1024]{1,0:T(8,128)} %copy-done.21) | copy-start | bytes 3145732 | tf_op jit(solution)/shard_map/conditional.1
  298.5 2.8 copy-start.57
  301.5 2.2 copy-start.9
  303.7 11.4 %copy-start.11 = (bf16[256,1024]{1,0:T(8,128)(2,1)S(1)}, bf16[256,1024]{1,0:T(8,128)(2,1)}, u32[]{:S(2)}) copy-start(bf16[256,1024]{1,0:T(8,128)(2,1)} %copy-done.10) | copy-start | bytes 1572868 | tf_op jit(solution)/shard_map/conditional.1
  303.7 11.4 %copy-start.35 = (bf16[256,1024]{1,0:T(8,128)(2,1)S(1)}, bf16[256,1024]{1,0:T(8,128)(2,1)}, u32[]{:S(2)}) copy-start(bf16[256,1024]{1,0:T(8,128)(2,1)} %copy-done.34) | copy-start | bytes 1572868 | tf_op jit(solution)/shard_map/conditional.1
  303.7 11.4 %copy-start.58 = (bf16[256,1024]{1,0:T(8,128)(2,1)S(1)}, bf16[256,1024]{1,0:T(8,128)(2,1)}, u32[]{:S(2)}) copy-start(bf16[256,1024]{1,0:T(8,128)(2,1)} %copy-done.57) | copy-start | bytes 1572868 | tf_op jit(solution)/shard_map/conditional.1
  315.3 333.2 %copy-start.31 = (bf16[256,1024]{1,0:T(8,128)(2,1)}, bf16[256,1024]{1,0:T(8,128)(2,1)S(1)}, u32[]{:S(2)}) copy-start(bf16[256,1024]{1,0:T(8,128)(2,1)S(1)} %get-tuple-element.301) | copy-start | bytes 1572868
  315.3 333.2 %copy-start.45 = (s32[3,1,2048]{2,1,0:T(1,128)}, s32[3,1,2048]{2,1,0:T(1,128)S(1)}, u32[]{:S(2)}) copy-start(s32[3,1,2048]{2,1,0:T(1,128)S(1)} %get-tuple-element.419.ids_ref) | copy-start | bytes 73732
  650.9 2.4 copy-start.44
  651.7 5.6 copy-start.49
  651.7 6.8 copy-start.32
  656.8 42.5 %collective-permute-start.2 = (bf16[2,2,1024]{2,1,0:T(2,128)(2,1)S(1)}, bf16[2,2,1024]{2,1,0:T(2,128)(2,1)}, u32[]{:S(2)}, u32[]{:S(2)}) collective-permute-start(bf16[2,2,1024]{2,1,0:T(2,128)(2,1)S(1)} %reshape.242), channel_id=1, source_target_pairs={{0,16},{16,0},{1,17},{17,1},{2,18},{18,2},{3,19},{19,3},{4,20},{20... | collective-permute-start | bytes 24584 | tf_op jit(solution)/shard_map/ppermute | solution.py:1244
  658.5 1.2 copy-start.36
  658.5 1.4 copy-start.37
  658.5 2.3 copy-start.28
  659.6 2.4 copy-start.46
  659.6 41.0 %collective-permute-start.1 = (bf16[256,1024]{1,0:T(8,128)(2,1)}, bf16[256,1024]{1,0:T(8,128)(2,1)S(1)}, u32[]{:S(2)}, u32[]{:S(2)}) collective-permute-start(bf16[256,1024]{1,0:T(8,128)(2,1)} %get-tuple-element.469), channel_id=1, source_target_pairs={{0,16},{16,0},{1,17},{17,1},{2,18},{18,2},{3,19},{19,3},{4,20},{20... | collective-permute-start | bytes 1572872 | tf_op jit(solution)/shard_map/ppermute | solution.py:1244
  662.0 38.6 %copy-start.33 = (bf16[1,1,256,1024]{3,2,1,0:T(8,128)(2,1)S(1)}, bf16[1,1,256,1024]{3,2,1,0:T(8,128)(2,1)}, u32[]{:S(2)}) copy-start(bf16[1,1,256,1024]{3,2,1,0:T(8,128)(2,1)} %get-tuple-element.468) | copy-start | bytes 1572868
Sparse Core Ops, SparseCore 0:
  11.1 8.7 sort.41.cloned.1.call-done
  189.7 7.7 sort.39.cloned.1.call-done
  (2 shorter events, 0.0 us)

commit v6 on v5

--- a/solution.py
+++ b/solution.py
@@ -1118,18 +1118,26 @@
 
 def place_kernel(starts_ref, ids_ref, rows_ref, out_ref):
     table, tile = pl.program_id(0), pl.program_id(1)
-    height, window = out_ref.shape[1], 256
+    height, window, align = out_ref.shape[1], 256, 128
+    count = rows_ref.shape[1]
     at = table * (pl.num_programs(1) + 1) + tile
+    first = starts_ref[at] // align * align
     places = tile * height + lax.broadcasted_iota(jnp.int32, (height, window), 0)
-    out_ref[...] = jnp.zeros(out_ref.shape, f32)
+    lanes = lax.broadcasted_iota(jnp.int32, (height, window), 1)
+
+    def placed(index):
+        wanted = first + index * window
+        begin = pl.multiple_of(jnp.minimum(wanted, count - window), align)
+        part = pl.ds(begin, window)
+        chosen = (places == ids_ref[0, :, part]) & (lanes >= wanted - begin)
+        return dot(chosen.astype(f32).astype(bf16), rows_ref[0, part, :])
 
     def body(index, carry):
-        part = pl.ds(pl.multiple_of(index * window, window), window)
-        chosen = (places == ids_ref[0, :, part]).astype(f32).astype(bf16)
-        out_ref[0] += dot(chosen, rows_ref[0, part, :])
+        out_ref[0] += placed(index)
         return carry
 
-    lax.fori_loop(starts_ref[at] // window, (starts_ref[at + 1] + window - 1) // window, body, 0)
+    out_ref[0] = placed(0)
+    lax.fori_loop(1, (starts_ref[at + 1] - first + window - 1) // window, body, 0)
 
 
 def place_rows(ids, rows, shard_rows):

time: 719 us -> 717 us (level)
  no operation moved by 1% of the time
where the time goes in v6:
time: 717 us; the launch traced here: 706 us
  Pallas kernels  610 us (85%)
  matrix products  30.4 us (4%)
  local copies, waits for them, and re-layouts  20.8 us (3%)
  other arithmetic  19.4 us (3%)
  between operations  14.4 us (2%)
  loops' own time  8.5 us (1%)
    pallas_call x1, Pallas kernels, backward_sums(): pl.pallas_call(functools.partial(backward_kernel, devices, table_rows, co...  333 us
    pallas_call x1, Pallas kernels, gather_rows(): pl.pallas_call(functools.partial(gather_kernel, devices), in_specs=[vmem,...  156 us
    pallas_call x1, Pallas kernels, place_rows(): pl.pallas_call(place_kernel, grid_spec=pltpu.PrefetchScalarGridSpec(num_s...  32.9 us
    pallas_call x2, Pallas kernels, feed_back(): pl.pallas_call(feed_back_kernel, grid=(tiles,), in_specs=[whole, whole, r...  24.9 us
    pallas_call x2, Pallas kernels, feed_forward(): pl.pallas_call(feed_kernel, grid=(tiles,), in_specs=[whole, row, gate, up...  20.9 us
    dot_general x6, matrix products, dot(): return jnp.dot(left, right, preferred_element_type=f32)  17.1 us
  transfers between devices with their start and end apart: 3, of which 0 were waited for; matrix products, arithmetic and copies ran while one was open for 2% of the time, Pallas kernels for 27%

profile of v6, /device:TPU:0, one launch (start us, length us, event | category | flops | bytes accessed | tf_op | source)
XLA Modules:
  0.0 706.1 jit_solution(6544039877132237725)
XLA Ops:
  7.3 1.1 dynamic-slice_bitcast_fusion
  8.9 0.8 copy.42
  12.0 0.7 copy.43
  12.7 1.3 copy.44
  15.3 1.8 all_gather.3
  17.1 0.8 pad.10.refs_4_
  18.4 1.6 sort.35.cloned.1.call-done
  20.1 1.4 fusion.64.refs_2_.refs_19_
  21.5 155.6 %gather_rows.1 = (bf16[1024,1024]{1,0:T(8,128)(2,1)}, s32[16,3,128]{2,1,0:T(4,128)S(1)}, bf16[1024,3072]{1,0:T(8,128)(2,1)}, bf16[1024,1024]{1,0:T(8,128)(2,1)},...) custom-call(s32[16,3,128]{2,1,0:T(4,128)} %bitcast.205, bf16[3,8192,512]{2,1,0:T(8,128)(2,1)} %refs_1_.1, ...), custom_call_target="tpu_custom_call" | custom-call | flops 49999998976 | bytes 400000000 | tf_op jit(solution)/shard_map/gather_rows/pallas_call | solution.py:239
  177.1 1.5 fusion.60
  178.6 136.7 %conditional.3 = (bf16[256,1024]{1,0:T(8,128)(2,1)S(1)}, bf16[256,1024]{1,0:T(8,128)(2,1)S(1)}, bf16[256,1024]{1,0:T(8,128)(2,1)}, bf16[256,1024]{1,0:T(8,128)(2...) conditional(s32[]{:T(128)} %convert_element_type.145, ...), branch_computations={%region_4.12_spmd, %region_12.20_spmd} | conditional | flops 50378838016 | bytes 360850560
  187.2 2.5 multiply_reduce_fusion.5
  189.8 0.8 copy-done.16
  190.6 7.6 %fusion.30.key_ref.value_ref = bf16[1024,2048]{1,0:T(8,128)(2,1)} fusion(bf16[1024,1024]{1,0:T(8,128)(2,1)} %get-tuple-element.180, bf16[1024,3072]{1,0:T(8,128)(2,1)S(1)} %copy-done.16), kind=kOutput, calls=%fused_computation.59 | convolution fusion | flops 4297064448 | bytes 10485760 | tf_op jit(solution)/shard_map/cond/branch_1_fun/dot_general | solution.py:29
  198.4 0.7 fusion.41.query_ref
  199.5 2.2 copy-done.6
  201.7 6.0 patch_attention.3
  207.7 0.7 convolution_add_fusion.1.hidden_ref
  208.5 10.3 %feed_forward.6 = (f32[256,1024]{1,0:T(8,128)S(1)}, bf16[256,1024]{1,0:T(8,128)(2,1)}, bf16[256,2816]{1,0:T(8,128)(2,1)S(1)}, bf16[256,2816]{1,0:T(8,128)(2,1)S(1)}, bf16[256,2816]{1,0:T(8,128)(2,1)}) custom-call(f32[256,1024]{1,0:T(8,128)S(1)} %convolution_add_fusion.1.hidden_ref, f32[1,1024]{1,0:T(1,128)S(1)} %get-tuple-element.453.gain_ref, ...), custom_call_target="tpu_custom_call" | custom-call | flops 4429185024 | bytes 24000000 | tf_op jit(solution)/shard_map/cond/branch_1_fun/feed_forward/pallas_call | solution.py:547
  219.4 4.8 convolution_convert_fusion.3.query_ref.key_ref.value_ref
  224.2 8.0 %causal_attention.3 = bf16[256,1024]{1,0:T(8,128)(2,1)S(1)} custom-call(bf16[256,3072]{1,0:T(8,128)(2,1)S(1)} %convolution_convert_fusion.3.query_ref.key_ref.value_ref, bf16[256,3072]{1,0:T(8,128)(2,1)S(1)} %convolution_convert_fusion.3.query_ref.key_ref.value_ref, bf16[256,3072]{1,0:T(8,128)(2,1)S(1)} %convolution_convert_fusion.3.query_ref.key_ref.value_ref), custom_call_target="tpu_custom_call" | custom-call | flops 2000000000 | bytes 2000000 | tf_op jit(solution)/shard_map/cond/branch_1_fun/causal_attention/pallas_call | solution.py:442
  232.2 0.7 convert_add_fusion.2.hidden_ref
  233.0 10.6 %feed_forward.7 = (f32[256,1024]{1,0:T(8,128)S(1)}, bf16[256,1024]{1,0:T(8,128)(2,1)}, bf16[256,2816]{1,0:T(8,128)(2,1)S(1)}, bf16[256,2816]{1,0:T(8,128)(2,1)S(1)}, bf16[256,2816]{1,0:T(8,128)(2,1)}) custom-call(f32[256,1024]{1,0:T(8,128)S(1)} %convert_add_fusion.2.hidden_ref, f32[1,1024]{1,0:T(1,128)S(1)} %get-tuple-element.451.gain_ref, ...), custom_call_target="tpu_custom_call" | custom-call | flops 4429185024 | bytes 24000000 | tf_op jit(solution)/shard_map/cond/branch_1_fun/feed_forward/pallas_call | solution.py:547
  243.6 12.2 %feed_back.6 = (f32[256,1024]{1,0:T(8,128)S(1)}, bf16[256,1024]{1,0:T(8,128)(2,1)S(1)}, bf16[256,1024]{1,0:T(8,128)(2,1)}, bf16[256,5632]{1,0:T(8,128)(2,1)}, f32[1,1024]{1,0:T(1,128)S(1)}) custom-call(f32[256,1024]{1,0:T(8,128)S(1)} %get-tuple-element.455.grad_ref, f32[256,1024]{1,0:T(8,128)S(1)} %convert_add_fusion.2.hidden_ref, ...), custom_call_target="tpu_custom_call" | custom-call | flops 4429185024 | bytes 24000000 | tf_op jit(solution)/shard_map/cond/branch_1_fun/feed_back/pallas_call | solution.py:613
  255.9 2.6 convolution_convert_fusion.5.grad_ref
  258.4 11.0 %causal_attention_back.3 = bf16[256,3072]{1,0:T(8,128)(2,1)S(1)} custom-call(bf16[256,3072]{1,0:T(8,128)(2,1)S(1)} %copy-done.3, bf16[256,3072]{1,0:T(8,128)(2,1)S(1)} %copy-done.3, bf16[256,3072]{1,0:T(8,128)(2,1)S(1)} %copy-done.3, bf16[256,1024]{1,0:T(8,128)(2,1)S(1)} %convolution_convert_fusion.5.grad_ref), custom_call_target="tpu_custom_call" | custom-call | flops 4000000000 | bytes 4000000 | tf_op jit(solution)/shard_map/cond/branch_1_fun/causal_attention_back/pallas_call | solution.py:483
  269.5 5.4 fusion.50
  275.5 12.6 %feed_back.7 = (f32[256,1024]{1,0:T(8,128)S(1)}, bf16[256,1024]{1,0:T(8,128)(2,1)S(1)}, bf16[256,1024]{1,0:T(8,128)(2,1)}, bf16[256,5632]{1,0:T(8,128)(2,1)}, f32[1,1024]{1,0:T(1,128)S(1)}) custom-call(f32[256,1024]{1,0:T(8,128)S(1)} %get-tuple-element.432.grad_ref, f32[256,1024]{1,0:T(8,128)S(1)} %convolution_add_fusion.1.hidden_ref, ...), custom_call_target="tpu_custom_call" | custom-call | flops 4429185024 | bytes 24000000 | tf_op jit(solution)/shard_map/cond/branch_1_fun/feed_back/pallas_call | solution.py:613
  288.1 2.5 convolution_convert_fusion.4.grad_ref
  290.6 7.9 %patch_attention_back.3 = (bf16[256,1024]{1,0:T(8,128)(2,1)S(1)}, bf16[1024,2048]{1,0:T(8,128)(2,1)}) custom-call(s32[1,1024]{1,0:T(1,128)S(1)} %bitcast.175, s32[1024,1]{1,0:T(8,128)S(1)} %copy.34.patch_col_ref, bf16[256,1024]{1,0:T(8,128)(2,1)S(1)} %fusion.41.query_ref, bf16[1024,2048]{1,0:T(8,128)(2,1)S(1)} %copy-done.7, ...), custom_call_target="tpu_custom_call" | custom-call | flops 6000000000 | bytes 10000000 | tf_op jit(solution)/shard_map/cond/branch_1_fun/patch_attention_back/pallas_call | solution.py:391
  298.5 2.7 multiply_reduce_fusion.3
  302.0 1.7 copy-done.9
  303.7 9.1 %byte_grads.3 = bf16[1024,1024]{1,0:T(8,128)(2,1)} custom-call(s32[1024,1]{1,0:T(8,128)S(1)} %copy.34.patch_col_ref, bf16[256,1024]{1,0:T(8,128)(2,1)S(1)} %divide_convert_fusion.1.grad_ref, bf16[1024,2048]{1,0:T(8,128)(2,1)S(1)} %copy-done.9, bf16[1024,2048]{1,0:T(8,128)(2,1)S(1)} %copy-done.9, bf16[1024,3072]{1,0:T(8,128)(2,1)} %get-tuple-element.185.w_key_ref.w_value_ref, ...), custom_call_target="tpu_custom_call" | custom-call | flops 5368709120 | bytes 11000000 | tf_op jit(solution)/shard_map/cond/branch_1_fun/byte_grads/pallas_call | solution.py:645
  312.8 1.4 fusion.54
  314.3 0.8 copy.41
  315.4 333.4 %backward_sums.1 = (bf16[2,64,6272]{2,1,0:T(8,128)(2,1)}, bf16[64,6272]{1,0:T(8,128)(2,1)}, bf16[16,32,512]{2,1,0:T(8,128)(2,1)}, bf16[3,2048,512]{2,1,0:T(8,128...) custom-call(bf16[256,1024]{1,0:T(8,128)(2,1)} %get-tuple-element.302, ...), custom_call_target="tpu_custom_call" | custom-call | flops 49999998976 | bytes 600000000 | tf_op jit(solution)/shard_map/backward_sums/pallas_call | solution.py:1202
  648.8 1.6 fusion.58
  650.4 0.8 slice.133
  651.2 0.8 slice.134
  652.0 0.9 slice.132
  653.5 0.9 slice_convert_fusion
  657.5 1.1 convert_reduce_fusion.1
  658.8 1.1 select_bitcast_fusion
  660.2 0.9 maximum_bitcast_fusion.1
  661.1 1.2 maximum_bitcast_fusion
  662.3 32.9 %place_rows.1 = f32[3,8192,512]{2,1,0:T(8,128)} custom-call(s32[27]{0:T(128)S(1)} %reshape.241.starts_ref, s32[3,1,2048]{2,1,0:T(1,128)S(1)} %copy-done.46, bf16[3,2048,512]{2,1,0:T(8,128)(2,1)} %get-tuple-element.298.rows_ref), custom_call_target="tpu_custom_call" | custom-call | flops 10000000000 | bytes 60000000 | tf_op jit(solution)/shard_map/place_rows/pallas_call | solution.py:1149
  695.9 0.7 maximum_bitcast_fusion.2
  698.0 1.1 maximum_select_fusion
  (136 shorter events, 14.2 us)
Async XLA Ops:
  7.2 6.9 copy-start.54
  7.2 8.1 %copy-start.48 = (bf16[1,2,1024]{2,1,0:T(2,128)(2,1)S(1)}, bf16[1,2,1024]{2,1,0:T(2,128)(2,1)}, u32[]{:S(2)}) copy-start(bf16[1,2,1024]{2,1,0:T(2,128)(2,1)} %param.20) | copy-start | bytes 12292
  7.2 9.9 %copy-start.43 = (bf16[260,512]{1,0:T(8,128)(2,1)S(1)}, bf16[260,512]{1,0:T(8,128)(2,1)}, u32[]{:S(2)}) copy-start(bf16[260,512]{1,0:T(8,128)(2,1)} %param.18) | copy-start | bytes 798724
  7.2 12.9 %sort.35.cloned.1.call-start = ((), (), s32[]{:S(2)}) async-start(), calls=%async_computation.2 | async-start | bytes 196640 | tf_op jit(solution)/shard_map/sort | solution.py:1281
  8.4 168.7 %collective-permute-start = (bf16[256,1024]{1,0:T(8,128)(2,1)S(1)}, bf16[256,1024]{1,0:T(8,128)(2,1)S(1)}, u32[]{:S(2)}, u32[]{:S(2)}) collective-permute-start(bf16[256,1024]{1,0:T(8,128)(2,1)S(1)} %dynamic-slice_bitcast_fusion), channel_id=1, source_target_pairs={{0,16},{16,0},{1,17},{17,1},{2,18},{18,2},{3,19},{19,3},{4,20},{20... | collective-permute-start | bytes 1572872 | tf_op jit(solution)/shard_map/ppermute | solution.py:1252
  12.7 164.4 %copy-start.47 = (s32[1,1,2,1024]{3,1,2,0:T(1,128)}, s32[1,1,2,1024]{3,1,2,0:T(1,128)S(1)}, u32[]{:S(2)}) copy-start(s32[1,1,2,1024]{3,1,2,0:T(1,128)S(1)} %copy.43) | copy-start | bytes 24580
  21.5 155.7 %copy-start.38 = (bf16[1,2,256,1024]{3,2,1,0:T(8,128)(2,1)S(1)}, bf16[1,2,256,1024]{3,2,1,0:T(8,128)(2,1)}, u32[]{:S(2)}) copy-start(bf16[1,2,256,1024]{3,2,1,0:T(8,128)(2,1)} %param.25) | copy-start | bytes 3145732
  186.5 126.4 %sort.33.cloned.1.call-start = ((), (), s32[]{:S(2)}) async-start(), calls=%async_computation.1 | async-start | bytes 98336 | tf_op jit(solution)/shard_map/cond/branch_1_fun/sort | solution.py:1359
  187.2 3.4 copy-start.16
  189.8 17.9 %copy-start.21 = (f32[256,1024]{1,0:T(8,128)}, f32[256,1024]{1,0:T(8,128)S(1)}, u32[]{:S(2)}) copy-start(f32[256,1024]{1,0:T(8,128)S(1)} %get-tuple-element.457) | copy-start | bytes 3145732 | tf_op jit(solution)/shard_map/conditional.1
  198.4 0.8 copy-start.42
  199.5 2.2 copy-start.6
  201.7 6.0 copy-start.25
  207.7 0.8 copy-start.30
  208.5 10.3 %copy-start.15 = (f32[256,1024]{1,0:T(8,128)S(1)}, f32[256,1024]{1,0:T(8,128)}, u32[]{:S(2)}) copy-start(f32[256,1024]{1,0:T(8,128)} %get-tuple-element.196) | copy-start | bytes 3145732 | tf_op jit(solution)/shard_map/conditional.1
  208.5 10.3 %copy-start.22 = (f32[256,1024]{1,0:T(8,128)S(1)}, f32[256,1024]{1,0:T(8,128)}, u32[]{:S(2)}) copy-start(f32[256,1024]{1,0:T(8,128)} %copy-done.21) | copy-start | bytes 3145732 | tf_op jit(solution)/shard_map/conditional.1
  219.2 82.1 %copy-start.10 = (bf16[256,1024]{1,0:T(8,128)(2,1)}, bf16[256,1024]{1,0:T(8,128)(2,1)S(1)}, u32[]{:S(2)}) copy-start(bf16[256,1024]{1,0:T(8,128)(2,1)S(1)} %get-tuple-element.496) | copy-start | bytes 1572868 | tf_op jit(solution)/shard_map/conditional.1
  219.4 4.8 copy-start.40
  224.2 8.0 %copy-start.2 = (bf16[256,3072]{1,0:T(8,128)(2,1)}, bf16[256,3072]{1,0:T(8,128)(2,1)S(1)}, u32[]{:S(2)}) copy-start(bf16[256,3072]{1,0:T(8,128)(2,1)S(1)} %convolution_convert_fusion.3.query_ref.key_ref.value_ref) | copy-start | bytes 4718596 | tf_op jit(solution)/shard_map/conditional.1
  224.2 8.0 %copy-start.27 = (bf16[1024,1024]{1,0:T(8,128)(2,1)S(1)}, bf16[1024,1024]{1,0:T(8,128)(2,1)}, u32[]{:S(2)}) copy-start(bf16[1024,1024]{1,0:T(8,128)(2,1)} %get-tuple-element.192) | copy-start | bytes 6291460 | tf_op jit(solution)/shard_map/conditional.1
  232.2 0.8 copy-start.34
  255.9 13.6 %copy-start.51 = (bf16[256,1024]{1,0:T(8,128)(2,1)}, bf16[256,1024]{1,0:T(8,128)(2,1)S(1)}, u32[]{:S(2)}) copy-start(bf16[256,1024]{1,0:T(8,128)(2,1)S(1)} %get-tuple-element.501) | copy-start | bytes 1572868 | tf_op jit(solution)/shard_map/conditional.1
  255.9 2.6 copy-start.3
  269.5 5.4 copy-start.56
  269.5 5.4 copy-start.13
  275.4 15.2 %copy-start.7 = (bf16[1024,2048]{1,0:T(8,128)(2,1)S(1)}, bf16[1024,2048]{1,0:T(8,128)(2,1)}, u32[]{:S(2)}) copy-start(bf16[1024,2048]{1,0:T(8,128)(2,1)} %fusion.30.key_ref.value_ref) | copy-start | bytes 12582916 | tf_op jit(solution)/shard_map/conditional.1
  288.1 10.4 %copy-start.53 = (bf16[256,1024]{1,0:T(8,128)(2,1)}, bf16[256,1024]{1,0:T(8,128)(2,1)S(1)}, u32[]{:S(2)}) copy-start(bf16[256,1024]{1,0:T(8,128)(2,1)S(1)} %get-tuple-element.508) | copy-start | bytes 1572868 | tf_op jit(solution)/shard_map/conditional.1
  290.6 7.9 %copy-start.23 = (f32[256,1024]{1,0:T(8,128)S(1)}, f32[256,1024]{1,0:T(8,128)}, u32[]{:S(2)}) copy-start(f32[256,1024]{1,0:T(8,128)} %copy-done.21) | copy-start | bytes 3145732 | tf_op jit(solution)/shard_map/conditional.1
  298.5 2.8 copy-start.57
  301.5 2.2 copy-start.9
  303.7 11.4 %copy-start.11 = (bf16[256,1024]{1,0:T(8,128)(2,1)S(1)}, bf16[256,1024]{1,0:T(8,128)(2,1)}, u32[]{:S(2)}) copy-start(bf16[256,1024]{1,0:T(8,128)(2,1)} %copy-done.10) | copy-start | bytes 1572868 | tf_op jit(solution)/shard_map/conditional.1
  303.7 11.4 %copy-start.35 = (bf16[256,1024]{1,0:T(8,128)(2,1)S(1)}, bf16[256,1024]{1,0:T(8,128)(2,1)}, u32[]{:S(2)}) copy-start(bf16[256,1024]{1,0:T(8,128)(2,1)} %copy-done.34) | copy-start | bytes 1572868 | tf_op jit(solution)/shard_map/conditional.1
  303.7 11.4 %copy-start.58 = (bf16[256,1024]{1,0:T(8,128)(2,1)S(1)}, bf16[256,1024]{1,0:T(8,128)(2,1)}, u32[]{:S(2)}) copy-start(bf16[256,1024]{1,0:T(8,128)(2,1)} %copy-done.57) | copy-start | bytes 1572868 | tf_op jit(solution)/shard_map/conditional.1
  315.3 333.4 %copy-start.31 = (bf16[256,1024]{1,0:T(8,128)(2,1)}, bf16[256,1024]{1,0:T(8,128)(2,1)S(1)}, u32[]{:S(2)}) copy-start(bf16[256,1024]{1,0:T(8,128)(2,1)S(1)} %get-tuple-element.301) | copy-start | bytes 1572868
  315.4 333.4 %copy-start.45 = (s32[3,1,2048]{2,1,0:T(1,128)}, s32[3,1,2048]{2,1,0:T(1,128)S(1)}, u32[]{:S(2)}) copy-start(s32[3,1,2048]{2,1,0:T(1,128)S(1)} %get-tuple-element.419.ids_ref) | copy-start | bytes 73732
  651.1 2.4 copy-start.44
  652.0 5.6 copy-start.49
  652.0 6.8 copy-start.32
  657.1 39.5 %collective-permute-start.2 = (bf16[2,2,1024]{2,1,0:T(2,128)(2,1)S(1)}, bf16[2,2,1024]{2,1,0:T(2,128)(2,1)}, u32[]{:S(2)}, u32[]{:S(2)}) collective-permute-start(bf16[2,2,1024]{2,1,0:T(2,128)(2,1)S(1)} %reshape.242), channel_id=1, source_target_pairs={{0,16},{16,0},{1,17},{17,1},{2,18},{18,2},{3,19},{19,3},{4,20},{20... | collective-permute-start | bytes 24584 | tf_op jit(solution)/shard_map/ppermute | solution.py:1252
  658.8 1.2 copy-start.36
  658.8 1.4 copy-start.37
  658.8 2.3 copy-start.28
  659.9 2.4 copy-start.46
  659.9 38.1 %collective-permute-start.1 = (bf16[256,1024]{1,0:T(8,128)(2,1)}, bf16[256,1024]{1,0:T(8,128)(2,1)S(1)}, u32[]{:S(2)}, u32[]{:S(2)}) collective-permute-start(bf16[256,1024]{1,0:T(8,128)(2,1)} %get-tuple-element.469), channel_id=1, source_target_pairs={{0,16},{16,0},{1,17},{17,1},{2,18},{18,2},{3,19},{19,3},{4,20},{20... | collective-permute-start | bytes 1572872 | tf_op jit(solution)/shard_map/ppermute | solution.py:1252
  662.3 35.7 %copy-start.33 = (bf16[1,1,256,1024]{3,2,1,0:T(8,128)(2,1)S(1)}, bf16[1,1,256,1024]{3,2,1,0:T(8,128)(2,1)}, u32[]{:S(2)}) copy-start(bf16[1,1,256,1024]{3,2,1,0:T(8,128)(2,1)} %get-tuple-element.468) | copy-start | bytes 1572868
Sparse Core Ops, SparseCore 0:
  11.1 8.7 sort.41.cloned.1.call-done
  189.7 7.7 sort.39.cloned.1.call-done
  (2 shorter events, 0.0 us)

commit v7 on v6

--- a/solution.py
+++ b/solution.py
@@ -1162,6 +1162,34 @@
         cost_estimate=pl.CostEstimate(flops=10**10, bytes_accessed=6 * 10**7, transcendentals=0),
         name="place_rows",
     )(starts, ids[:, None, :], rows)
+
+
+def join_kernel(section_ref, sums_ref, theirs_ref, gate_up_ref, down_ref, qkv_ref, out_ref):
+    section = section_ref[0]
+    mine, theirs = sums_ref[section].astype(f32), theirs_ref[...].astype(f32)
+    lower, upper = jnp.where(section == 0, mine, theirs), jnp.where(section == 0, theirs, mine)
+    half, half_ff, rest = D // 2, FF // 2, FF + FF // 2
+    for core, part in enumerate((lower, upper)):
+        gate_up_ref[:, core * FF : (core + 1) * FF] = part[:, :FF]
+        down_ref[:, core * half_ff : (core + 1) * half_ff] = part[:, FF:rest]
+        for index in range(3):
+            first = index * D + core * half
+            qkv_ref[:, first : first + half] = part[:, rest + index * half : rest + (index + 1) * half]
+        out_ref[:, core * half : (core + 1) * half] = part[:, rest + 3 * half :]
+
+
+def join_sums(section, sums, theirs):
+    rows = theirs.shape[0]
+    vmem = pl.BlockSpec(memory_space=pltpu.VMEM)
+    return pl.pallas_call(
+        join_kernel,
+        in_specs=[pl.BlockSpec(memory_space=pltpu.SMEM), vmem, vmem],
+        out_specs=[vmem] * 4,
+        out_shape=[jax.ShapeDtypeStruct((rows, width), f32) for width in (2 * FF, FF, 3 * D, D)],
+        compiler_params=pltpu.CompilerParams(vmem_limit_bytes=VMEM_BYTES),
+        cost_estimate=pl.CostEstimate(flops=10**6, bytes_accessed=8 * 10**6, transcendentals=0),
+        name="join_sums",
+    )(section.reshape(1).astype(jnp.int32), sums, theirs)
 
 
 def table_block_rows(devices, table_rows):
@@ -1396,19 +1424,8 @@
     gains_grad = lax.dynamic_index_in_dim(gain_sums, section, 0, keepdims=True)
     gains_grad = lax.dynamic_index_in_dim(gains_grad, lax.axis_index("rows"), 2, keepdims=False)
 
-    mine = lax.dynamic_index_in_dim(sums, section, 0, keepdims=False)
-    lower = jnp.where(first_core, mine, theirs).astype(f32)
-    upper = jnp.where(first_core, theirs, mine).astype(f32)
-    half, half_ff = D // 2, FF // 2
-    gate_up_grad = jnp.concatenate([lower[:, :FF], upper[:, :FF]], axis=1)
-    down_grad = jnp.concatenate([lower[:, FF : FF + half_ff], upper[:, FF : FF + half_ff]], axis=1).T
-    low_rest, high_rest = lower[:, FF + half_ff :], upper[:, FF + half_ff :]
-    columns = []
-    for index in range(4):
-        part = slice(index * half, (index + 1) * half)
-        columns.append(jnp.concatenate([low_rest[:, part], high_rest[:, part]], axis=1))
-    qkv_grad = jnp.concatenate(columns[:3], axis=1)
-    out_grad = columns[3]
+    gate_up_grad, down_grad, qkv_grad, out_grad = join_sums(section, sums, theirs)
+    down_grad = down_grad.T
 
     return (
         section_out,

time: 717 us -> 706 us (0.985)
  no operation moved by 1% of the time
where the time goes in v7:
time: 706 us; the launch traced here: 693 us
  Pallas kernels  608 us (86%)
  matrix products  30.4 us (4%)
  local copies, waits for them, and re-layouts  14.8 us (2%)
  between operations  14.4 us (2%)
  other arithmetic  13.3 us (2%)
  loops' own time  8.5 us (1%)
    pallas_call x1, Pallas kernels, backward_sums(): pl.pallas_call(functools.partial(backward_kernel, devices, table_rows, co...  333 us
    pallas_call x1, Pallas kernels, gather_rows(): pl.pallas_call(functools.partial(gather_kernel, devices), in_specs=[vmem,...  156 us
    pallas_call x1, Pallas kernels, place_rows(): pl.pallas_call(place_kernel, grid_spec=pltpu.PrefetchScalarGridSpec(num_s...  30 us
    pallas_call x2, Pallas kernels, feed_back(): pl.pallas_call(feed_back_kernel, grid=(tiles,), in_specs=[whole, whole, r...  24.9 us
    pallas_call x2, Pallas kernels, feed_forward(): pl.pallas_call(feed_kernel, grid=(tiles,), in_specs=[whole, row, gate, up...  21 us
    dot_general x6, matrix products, dot(): return jnp.dot(left, right, preferred_element_type=f32)  17.1 us
  transfers between devices with their start and end apart: 3, of which 0 were waited for; matrix products, arithmetic and copies ran while one was open for 2% of the time, Pallas kernels for 27%

profile of v7, /device:TPU:0, one launch (start us, length us, event | category | flops | bytes accessed | tf_op | source)
XLA Modules:
  0.0 692.7 jit_solution(2275107884450969459)
XLA Ops:
  7.2 1.1 dynamic-slice_bitcast_fusion
  8.9 0.8 copy.42
  9.6 0.7 add_select_fusion.5
  10.4 0.7 convert_bitcast_fusion
  12.0 1.2 dynamic_slice.22
  13.2 0.7 iota_compare_fusion.2
  13.9 0.7 copy.43
  14.6 1.3 copy.44
  15.9 1.8 all_gather.3
  17.8 0.8 pad.10.refs_4_
  19.1 1.0 sort.35.cloned.1.call-done
  20.0 1.4 fusion.62.refs_2_.refs_19_
  21.4 155.6 %gather_rows.1 = (bf16[1024,1024]{1,0:T(8,128)(2,1)}, s32[16,3,128]{2,1,0:T(4,128)S(1)}, bf16[1024,3072]{1,0:T(8,128)(2,1)}, bf16[1024,1024]{1,0:T(8,128)(2,1)},...) custom-call(s32[16,3,128]{2,1,0:T(4,128)} %bitcast.200, bf16[3,8192,512]{2,1,0:T(8,128)(2,1)} %refs_1_.1, ...), custom_call_target="tpu_custom_call" | custom-call | flops 49999998976 | bytes 400000000 | tf_op jit(solution)/shard_map/gather_rows/pallas_call | solution.py:239
  177.1 1.5 fusion.58
  178.6 136.7 %conditional.3 = (bf16[256,1024]{1,0:T(8,128)(2,1)S(1)}, bf16[256,1024]{1,0:T(8,128)(2,1)S(1)}, bf16[256,1024]{1,0:T(8,128)(2,1)}, bf16[256,1024]{1,0:T(8,128)(2...) conditional(s32[]{:T(128)} %convert_element_type.139, ...), branch_computations={%region_4.12_spmd, %region_12.20_spmd} | conditional | flops 50378838016 | bytes 360850560
  186.4 0.6 bitcast_add_fusion.1
  187.2 2.5 multiply_reduce_fusion.5
  189.7 0.8 copy-done.18
  190.6 7.6 %fusion.30.key_ref.value_ref = bf16[1024,2048]{1,0:T(8,128)(2,1)} fusion(bf16[1024,1024]{1,0:T(8,128)(2,1)} %get-tuple-element.180, bf16[1024,3072]{1,0:T(8,128)(2,1)S(1)} %copy-done.18), kind=kOutput, calls=%fused_computation.59 | convolution fusion | flops 4297064448 | bytes 10485760 | tf_op jit(solution)/shard_map/cond/branch_1_fun/dot_general | solution.py:29
  198.4 0.7 fusion.41.query_ref
  199.4 2.2 copy-done.8
  201.6 6.0 patch_attention.3
  207.6 0.7 convolution_add_fusion.1.hidden_ref
  208.4 10.3 %feed_forward.6 = (f32[256,1024]{1,0:T(8,128)S(1)}, bf16[256,1024]{1,0:T(8,128)(2,1)}, bf16[256,2816]{1,0:T(8,128)(2,1)S(1)}, bf16[256,2816]{1,0:T(8,128)(2,1)S(1)}, bf16[256,2816]{1,0:T(8,128)(2,1)}) custom-call(f32[256,1024]{1,0:T(8,128)S(1)} %convolution_add_fusion.1.hidden_ref, f32[1,1024]{1,0:T(1,128)S(1)} %get-tuple-element.461.gain_ref, ...), custom_call_target="tpu_custom_call" | custom-call | flops 4429185024 | bytes 24000000 | tf_op jit(solution)/shard_map/cond/branch_1_fun/feed_forward/pallas_call | solution.py:547
  219.3 4.8 convolution_convert_fusion.3.query_ref.key_ref.value_ref
  224.1 8.0 %causal_attention.3 = bf16[256,1024]{1,0:T(8,128)(2,1)S(1)} custom-call(bf16[256,3072]{1,0:T(8,128)(2,1)S(1)} %convolution_convert_fusion.3.query_ref.key_ref.value_ref, bf16[256,3072]{1,0:T(8,128)(2,1)S(1)} %convolution_convert_fusion.3.query_ref.key_ref.value_ref, bf16[256,3072]{1,0:T(8,128)(2,1)S(1)} %convolution_convert_fusion.3.query_ref.key_ref.value_ref), custom_call_target="tpu_custom_call" | custom-call | flops 2000000000 | bytes 2000000 | tf_op jit(solution)/shard_map/cond/branch_1_fun/causal_attention/pallas_call | solution.py:442
  232.1 0.7 convert_add_fusion.2.hidden_ref
  232.9 10.6 %feed_forward.7 = (f32[256,1024]{1,0:T(8,128)S(1)}, bf16[256,1024]{1,0:T(8,128)(2,1)}, bf16[256,2816]{1,0:T(8,128)(2,1)S(1)}, bf16[256,2816]{1,0:T(8,128)(2,1)S(1)}, bf16[256,2816]{1,0:T(8,128)(2,1)}) custom-call(f32[256,1024]{1,0:T(8,128)S(1)} %convert_add_fusion.2.hidden_ref, f32[1,1024]{1,0:T(1,128)S(1)} %get-tuple-element.459.gain_ref, ...), custom_call_target="tpu_custom_call" | custom-call | flops 4429185024 | bytes 24000000 | tf_op jit(solution)/shard_map/cond/branch_1_fun/feed_forward/pallas_call | solution.py:547
  243.6 12.2 %feed_back.6 = (f32[256,1024]{1,0:T(8,128)S(1)}, bf16[256,1024]{1,0:T(8,128)(2,1)S(1)}, bf16[256,1024]{1,0:T(8,128)(2,1)}, bf16[256,5632]{1,0:T(8,128)(2,1)}, f32[1,1024]{1,0:T(1,128)S(1)}) custom-call(f32[256,1024]{1,0:T(8,128)S(1)} %get-tuple-element.463.grad_ref, f32[256,1024]{1,0:T(8,128)S(1)} %convert_add_fusion.2.hidden_ref, ...), custom_call_target="tpu_custom_call" | custom-call | flops 4429185024 | bytes 24000000 | tf_op jit(solution)/shard_map/cond/branch_1_fun/feed_back/pallas_call | solution.py:613
  255.8 2.6 convolution_convert_fusion.5.grad_ref
  258.4 11.0 %causal_attention_back.3 = bf16[256,3072]{1,0:T(8,128)(2,1)S(1)} custom-call(bf16[256,3072]{1,0:T(8,128)(2,1)S(1)} %copy-done.5, bf16[256,3072]{1,0:T(8,128)(2,1)S(1)} %copy-done.5, bf16[256,3072]{1,0:T(8,128)(2,1)S(1)} %copy-done.5, bf16[256,1024]{1,0:T(8,128)(2,1)S(1)} %convolution_convert_fusion.5.grad_ref), custom_call_target="tpu_custom_call" | custom-call | flops 4000000000 | bytes 4000000 | tf_op jit(solution)/shard_map/cond/branch_1_fun/causal_attention_back/pallas_call | solution.py:483
  269.4 5.4 fusion.50
  275.4 12.6 %feed_back.7 = (f32[256,1024]{1,0:T(8,128)S(1)}, bf16[256,1024]{1,0:T(8,128)(2,1)S(1)}, bf16[256,1024]{1,0:T(8,128)(2,1)}, bf16[256,5632]{1,0:T(8,128)(2,1)}, f32[1,1024]{1,0:T(1,128)S(1)}) custom-call(f32[256,1024]{1,0:T(8,128)S(1)} %get-tuple-element.440.grad_ref, f32[256,1024]{1,0:T(8,128)S(1)} %convolution_add_fusion.1.hidden_ref, ...), custom_call_target="tpu_custom_call" | custom-call | flops 4429185024 | bytes 24000000 | tf_op jit(solution)/shard_map/cond/branch_1_fun/feed_back/pallas_call | solution.py:613
  288.0 2.5 convolution_convert_fusion.4.grad_ref
  290.6 7.9 %patch_attention_back.3 = (bf16[256,1024]{1,0:T(8,128)(2,1)S(1)}, bf16[1024,2048]{1,0:T(8,128)(2,1)}) custom-call(s32[1,1024]{1,0:T(1,128)S(1)} %bitcast.166, s32[1024,1]{1,0:T(8,128)S(1)} %copy.34.patch_col_ref, bf16[256,1024]{1,0:T(8,128)(2,1)S(1)} %fusion.41.query_ref, bf16[1024,2048]{1,0:T(8,128)(2,1)S(1)} %copy-done.9, ...), custom_call_target="tpu_custom_call" | custom-call | flops 6000000000 | bytes 10000000 | tf_op jit(solution)/shard_map/cond/branch_1_fun/patch_attention_back/pallas_call | solution.py:391
  298.5 2.7 multiply_reduce_fusion.3
  301.9 1.7 copy-done.11
  303.6 9.1 %byte_grads.3 = bf16[1024,1024]{1,0:T(8,128)(2,1)} custom-call(s32[1024,1]{1,0:T(8,128)S(1)} %copy.34.patch_col_ref, bf16[256,1024]{1,0:T(8,128)(2,1)S(1)} %divide_convert_fusion.1.grad_ref, bf16[1024,2048]{1,0:T(8,128)(2,1)S(1)} %copy-done.11, bf16[1024,2048]{1,0:T(8,128)(2,1)S(1)} %copy-done.11, ...), custom_call_target="tpu_custom_call" | custom-call | flops 5368709120 | bytes 11000000 | tf_op jit(solution)/shard_map/cond/branch_1_fun/byte_grads/pallas_call | solution.py:645
  312.8 1.4 fusion.54
  314.2 0.8 copy.41
  315.3 333.3 %backward_sums.1 = (bf16[2,64,6272]{2,1,0:T(8,128)(2,1)}, bf16[64,6272]{1,0:T(8,128)(2,1)}, bf16[16,32,512]{2,1,0:T(8,128)(2,1)}, bf16[3,2048,512]{2,1,0:T(8,128...) custom-call(bf16[256,1024]{1,0:T(8,128)(2,1)} %get-tuple-element.310, ...), custom_call_target="tpu_custom_call" | custom-call | flops 49999998976 | bytes 600000000 | tf_op jit(solution)/shard_map/backward_sums/pallas_call | solution.py:1230
  648.5 0.7 slice.64
  649.7 1.1 convert_reduce_fusion.1
  651.3 30.0 %place_rows.1 = f32[3,8192,512]{2,1,0:T(8,128)} custom-call(s32[27]{0:T(128)S(1)} %reshape.244.starts_ref, s32[3,1,2048]{2,1,0:T(1,128)S(1)} %get-tuple-element.427.ids_ref, bf16[3,2048,512]{2,1,0:T(8,128)(2,1)} %get-tuple-element.302.rows_ref), custom_call_target="tpu_custom_call" | custom-call | flops 10000000000 | bytes 60000000 | tf_op jit(solution)/shard_map/place_rows/pallas_call | solution.py:1149
  681.3 0.9 slice_convert_fusion
  682.1 1.8 join_sums.1
  684.0 0.6 constant_dynamic-slice_fusion
  684.6 1.1 maximum_select_fusion
  (109 shorter events, 5.6 us)
Async XLA Ops:
  7.2 8.8 %copy-start.42 = (bf16[1,2,1024]{2,1,0:T(2,128)(2,1)S(1)}, bf16[1,2,1024]{2,1,0:T(2,128)(2,1)}, u32[]{:S(2)}) copy-start(bf16[1,2,1024]{2,1,0:T(2,128)(2,1)} %param.20) | copy-start | bytes 12292
  7.2 10.6 %copy-start.39 = (bf16[260,512]{1,0:T(8,128)(2,1)S(1)}, bf16[260,512]{1,0:T(8,128)(2,1)}, u32[]{:S(2)}) copy-start(bf16[260,512]{1,0:T(8,128)(2,1)} %param.18) | copy-start | bytes 798724
  7.2 12.8 %sort.35.cloned.1.call-start = ((), (), s32[]{:S(2)}) async-start(), calls=%async_computation.2 | async-start | bytes 196640 | tf_op jit(solution)/shard_map/sort | solution.py:1309
  8.4 168.7 %collective-permute-start = (bf16[256,1024]{1,0:T(8,128)(2,1)S(1)}, bf16[256,1024]{1,0:T(8,128)(2,1)S(1)}, u32[]{:S(2)}, u32[]{:S(2)}) collective-permute-start(bf16[256,1024]{1,0:T(8,128)(2,1)S(1)} %dynamic-slice_bitcast_fusion), channel_id=1, source_target_pairs={{0,16},{16,0},{1,17},{17,1},{2,18},{18,2},{3,19},{19,3},{4,20},{20... | collective-permute-start | bytes 1572872 | tf_op jit(solution)/shard_map/ppermute | solution.py:1280
  14.6 162.5 %copy-start.41 = (s32[1,1,2,1024]{3,1,2,0:T(1,128)}, s32[1,1,2,1024]{3,1,2,0:T(1,128)S(1)}, u32[]{:S(2)}) copy-start(s32[1,1,2,1024]{3,1,2,0:T(1,128)S(1)} %copy.43) | copy-start | bytes 24580
  21.4 155.6 %copy-start.34 = (bf16[1,2,256,1024]{3,2,1,0:T(8,128)(2,1)S(1)}, bf16[1,2,256,1024]{3,2,1,0:T(8,128)(2,1)}, u32[]{:S(2)}) copy-start(bf16[1,2,256,1024]{3,2,1,0:T(8,128)(2,1)} %param.25) | copy-start | bytes 3145732
  186.4 126.4 %sort.33.cloned.1.call-start = ((), (), s32[]{:S(2)}) async-start(), calls=%async_computation.1 | async-start | bytes 98336 | tf_op jit(solution)/shard_map/cond/branch_1_fun/sort | solution.py:1387
  187.2 3.4 copy-start.18
  189.7 17.9 %copy-start.23 = (f32[256,1024]{1,0:T(8,128)}, f32[256,1024]{1,0:T(8,128)S(1)}, u32[]{:S(2)}) copy-start(f32[256,1024]{1,0:T(8,128)S(1)} %get-tuple-element.465) | copy-start | bytes 3145732 | tf_op jit(solution)/shard_map/conditional.1
  198.4 0.8 copy-start.38
  199.4 2.2 copy-start.8
  201.6 6.0 copy-start.27
  207.6 0.8 copy-start.31
  208.4 10.3 %copy-start.17 = (f32[256,1024]{1,0:T(8,128)S(1)}, f32[256,1024]{1,0:T(8,128)}, u32[]{:S(2)}) copy-start(f32[256,1024]{1,0:T(8,128)} %get-tuple-element.196) | copy-start | bytes 3145732 | tf_op jit(solution)/shard_map/conditional.1
  208.4 10.3 %copy-start.24 = (f32[256,1024]{1,0:T(8,128)S(1)}, f32[256,1024]{1,0:T(8,128)}, u32[]{:S(2)}) copy-start(f32[256,1024]{1,0:T(8,128)} %copy-done.23) | copy-start | bytes 3145732 | tf_op jit(solution)/shard_map/conditional.1
  219.1 82.1 %copy-start.12 = (bf16[256,1024]{1,0:T(8,128)(2,1)}, bf16[256,1024]{1,0:T(8,128)(2,1)S(1)}, u32[]{:S(2)}) copy-start(bf16[256,1024]{1,0:T(8,128)(2,1)S(1)} %get-tuple-element.498) | copy-start | bytes 1572868 | tf_op jit(solution)/shard_map/conditional.1
  219.3 4.8 copy-start.36
  224.1 8.0 %copy-start.4 = (bf16[256,3072]{1,0:T(8,128)(2,1)}, bf16[256,3072]{1,0:T(8,128)(2,1)S(1)}, u32[]{:S(2)}) copy-start(bf16[256,3072]{1,0:T(8,128)(2,1)S(1)} %convolution_convert_fusion.3.query_ref.key_ref.value_ref) | copy-start | bytes 4718596 | tf_op jit(solution)/shard_map/conditional.1
  224.1 8.0 %copy-start.29 = (bf16[1024,1024]{1,0:T(8,128)(2,1)S(1)}, bf16[1024,1024]{1,0:T(8,128)(2,1)}, u32[]{:S(2)}) copy-start(bf16[1024,1024]{1,0:T(8,128)(2,1)} %get-tuple-element.192) | copy-start | bytes 6291460 | tf_op jit(solution)/shard_map/conditional.1
  232.1 0.8 copy-start.32
  255.8 13.6 %copy-start.45 = (bf16[256,1024]{1,0:T(8,128)(2,1)}, bf16[256,1024]{1,0:T(8,128)(2,1)S(1)}, u32[]{:S(2)}) copy-start(bf16[256,1024]{1,0:T(8,128)(2,1)S(1)} %get-tuple-element.503) | copy-start | bytes 1572868 | tf_op jit(solution)/shard_map/conditional.1
  255.8 2.6 copy-start.5
  269.4 5.4 copy-start.49
  269.4 5.4 copy-start.15
  275.4 15.2 %copy-start.9 = (bf16[1024,2048]{1,0:T(8,128)(2,1)S(1)}, bf16[1024,2048]{1,0:T(8,128)(2,1)}, u32[]{:S(2)}) copy-start(bf16[1024,2048]{1,0:T(8,128)(2,1)} %fusion.30.key_ref.value_ref) | copy-start | bytes 12582916 | tf_op jit(solution)/shard_map/conditional.1
  288.0 10.4 %copy-start.47 = (bf16[256,1024]{1,0:T(8,128)(2,1)}, bf16[256,1024]{1,0:T(8,128)(2,1)S(1)}, u32[]{:S(2)}) copy-start(bf16[256,1024]{1,0:T(8,128)(2,1)S(1)} %get-tuple-element.510) | copy-start | bytes 1572868 | tf_op jit(solution)/shard_map/conditional.1
  290.5 7.9 %copy-start.25 = (f32[256,1024]{1,0:T(8,128)S(1)}, f32[256,1024]{1,0:T(8,128)}, u32[]{:S(2)}) copy-start(f32[256,1024]{1,0:T(8,128)} %copy-done.23) | copy-start | bytes 3145732 | tf_op jit(solution)/shard_map/conditional.1
  298.5 2.8 copy-start.50
  301.4 2.2 copy-start.11
  303.6 11.4 %copy-start.13 = (bf16[256,1024]{1,0:T(8,128)(2,1)S(1)}, bf16[256,1024]{1,0:T(8,128)(2,1)}, u32[]{:S(2)}) copy-start(bf16[256,1024]{1,0:T(8,128)(2,1)} %copy-done.12) | copy-start | bytes 1572868 | tf_op jit(solution)/shard_map/conditional.1
  303.6 11.4 %copy-start.33 = (bf16[256,1024]{1,0:T(8,128)(2,1)S(1)}, bf16[256,1024]{1,0:T(8,128)(2,1)}, u32[]{:S(2)}) copy-start(bf16[256,1024]{1,0:T(8,128)(2,1)} %copy-done.32) | copy-start | bytes 1572868 | tf_op jit(solution)/shard_map/conditional.1
  303.6 11.4 %copy-start.51 = (bf16[256,1024]{1,0:T(8,128)(2,1)S(1)}, bf16[256,1024]{1,0:T(8,128)(2,1)}, u32[]{:S(2)}) copy-start(bf16[256,1024]{1,0:T(8,128)(2,1)} %copy-done.50) | copy-start | bytes 1572868 | tf_op jit(solution)/shard_map/conditional.1
  315.3 334.4 %copy-start.43 = (s32[9]{0:T(128)S(1)}, s32[9]{0:T(128)}, u32[]{:S(2)}) copy-start(s32[9]{0:T(128)} %iota_multiply_fusion) | copy-start | bytes 112
  649.3 34.6 %collective-permute-start.2 = (bf16[2,2,1024]{2,1,0:T(2,128)(2,1)S(1)}, bf16[2,2,1024]{2,1,0:T(2,128)(2,1)S(1)}, u32[]{:S(2)}, u32[]{:S(2)}) collective-permute-start(bf16[2,2,1024]{2,1,0:T(2,128)(2,1)S(1)} %reshape.245), channel_id=1, source_target_pairs={{0,16},{16,0},{1,17},{17,1},{2,18},{18,2},{3,19},{19,3},{4,20},{20... | collective-permute-start | bytes 24584 | tf_op jit(solution)/shard_map/ppermute | solution.py:1280
  651.0 33.5 %collective-permute-start.1 = (bf16[256,1024]{1,0:T(8,128)(2,1)S(1)}, bf16[256,1024]{1,0:T(8,128)(2,1)S(1)}, u32[]{:S(2)}, u32[]{:S(2)}) collective-permute-start(bf16[256,1024]{1,0:T(8,128)(2,1)S(1)} %get-tuple-element.471), channel_id=1, source_target_pairs={{0,16},{16,0},{1,17},{17,1},{2,18},{18,2},{3,19},{19,3},{4,20},{20... | collective-permute-start | bytes 1572872 | tf_op jit(solution)/shard_map/ppermute | solution.py:1280
  651.2 30.0 %copy-start.40 = (bf16[16,32,512]{2,1,0:T(8,128)(2,1)S(1)}, bf16[16,32,512]{2,1,0:T(8,128)(2,1)}, u32[]{:S(2)}) copy-start(bf16[16,32,512]{2,1,0:T(8,128)(2,1)} %get-tuple-element.299) | copy-start | bytes 1572868
  651.2 30.9 %copy-start = (bf16[2,64,6272]{2,1,0:T(8,128)(2,1)S(1)}, bf16[2,64,6272]{2,1,0:T(8,128)(2,1)}, u32[]{:S(2)}) copy-start(bf16[2,64,6272]{2,1,0:T(8,128)(2,1)} %get-tuple-element.303.sums_ref) | copy-start | bytes 4816900
  651.3 30.9 %copy-start.1 = (bf16[64,6272]{1,0:T(8,128)(2,1)S(1)}, bf16[64,6272]{1,0:T(8,128)(2,1)}, u32[]{:S(2)}) copy-start(bf16[64,6272]{1,0:T(8,128)(2,1)} %get-tuple-element.304.theirs_ref) | copy-start | bytes 2408452
Sparse Core Ops, SparseCore 0:
  11.1 8.7 sort.41.cloned.1.call-done
  189.7 7.6 sort.39.cloned.1.call-done
  (2 shorter events, 0.0 us)
